TPU v7x, 128 devices: a whole 4x4x4 slice. The times are simulated.
128 devices in a mesh: section: 2 (over core), dp: 64 (over z, x, y).
Axes of the slice: x: 4, y: 4, z: 4, core: 2. Of those that a mesh axis runs over, the one named last changes fastest.
Arguments:
- ends_in: bfloat16 [2, 16384, 1536], P('section', 'dp'), may hold values from -6 to 6
- seg_ids: int32 [128, 128], P('dp'), may hold values from 0 to 2, never falling along the last dimension, each value on 1 to 96 neighbouring positions
- block_counts: int32 [128], P('dp'), may hold values from 64 to 128, as said below
- in_weight: bfloat16 [2, 1536, 6448], P('section', 'dp'), may hold values from -0.15625 to 0.15625
- conv_weight: bfloat16 [2, 4, 3328], P('section', None, 'dp'), may hold values from -3 to 3
- conv_bias: bfloat16 [2, 3328], P('section', 'dp'), may hold values from -1.5 to 1.5
- pre_gain: bfloat16 [2, 1536], P('section', 'dp'), may hold values from 0.5 to 1.5
- gate_gain: bfloat16 [2, 3072], P('section', 'dp'), may hold values from 0.5 to 1.5
- out_weight: bfloat16 [2, 3072, 1536], P('section', 'dp'), may hold values from -0.109375 to 0.109375
- dt_bias: bfloat16 [2, 48], P('section'), may hold values from -6.5 to -2.5
- a_log: bfloat16 [2, 48], P('section'), may hold values from 0 to 2.765625
- skip: bfloat16 [2, 48], P('section'), may hold values from 0.5 to 1.5
Outputs:
- ends_out: bfloat16 [2, 16384, 1536], P('section', 'dp')
- d_in_weight: float32 [2, 1536, 6448], P('section', 'dp')
- d_conv_weight: float32 [2, 4, 3328], P('section', None, 'dp')
- d_conv_bias: float32 [2, 3328], P('section', 'dp')
- d_pre_gain: float32 [2, 1536], P('section', 'dp')
- d_gate_gain: float32 [2, 3072], P('section', 'dp')
- d_out_weight: float32 [2, 3072, 1536], P('section', 'dp')
- d_dt_bias: float32 [2, 48], P('section')
- d_a_log: float32 [2, 48], P('section')
- d_skip: float32 [2, 48], P('section')
Inputs may be any that keep to these rules, and one draw needn't show every extreme that they name: The first block_counts[b] slots of block b hold tokens, the rest are padding; some block is full and some holds 64. `seg_ids`: within a block the numbers never fall; one number is one packed sequence of at most 96 slots.
All inputs are finite; a program needn't handle non-finite values.
Results may differ from a plain program's by a relative error of at most 0.013.
Values may be sent and summed in bfloat16 or wider, within the bound.
A program may use at most 256 MiB of HBM per device.

v0:
```python
import jax
import jax.numpy as jnp
from jax import lax
from jax.sharding import PartitionSpec as P

D = 1536
DI = 3072
N = 128
HEAD_DIM = 64
KC = 4
CC = 3328


EPSILON = 1e-05


def shifted(block, axis, distance):
    devices = range(lax.axis_size(axis))
    route = [(i - distance, i) for i in devices if i - distance in devices]
    return lax.ppermute(block, axis, route)


def norm_piece(hidden, gain_in, valid_rows):
    return (
        hidden
        * lax.rsqrt(jnp.mean(hidden * hidden, axis=-1, keepdims=True) + EPSILON)
        * gain_in
        * valid_rows[:, None]
    )


def mix_piece(projected, kernel_taps, kernel_bias, rate_bias, decay_log, segment):
    length = projected.shape[0]
    gate_z = projected[:, :DI]
    channels = projected[:, DI : DI + CC]
    rate_raw = projected[:, DI + CC :]
    padded = jnp.concatenate([jnp.zeros((KC - 1, CC), jnp.float32), channels], axis=0)
    seg_pad = jnp.concatenate([jnp.full((KC - 1,), -1, jnp.int32), segment], axis=0)
    convolved = jnp.zeros_like(channels) + kernel_bias[None, :]
    for offset in range(KC):
        same_segment = (seg_pad[offset : offset + length] == segment).astype(jnp.float32)
        convolved = (
            convolved
            + kernel_taps[offset][None, :]
            * padded[offset : offset + length]
            * same_segment[:, None]
        )
    activated = jax.nn.silu(convolved)
    heads_x = activated[:, :DI].reshape(length, DI // HEAD_DIM, HEAD_DIM)
    in_state = activated[:, DI : DI + N]
    out_state = activated[:, DI + N :]
    step_size = jax.nn.softplus(rate_raw + rate_bias[None, :])
    cumulative = jnp.cumsum(step_size * (-jnp.exp(decay_log))[None, :], axis=0)
    return (gate_z, heads_x, in_state, out_state, step_size, cumulative)


def weight_piece(scores, cumulative, step_size, segment):
    length = scores.shape[0]
    positions = jnp.arange(length, dtype=jnp.int32)
    allowed = (positions[:, None] >= positions[None, :]) & (segment[:, None] == segment[None, :])
    across = cumulative.T
    gaps = across[:, :, None] - across[:, None, :]
    decay = jnp.exp(jnp.where(allowed[None, :, :], gaps, 0.0)) * allowed[None, :, :].astype(
        jnp.float32
    )
    return scores[None, :, :] * decay * step_size.T[:, None, :]


def gate_piece(ssd_out, gate_z, gain_out):
    gated = ssd_out * jax.nn.silu(gate_z)
    return gated * lax.rsqrt(jnp.mean(gated * gated, axis=-1, keepdims=True) + EPSILON) * gain_out


def layer_parts(hidden, segment, valid_rows, weights, heads):
    proj_in, proj_out, kernel_taps, kernel_bias, gain_in, gain_out = weights
    rate_bias, decay_log, skip_gain = heads
    length = hidden.shape[0]
    normed_in, norm_pull = jax.vjp(
        lambda a, b: norm_piece(a, b, valid_rows), hidden, gain_in.astype(jnp.float32)
    )
    input_low = normed_in.astype(jnp.bfloat16)
    projected = jnp.dot(input_low, proj_in, preferred_element_type=jnp.float32)
    mixed, mix_pull = jax.vjp(
        lambda a, b, c, d, e: mix_piece(a, b, c, d, e, segment),
        projected,
        kernel_taps.astype(jnp.float32),
        kernel_bias.astype(jnp.float32),
        rate_bias,
        decay_log,
    )
    gate_z, heads_x, in_state, out_state, step_size, cumulative = mixed
    x_low = heads_x.astype(jnp.bfloat16)
    state_in_low = in_state.astype(jnp.bfloat16)
    state_out_low = out_state.astype(jnp.bfloat16)
    scores = jnp.dot(state_out_low, state_in_low.T, preferred_element_type=jnp.float32)
    mix_weights, weight_pull = jax.vjp(
        lambda a, b, c: weight_piece(a, b, c, segment), scores, cumulative, step_size
    )
    mix_low = mix_weights.astype(jnp.bfloat16)
    ssd_out = (
        jnp.einsum("hts,shp->thp", mix_low, x_low, preferred_element_type=jnp.float32)
        + skip_gain[None, :, None] * heads_x
    )
    ssd_out = ssd_out.reshape(length, DI)
    normed, gate_pull = jax.vjp(gate_piece, ssd_out, gate_z, gain_out.astype(jnp.float32))
    normed_low = normed.astype(jnp.bfloat16)
    return (
        input_low,
        norm_pull,
        mix_pull,
        heads_x,
        x_low,
        state_in_low,
        state_out_low,
        weight_pull,
        mix_low,
        gate_pull,
        normed_low,
    )


def layer_forward(hidden, segment, valid_rows, weights, heads):
    parts = layer_parts(hidden, segment, valid_rows, weights, heads)
    return hidden + jnp.dot(parts[10], weights[1], preferred_element_type=jnp.float32)


def layer_backward(hidden, upstream, segment, valid_rows, weights, heads):
    proj_in, proj_out = (weights[0], weights[1])
    skip_gain = heads[2]
    length = hidden.shape[0]
    (
        input_low,
        norm_pull,
        mix_pull,
        heads_x,
        x_low,
        state_in_low,
        state_out_low,
        weight_pull,
        mix_low,
        gate_pull,
        normed_low,
    ) = layer_parts(hidden, segment, valid_rows, weights, heads)
    upstream_low = upstream.astype(jnp.bfloat16)
    d_proj_out = jnp.dot(normed_low.T, upstream_low, preferred_element_type=jnp.float32)
    d_normed = jnp.dot(upstream_low, proj_out.T, preferred_element_type=jnp.float32)
    d_ssd, d_gate_z, d_gain_out = gate_pull(d_normed)
    d_ssd_low = d_ssd.astype(jnp.bfloat16).reshape(length, DI // HEAD_DIM, HEAD_DIM)
    d_ssd_wide = d_ssd_low.astype(jnp.float32)
    d_mix = jnp.einsum("thp,shp->hts", d_ssd_low, x_low, preferred_element_type=jnp.float32)
    d_heads_x = jnp.einsum("hts,thp->shp", mix_low, d_ssd_low, preferred_element_type=jnp.float32)
    d_heads_x = d_heads_x + skip_gain[None, :, None] * d_ssd_wide
    d_skip = jnp.sum(d_ssd_wide * heads_x, axis=(0, 2))
    d_scores, d_cumulative, d_step = weight_pull(d_mix)
    d_scores_low = d_scores.astype(jnp.bfloat16)
    d_out_state = jnp.dot(d_scores_low, state_in_low, preferred_element_type=jnp.float32)
    d_in_state = jnp.dot(d_scores_low.T, state_out_low, preferred_element_type=jnp.float32)
    d_projected, d_taps, d_kernel_bias, d_rate_bias, d_decay_log = mix_pull(
        (d_gate_z, d_heads_x, d_in_state, d_out_state, d_step, d_cumulative)
    )
    d_projected_low = d_projected.astype(jnp.bfloat16)
    d_proj_in = jnp.dot(input_low.T, d_projected_low, preferred_element_type=jnp.float32)
    d_normed_in = jnp.dot(d_projected_low, proj_in.T, preferred_element_type=jnp.float32)
    d_hidden, d_gain_in = norm_pull(d_normed_in)
    return (
        upstream + d_hidden,
        (d_proj_in, d_proj_out, d_taps, d_kernel_bias, d_gain_in, d_gain_out),
        (d_rate_bias, d_decay_log, d_skip),
    )


def body(
    ends_in,
    seg_ids,
    block_counts,
    in_weight,
    conv_weight,
    conv_bias,
    pre_gain,
    gate_gain,
    out_weight,
    dt_bias,
    a_log,
    skip,
):
    leading = lax.axis_index("section") == 0
    blocks_here = block_counts.shape[0]
    length = seg_ids.shape[1]
    own_rows = ends_in[0].reshape(blocks_here, length, D)
    valid_all = (jnp.arange(length, dtype=jnp.int32)[None, :] < block_counts[:, None]).astype(
        jnp.float32
    )
    heads = (
        dt_bias[0].astype(jnp.float32),
        a_log[0].astype(jnp.float32),
        skip[0].astype(jnp.float32),
    )
    shards = (in_weight[0], out_weight[0], conv_weight[0], conv_bias[0], pre_gain[0], gate_gain[0])
    gathered = (
        lax.all_gather(shards[0], "dp", axis=0, tiled=True),
        lax.all_gather(shards[1], "dp", axis=0, tiled=True),
        lax.all_gather(shards[2], "dp", axis=1, tiled=True),
        lax.all_gather(shards[3], "dp", axis=0, tiled=True),
        lax.all_gather(shards[4], "dp", axis=0, tiled=True),
        lax.all_gather(shards[5], "dp", axis=0, tiled=True),
    )
    incoming = jnp.zeros((length, D), jnp.bfloat16)
    kept_inputs = []
    outputs = []
    for step in range(blocks_here + 1):
        first_block = min(step, blocks_here - 1)
        second_block = max(step - 1, 0)
        block_in = jnp.where(leading, own_rows[first_block], incoming)
        segment = jnp.where(leading, seg_ids[first_block], seg_ids[second_block])
        valid_rows = jnp.where(leading, valid_all[first_block], valid_all[second_block])
        result = layer_forward(block_in.astype(jnp.float32), segment, valid_rows, gathered, heads)
        if step >= 1:
            kept_inputs.append(incoming)
            outputs.append(result)
        if step < blocks_here:
            incoming = shifted(result.astype(jnp.bfloat16), "section", 1)
    weights_back = (
        lax.all_gather(shards[0], "dp", axis=0, tiled=True),
        lax.all_gather(shards[1], "dp", axis=0, tiled=True),
        lax.all_gather(shards[2], "dp", axis=1, tiled=True),
        lax.all_gather(shards[3], "dp", axis=0, tiled=True),
        lax.all_gather(shards[4], "dp", axis=0, tiled=True),
        lax.all_gather(shards[5], "dp", axis=0, tiled=True),
    )
    returning = jnp.zeros((length, D), jnp.bfloat16)
    input_grads = []
    totals = None
    head_totals = None
    for step in range(blocks_here + 1):
        late_block = min(step, blocks_here - 1)
        early_block = max(step - 1, 0)
        block_in = jnp.where(leading, own_rows[early_block], kept_inputs[late_block])
        upstream = jnp.where(leading, returning, own_rows[late_block]).astype(jnp.float32)
        segment = jnp.where(leading, seg_ids[early_block], seg_ids[late_block])
        valid_rows = jnp.where(leading, valid_all[early_block], valid_all[late_block])
        active = jnp.where(leading, step >= 1, step < blocks_here)
        d_block, grads, head_grads = layer_backward(
            block_in.astype(jnp.float32), upstream, segment, valid_rows, weights_back, heads
        )
        grads = tuple((jnp.where(active, value, 0.0) for value in grads))
        head_grads = tuple((jnp.where(active, value, 0.0) for value in head_grads))
        if step >= 1:
            input_grads.append(d_block)
        if step < blocks_here:
            returning = shifted(d_block.astype(jnp.bfloat16), "section", -1)
        totals = grads if totals is None else tuple((a + b for a, b in zip(totals, grads)))
        head_totals = (
            head_grads
            if head_totals is None
            else tuple((a + b for a, b in zip(head_totals, head_grads)))
        )
    totals = (
        lax.psum_scatter(totals[0], "dp", scatter_dimension=0, tiled=True),
        lax.psum_scatter(totals[1], "dp", scatter_dimension=0, tiled=True),
        lax.psum_scatter(totals[2], "dp", scatter_dimension=1, tiled=True),
        lax.psum_scatter(totals[3], "dp", scatter_dimension=0, tiled=True),
        lax.psum_scatter(totals[4], "dp", scatter_dimension=0, tiled=True),
        lax.psum_scatter(totals[5], "dp", scatter_dimension=0, tiled=True),
    )
    head_sums = lax.psum(head_totals, "dp")
    ends_out = jnp.where(
        leading, jnp.concatenate(input_grads, axis=0), jnp.concatenate(outputs, axis=0)
    )
    ends_out = ends_out.astype(jnp.bfloat16)[None]
    d_proj_in, d_proj_out, d_taps, d_kernel_bias, d_gain_in, d_gain_out = totals
    return (
        ends_out,
        d_proj_in[None],
        d_taps[None],
        d_kernel_bias[None],
        d_gain_in[None],
        d_gain_out[None],
        d_proj_out[None],
        head_sums[0][None],
        head_sums[1][None],
        head_sums[2][None],
    )


def solution(mesh):
    placed = (
        P("section", "dp", None),
        P("dp", None),
        P("dp"),
        P("section", "dp", None),
        P("section", None, "dp"),
        P("section", "dp"),
        P("section", "dp"),
        P("section", "dp"),
        P("section", "dp", None),
        P("section", None),
        P("section", None),
        P("section", None),
    )
    return jax.shard_map(
        body,
        mesh=mesh,
        in_specs=placed,
        out_specs=(
            P("section", "dp", None),
            P("section", "dp", None),
            P("section", None, "dp"),
            P("section", "dp"),
            P("section", "dp"),
            P("section", "dp"),
            P("section", "dp", None),
            P("section", None),
            P("section", None),
            P("section", None),
        ),
        check_vma=False,
    )
```

profile of v0, /device:TPU:0, one launch (start us, length us, event | category | flops | bytes accessed | tf_op | source)
XLA Modules:
  0.0 1600.4 jit_solution(3149074298109036930)
XLA Ops:
  14.5 352.2 %all-reduce.60 = (bf16[1536]{0:T(1024)(128)(2,1)S(1)}, bf16[3328]{0:T(1024)(128)(2,1)S(1)}, bf16[3072]{0:T(1024)(128)(2,1)S(1)}) all-reduce(bf16[1536]{0:T(1024)(128)(2,1)S(1)} %dynamic-update-slice.1, bf16[3328]{0:T(1024)(128)(2,1)S(1)} %dynamic-update-slice, ...), channel_id=4, replica_groups=mesh['section'=2,'dp'=64] {'dp'}, use_global_device_ids=true, to_apply=%add.52 | all-reduce | flops 7936 | bytes 31744
  367.6 178.7 %all-gather.1 = bf16[1,4,3328]{1,0,2:T(2,128)(2,1)S(1)} all-gather(bf16[1,4,52]{1,0,2:T(2,128)(2,1)S(1)} %copy.138), channel_id=3, replica_groups=mesh['section'=2,'dp'=64] {'dp'}, dimensions={2}, use_global_device_ids=true | all-gather | bytes 27040 | tf_op jit(solution)/shard_map/all_gather | solution.py:225
  552.5 69.1 %slice_reduce_fusion.3 = (f32[3328]{0:T(1024)S(1)}, f32[3328]{0:T(1024)S(1)}, f32[3328]{0:T(1024)S(1)}, f32[3328]{0:T(1024)S(1)}) fusion(f32[1,4,3328]{1,0,2:T(1,128)S(1)} %convert_element_type.379), kind=kLoop, calls=%fused_computation.126 | loop fusion | bytes 106496 | tf_op jit(solution)/shard_map/jvp()/slice | solution.py:44
  621.7 12.7 fusion.14
  652.8 12.7 fusion.12
  667.8 12.5 fusion.8
  683.0 12.7 fusion.292
  753.0 12.3 fusion.133
  765.4 8.2 fusion.153
  779.5 12.7 fusion.6
  793.7 12.8 fusion.2
  812.2 12.5 fusion.290
  850.0 9.0 multiply_reduce_fusion.12
  867.9 11.6 fusion.130
  881.4 8.5 fusion.154
  917.6 6.7 multiply_reduce_fusion.8
  933.1 11.3 fusion.127
  946.5 12.1 select_add_fusion.1
  959.6 17.8 %fusion.271 = f32[1536,6448]{1,0:T(8,128)} fusion(bf16[128,1536]{1,0:T(8,128)(2,1)S(1)} %copy-done.26, f32[1536]{0:T(1024)S(1)} %convert_element_type.383, f32[128]{0:T(128)S(1)} %copy-done.87, f32[128]{0:T(128)S(1)} %copy-done.71, f32[128,3072]{0,1:T(8,128)} %get-tuple-element.126, f32[128,3328]{0,1:T(8,128)} %copy-done.30, f32[128,48]{0,1:T(8,128)S(1)} %copy-done.46), kind=kOutput, calls=%fused_computation.516 | convolution fusion | flops 2538915840 | bytes 43318272 | tf_op jit(solution)/shard_map/dot_general | solution.py:162
  977.4 17.8 %fusion.274 = f32[1536,6448]{1,0:T(8,128)} fusion(bf16[128,1536]{1,0:T(8,128)(2,1)S(1)} %copy-done.19, f32[1536]{0:T(1024)S(1)} %convert_element_type.383, f32[128]{0:T(128)S(1)} %copy-done.90, f32[128]{0:T(128)S(1)} %copy-done.74, f32[128,3072]{0,1:T(8,128)} %get-tuple-element.125, f32[128,3328]{0,1:T(8,128)} %pad_add_fusion.3, ...), kind=kOutput, calls=%fused_computation.517 | convolution fusion | flops 2538915840 | bytes 43318272 | tf_op jit(solution)/shard_map/dot_general | solution.py:162
  995.2 27.7 %select_add_fusion = f32[1536,6448]{1,0:T(8,128)} fusion(f32[1536,6448]{1,0:T(8,128)} %fusion.274, f32[1536,6448]{1,0:T(8,128)} %fusion.271, pred[]{:T(512)S(6)} %eq.145, pred[]{:T(512)S(6)} %select_n.339, bf16[128,1536]{1,0:T(8,128)(2,1)S(1)} %copy-done.16, f32[1536]{0:T(1024)S(1)} %convert_element_type.383, f32[128]{0:T(128)S(1)} %copy-done.102, ...), kind=kOutput, calls=%fused_computation | convolution fusion | flops 2578532352 | bytes 122551296 | tf_op jit(solution)/shard_map/dot_general | solution.py:162
  1033.0 35.4 %all-reduce.63.cloned.1.call-done = (f32[4,3328]{1,0:T(4,128)}, f32[3328]{0:T(1024)}, f32[1536]{0:T(1024)}, f32[3072]{0:T(1024)}, f32[1,48]{1,0:T(1,128)}, /*index=5*/f32[1,48]{1,0:T(1,128)}, f32[1,48]{1,0:T(1,128)}) async-done(((f32[4,3328]{1,0:T(4,128)}, f32[3328]{0:T(1024)}, f32[1536]{0:T(1024)}, f32[3072]{0:T(1024)}, f32[1,48]{1,0:T(1,128)}, /*index=5*/f32[1,48]{1,0:T(1,128)}, f32[1,48]{1,0:T(1,128)}), ...) | async-done | bytes 85584
  1073.5 236.9 %reduce-scatter.6.cloned.1.call-done = f32[48,1536]{1,0:T(8,128)} async-done(((f32[3072,1536]{1,0:T(8,128)}), f32[48,1536]{1,0:T(8,128)}) %reduce-scatter.6.cloned.1.call-update) | async-done | bytes 294928 | tf_op jit(solution)/shard_map/reduce_scatter | solution.py:259
  1310.5 279.7 %reduce-scatter.8.cloned.1.call-done = f32[24,6448]{1,0:T(8,128)} async-done(((f32[1536,6448]{1,0:T(8,128)}), f32[24,6448]{1,0:T(8,128)}) %reduce-scatter.8.cloned.1.call-update) | async-done | bytes 619024
  (521 shorter events, 196.7 us)
Async XLA Ops:
  7.2 614.5 %all-gather.9.cloned.1.call-start = ((), (), s32[]{:S(2)}) async-start(), calls=%async_computation.3 | async-start | bytes 20367360 | tf_op jit(solution)/shard_map/all_gather | solution.py:200
  7.9 636.6 %all-gather.11.cloned.1.call-start = ((), (), s32[]{:S(2)}) async-start(), calls=%async_computation.4 | async-start | bytes 9584640 | tf_op jit(solution)/shard_map/all_gather | solution.py:201
  8.7 1059.7 %all-reduce.63.cloned.1.call-start = ((), (), s32[]{:S(2)}) async-start(), calls=%async_computation.6 | async-start | bytes 183296
  548.4 92.8 %copy-start.150 = (f32[48]{0:T(128)}, f32[48]{0:T(128)S(1)}, u32[]{:S(2)}) copy-start(f32[48]{0:T(128)S(1)} %bitcast_convert_fusion) | copy-start | bytes 580
  548.4 173.9 %copy-start.91 = (f32[48]{0:T(128)}, f32[48]{0:T(128)S(1)}, u32[]{:S(2)}) copy-start(f32[48]{0:T(128)S(1)} %bitcast_convert_fusion.1) | copy-start | bytes 580
  548.5 173.9 %copy-start.95 = (f32[48]{0:T(128)}, f32[48]{0:T(128)S(1)}, u32[]{:S(2)}) copy-start(f32[48]{0:T(128)S(1)} %negate_bitcast_fusion) | copy-start | bytes 580
  549.1 203.8 %copy-start.70 = (f32[128]{0:T(128)}, f32[128]{0:T(128)S(1)}, u32[]{:S(2)}) copy-start(f32[128]{0:T(128)S(1)} %get-tuple-element.170) | copy-start | bytes 1540
  551.0 85.6 %copy-start.112 = (f32[128]{0:T(128)}, f32[128]{0:T(128)S(1)}, u32[]{:S(2)}) copy-start(f32[128]{0:T(128)S(1)} %get-tuple-element.198) | copy-start | bytes 1540
  551.0 132.0 %copy-start.108 = (f32[128]{0:T(128)}, f32[128]{0:T(128)S(1)}, u32[]{:S(2)}) copy-start(f32[128]{0:T(128)S(1)} %get-tuple-element.196) | copy-start | bytes 1540
  551.0 132.0 %copy-start.110 = (f32[128]{0:T(128)}, f32[128]{0:T(128)S(1)}, u32[]{:S(2)}) copy-start(f32[128]{0:T(128)S(1)} %get-tuple-element.197) | copy-start | bytes 1540
  551.1 90.2 %copy-start.57 = (f32[128,128]{1,0:T(8,128)}, f32[128,128]{1,0:T(8,128)S(1)}, u32[]{:S(2)}) copy-start(f32[128,128]{1,0:T(8,128)S(1)} %get-tuple-element.195) | copy-start | bytes 196612
  551.1 90.2 %copy-start.106 = (pred[128,128]{1,0:T(8,128)(4,1)}, pred[128,128]{1,0:T(8,128)(4,1)S(1)}, u32[]{:S(2)}) copy-start(pred[128,128]{1,0:T(8,128)(4,1)S(1)} %get-tuple-element.194) | copy-start | bytes 49156
  649.7 2.7 collective-permute-start
  665.6 78.0 %copy-start = (f32[128,6448]{0,1:T(8,128)}, f32[128,6448]{0,1:T(8,128)S(1)}, u32[]{:S(2)}) copy-start(f32[128,6448]{0,1:T(8,128)S(1)} %fusion.12) | copy-start | bytes 9904132
  682.9 23.3 %copy-start.84 = (f32[48,128]{1,0:T(8,128)}, f32[48,128]{1,0:T(8,128)S(1)}, u32[]{:S(2)}) copy-start(f32[48,128]{1,0:T(8,128)S(1)} %copy.143) | copy-start | bytes 73732
  740.6 36.1 %collective-permute-start.2 = (bf16[128,1536]{1,0:T(8,128)(2,1)}, bf16[128,1536]{1,0:T(8,128)(2,1)}, u32[]{:S(2)}, u32[]{:S(2)}) collective-permute-start(bf16[128,1536]{1,0:T(8,128)(2,1)} %fusion.46), channel_id=1, source_target_pairs={{0,64},{1,65},{2,66},{3,67},{4,68},{5,69},{6,70},{7,71},{8,72},{9,... | collective-permute-start | bytes 1179656 | tf_op jit(solution)/shard_map/ppermute | solution.py:20
  792.2 36.1 %copy-start.1 = (f32[128,6448]{0,1:T(8,128)}, f32[128,6448]{0,1:T(8,128)S(1)}, u32[]{:S(2)}) copy-start(f32[128,6448]{0,1:T(8,128)S(1)} %fusion.6) | copy-start | bytes 9904132
  808.8 24.3 %collective-permute-start.1 = (bf16[128,1536]{1,0:T(8,128)(2,1)}, bf16[128,1536]{1,0:T(8,128)(2,1)}, u32[]{:S(2)}, u32[]{:S(2)}) collective-permute-start(bf16[128,1536]{1,0:T(8,128)(2,1)} %get-tuple-element.155), channel_id=1, source_target_pairs={{64,0},{65,1},{66,2},{67,3},{68,4},{69,5},{70,6},{71,7},{72,8},{73... | collective-permute-start | bytes 1179656 | tf_op jit(solution)/shard_map/ppermute | solution.py:20
  824.8 73.5 %copy-start.56 = (f32[128,128]{1,0:T(8,128)}, f32[128,128]{1,0:T(8,128)S(1)}, u32[]{:S(2)}) copy-start(f32[128,128]{1,0:T(8,128)S(1)} %fusion.200) | copy-start | bytes 196612
  833.1 60.2 %copy-start.114 = (f32[128]{0:T(128)}, f32[128]{0:T(128)S(1)}, u32[]{:S(2)}) copy-start(f32[128]{0:T(128)S(1)} %fusion.254) | copy-start | bytes 1540
  834.2 47.2 %copy-start.22 = (bf16[128,1536]{1,0:T(8,128)(2,1)}, bf16[128,1536]{1,0:T(8,128)(2,1)S(1)}, u32[]{:S(2)}) copy-start(bf16[128,1536]{1,0:T(8,128)(2,1)S(1)} %bitcast_select_fusion.3) | copy-start | bytes 1179652
  879.8 10.1 collective-permute-start.3
  946.4 364.1 %reduce-scatter.6.cloned.1.call-start = ((), (), s32[]{:S(2)}) async-start(), calls=%async_computation.2 | async-start | bytes 19169280 | tf_op jit(solution)/shard_map/reduce_scatter | solution.py:259
  958.7 631.5 %reduce-scatter.8.cloned.1.call-start = ((), (), s32[]{:S(2)}) async-start(), calls=%async_computation.5 | async-start | bytes 40734720
  (149 other events, 1019.1 us)
Sparse Core Ops, SparseCore 0:
  10.9 117.7 all-gather.8
  131.4 81.8 all-gather.10
  946.5 121.8 all-reduce.62
  1074.3 236.1 reduce-scatter.5
  1316.0 274.1 reduce-scatter.7
where the time goes:
time: 1610 us; the launch traced here: 1600 us
  waiting for transfers between devices  554 us (34%)
  blocking collectives  531 us (33%)
  matrix products  251 us (16%)
  other arithmetic  123 us (8%)
  local copies, waits for them, and re-layouts  115 us (7%)
  between operations  20.1 us (1%)
    unnamed x1, blocking collectives  352 us
    unnamed x7, waiting for transfers between devices  317 us
    reduce_scatter x1, waiting for transfers between devices, body(): lax.psum_scatter(totals[1], 'dp', scatter_dimension=0, tiled=True)  237 us
    all_gather x1, blocking collectives, body(): lax.all_gather(shards[2], 'dp', axis=1, tiled=True)  179 us
    slice x1, local copies, waits for them, and re-layouts, mix_piece(): kernel_taps[offset][None, :] * padded[offset:offset + length]  69.1 us
    dot_general x5, matrix products, layer_parts(): projected = jnp.dot(input_low, proj_in, preferred_element_type=jnp.float32)  63.4 us
    dot_general x3, matrix products, layer_backward(): jnp.dot(input_low.T, d_projected_low, preferred_element_type=jnp.float32)  63.3 us
    dot_general x3, matrix products, layer_backward(): jnp.dot(d_projected_low, proj_in.T, preferred_element_type=jnp.float32)  35.2 us
  transfers between devices with their start and end apart: 9, of which 3 were waited for; matrix products, arithmetic and copies ran while one was open for 16% of the time, Pallas kernels for 0%

commit v1 on v0

v1 whole, which is shorter than its diff:
```python
import jax
import jax.numpy as jnp
from jax import lax
from jax.experimental import pallas as pl
from jax.experimental.pallas import tpu as pltpu
from jax.sharding import PartitionSpec as P

D = 1536
DI = 3072
N = 128
HEAD_DIM = 64
H = 48
KC = 4
CC = 3328
EPSILON = 1e-05
F32 = jnp.float32
BF = jnp.bfloat16


def to_panels(w):
    rows = w.shape[0]
    z, x = w[:, :DI], w[:, DI : 2 * DI]
    rates = jnp.pad(w[:, 2 * DI + 2 * N :], ((0, 0), (0, N - H)))
    extras = (w[:, 2 * DI : 2 * DI + N], w[:, 2 * DI + N : 2 * DI + 2 * N], rates)
    panels = []
    for j in range(3):
        pieces = []
        for g in (2 * j, 2 * j + 1):
            pieces += [z[:, 512 * g : 512 * g + 512], x[:, 512 * g : 512 * g + 512]]
        panels.append(jnp.concatenate(pieces + [extras[j]], axis=1))
    return panels


def from_panels(p):
    z = [p[g // 2][:, 1024 * (g % 2) : 1024 * (g % 2) + 512] for g in range(6)]
    x = [p[g // 2][:, 1024 * (g % 2) + 512 : 1024 * (g % 2) + 1024] for g in range(6)]
    extras = [p[0][:, 2048:], p[1][:, 2048:], p[2][:, 2048 : 2048 + H]]
    return jnp.concatenate(z + x + extras, axis=1)


def pack_small(taps, bias, gain_in, gain_out, heads):
    lead = taps.shape[:-2]
    wide = lambda v: jnp.pad(v, [(0, 0)] * (v.ndim - 1) + [(0, 128 - v.shape[-1])])
    pair = lambda a, b: jnp.concatenate([jnp.pad(a, [(0, 0)] * (a.ndim - 1) + [(0, 64 - a.shape[-1])]), jnp.pad(b, [(0, 0)] * (b.ndim - 1) + [(0, 64 - b.shape[-1])])], axis=-1)
    spread = [jnp.broadcast_to(h, lead + (H,)) for h in heads]
    rows = [wide(taps), wide(bias)[..., None, :], pair(gain_in, spread[1])[..., None, :], pair(gain_out, spread[2])[..., None, :], wide(spread[0])[..., None, :]]
    return jnp.concatenate(rows, axis=-2)


def unpack_small(s):
    taps = jnp.transpose(s[:, 0:4, 0:52], (1, 0, 2)).reshape(4, CC)
    return taps, s[:, 4, 0:52].reshape(CC), s[:, 5, 0:24].reshape(D), s[:, 6, 0:48].reshape(DI), (s[0, 7, 0:48], s[0, 5, 64:112], s[0, 6, 64:112])


MESH = pl.DeviceIdType.MESH
ORDERS = ((2, 1, 0), (1, 0, 2), (0, 2, 1))


def device(section, pos):
    return {"section": section, "dp": pos[0] * 16 + pos[1] * 4 + pos[2]}


def moved(pos, axis, by):
    out = list(pos)
    out[axis] = lax.rem(pos[axis] + by, 4)
    return tuple(out)


def block_index(order, phase, pos, half):
    index = [pos[0], pos[1], pos[2]]
    for a in order[:phase]:
        index[a] = slice(None)
    if phase > 0 and half is not None:
        a = min(order[:phase])
        index[a] = pl.ds(2 * half, 2)
    return tuple(index)


def gather_kernel(in_ref, out_ref, small_ref, gin, gout, gsmall, send, recv, local, dsend, drecv):
    section = lax.axis_index("section")
    dp = lax.axis_index("dp")
    pos = (lax.div(dp, 16), lax.rem(lax.div(dp, 4), 4), lax.rem(dp, 4))
    other = 1 - section

    barrier = pltpu.get_barrier_semaphore()
    for axis in range(3):
        for by in (1, 3):
            pl.semaphore_signal(barrier, inc=1, device_id=device(section, moved(pos, axis, by)), device_id_type=MESH)
    pl.semaphore_signal(barrier, inc=1, device_id=device(other, pos), device_id_type=MESH)
    pl.semaphore_wait(barrier, 7)

    streams = []
    for j in range(3):
        streams.append((in_ref.at[j], gin.at[section, j], ORDERS[j], 0))
        streams.append((out_ref.at[j], gout.at[section, j], ORDERS[j], 1))
    streams.append((small_ref, gsmall.at[section], ORDERS[0], 0))

    own = []
    for n, (src, dst, order, turn) in enumerate(streams):
        copy = pltpu.make_async_copy(src, dst.at[pos], local.at[n])
        copy.start()
        own.append(copy)

    sib = []

    def to_sibling(n, index, tag):
        dst = streams[n][1].at[index]
        copy = pltpu.make_async_remote_copy(dst, dst, dsend.at[n, tag], drecv.at[n, tag], device_id=device(other, pos), device_id_type=MESH)
        copy.start()
        sib.append((n, index, tag))

    def remote(n, phase, k, src, dst, to):
        return pltpu.make_async_remote_copy(src, dst, send.at[n, phase, k], recv.at[n, phase, k], device_id=device(section, to), device_id_type=MESH)

    def halves(n, phase, at):
        order, turn = streams[n][2], streams[n][3]
        if phase == 0:
            whole = block_index(order, 0, at, None)
            return (whole, None) if turn == 0 else (None, whole)
        return tuple(block_index(order, phase, at, h) for h in (0, 1))

    N = len(streams)
    for phase in range(3):
        started = []
        for n, (src, dst, order, turn) in enumerate(streams):
            axis = order[phase]
            right, left = moved(pos, axis, 1), moved(pos, axis, 3)
            mine = halves(n, phase, pos)
            for k, (h, to) in enumerate(((0, right), (1, left), (1, right), (0, left))):
                if mine[h] is None:
                    continue
                source = src if phase == 0 else dst.at[mine[h]]
                c = remote(n, phase, k, source, dst.at[mine[h]], to)
                c.start()
                started.append(c)
        if phase == 0:
            for c in own:
                c.wait()
        for n, (src, dst, order, turn) in enumerate(streams):
            axis = order[phase]
            right, left = moved(pos, axis, 1), moved(pos, axis, 3)
            for k, h, frm, to in ((0, 0, left, right), (1, 1, right, left)):
                got = halves(n, phase, frm)[h]
                if got is None:
                    continue
                remote(n, phase, k, dst.at[got], dst.at[got], to).wait_recv()
                c = remote(n, phase, 4 + k, dst.at[got], dst.at[got], to)
                c.start()
                started.append(c)
                if phase == 2:
                    to_sibling(n, got, 2 * k)
        for n, (src, dst, order, turn) in enumerate(streams):
            axis = order[phase]
            right, left = moved(pos, axis, 1), moved(pos, axis, 3)
            for k, h, frm in ((2, 1, left), (3, 0, right)):
                got = halves(n, phase, frm)[h]
                if got is None:
                    continue
                remote(n, phase, k, dst.at[got], dst.at[got], frm).wait_recv()
                if phase == 2:
                    to_sibling(n, got, 2 * (k - 2) + 1)
        if phase == 2:
            for n, (src, dst, order, turn) in enumerate(streams):
                to_sibling(n, block_index(order, 2, pos, None), 4)
        for n, (src, dst, order, turn) in enumerate(streams):
            axis = order[phase]
            far = moved(pos, axis, 2)
            for k, h in ((0, 0), (1, 1)):
                got = halves(n, phase, far)[h]
                if got is None:
                    continue
                remote(n, phase, 4 + k, dst.at[got], dst.at[got], far).wait_recv()
                if phase == 2:
                    to_sibling(n, got, 5 + k)
        for c in started:
            c.wait_send()
    theirs = [gin.at[other, 0], gout.at[other, 0], gin.at[other, 1], gout.at[other, 1], gin.at[other, 2], gout.at[other, 2], gsmall.at[other]]
    for n, index, tag in sib:
        mine = streams[n][1].at[index]
        pltpu.make_async_remote_copy(mine, theirs[n].at[index], dsend.at[n, tag], drecv.at[n, tag], device_id=device(other, pos), device_id_type=MESH).wait()


def gather(a_in, a_out, a_small):
    any_ = pl.BlockSpec(memory_space=pl.ANY)
    return pl.pallas_call(
        gather_kernel,
        out_shape=(
            jax.ShapeDtypeStruct((2, 3, 4, 4, 4) + a_in.shape[1:], a_in.dtype),
            jax.ShapeDtypeStruct((2, 3, 4, 4, 4) + a_out.shape[1:], a_out.dtype),
            jax.ShapeDtypeStruct((2, 4, 4, 4) + a_small.shape, a_small.dtype),
        ),
        in_specs=[any_] * 3,
        out_specs=(any_,) * 3,
        scratch_shapes=[
            pltpu.SemaphoreType.DMA((7, 3, 6)),
            pltpu.SemaphoreType.DMA((7, 3, 6)),
            pltpu.SemaphoreType.DMA((7,)),
            pltpu.SemaphoreType.DMA((7, 7)),
            pltpu.SemaphoreType.DMA((7, 7)),
        ],
        compiler_params=pltpu.CompilerParams(collective_id=0, has_side_effects=True),
        name="gather_weights",
    )(a_in, a_out, a_small)


def lead(n):
    return {2: 16, 1: 4, 0: 1}[n]


def scatter_kernel(win, wout, small, oin, oout, osmall, *scratch):
    got = {}
    it = iter(scratch)
    for phase in (2, 1, 0):
        for kind in (0, 1):
            got[phase, kind] = next(it)
    acc = {}
    for phase in (2, 1):
        for kind in (0, 1):
            acc[phase, kind] = next(it)
    mine = {kind: next(it) for kind in (0, 1)}
    sgot = {phase: next(it) for phase in (2, 1, 0)}
    sacc = {phase: next(it) for phase in (3, 2, 1)}
    send, recv, ssend, srecv, lsem, ssem = it

    section = lax.axis_index("section")
    dp = lax.axis_index("dp")
    pos = (lax.div(dp, 16), lax.rem(lax.div(dp, 4), 4), lax.rem(dp, 4))

    barrier = pltpu.get_barrier_semaphore()
    for axis in range(3):
        for by in (1, 2, 3):
            pl.semaphore_signal(barrier, inc=1, device_id=device(section, moved(pos, axis, by)), device_id_type=MESH)
    first = pltpu.make_async_copy(small, sacc[3], ssem.at[0])
    first.start()
    pl.semaphore_wait(barrier, 9)

    def small_phase(phase):
        axis = ORDERS[0][phase]
        here = pos[axis]
        cur = sacc[phase + 1]
        if phase == 2:
            first.wait()
        sends = []
        for by in (1, 2, 3):
            to = moved(pos, axis, by)
            c = pltpu.make_async_remote_copy(cur.at[to[axis]], sgot[phase].at[by - 1], ssend.at[phase, by - 1], srecv.at[phase, by - 1], device_id=device(section, to), device_id_type=MESH)
            c.start()
            sends.append(c)
        def finish():
            for c in sends:
                c.wait()
            total = cur[here] + sgot[phase][0] + sgot[phase][1] + sgot[phase][2]
            if phase == 0:
                osmall[...] = total
            else:
                sacc[phase][...] = total
        return finish

    def add_into(dst, parts, slices):
        def one(i, carry):
            dst(i, [p[i].astype(F32) for p in parts])
            return carry
        lax.fori_loop(0, slices, one, 0)

    refs = (win, wout)
    for phase in (2, 1, 0):
        half = {2: 8, 1: 2, 0: 1}[phase]
        streams = [(j, kind) for j in range(3) for kind in (0, 1)]

        def own(j, kind, k, h):
            order = ORDERS[j]
            axis = order[phase]
            if phase == 2:
                at = list(pos)
                at[axis] = k
                return refs[kind].at[(j,) + block_index(order, 2, tuple(at), h)]
            return acc[phase + 1, kind].at[j, k, pl.ds(half * h, half)] if phase == 1 else acc[1, kind].at[j, k]

        def have(kind, h):
            return phase != 0 or h == kind

        def slot_ref(j, kind, slot):
            return got[phase, kind].at[(j, slot, 0) if phase == 0 else (j, slot)]

        def copy(n, slot, src, to):
            j, kind = streams[n]
            return pltpu.make_async_remote_copy(src, slot_ref(j, kind, slot), send.at[phase, n, slot], recv.at[phase, n, slot], device_id=device(section, to), device_id_type=MESH)

        finish_small = small_phase(phase)
        started = []
        loads = []
        for n, (j, kind) in enumerate(streams):
            axis = ORDERS[j][phase]
            left, right, far = (moved(pos, axis, by)[axis] for by in (3, 1, 2))
            to_left, to_right = moved(pos, axis, 3), moved(pos, axis, 1)
            for slot, k, h, to in ((0, far, 0, to_left), (1, far, 1, to_right), (2, left, 1, to_left), (3, right, 0, to_right)):
                if have(kind, h):
                    c = copy(n, slot, own(j, kind, k, h), to)
                    c.start()
                    started.append(c)
            if phase == 2:
                for i, (k, h) in enumerate(((left, 0), (right, 1))):
                    c = pltpu.make_async_copy(own(j, kind, k, h), mine[kind].at[j, i], lsem.at[n, i])
                    c.start()
                    loads.append(c)
        for n, (j, kind) in enumerate(streams):
            axis = ORDERS[j][phase]
            left, right = (moved(pos, axis, by)[axis] for by in (3, 1))
            to_left, to_right = moved(pos, axis, 3), moved(pos, axis, 1)
            for i, (slot, k, h, to) in enumerate(((0, left, 0, to_left), (1, right, 1, to_right))):
                if not have(kind, h):
                    continue
                copy(n, slot, slot_ref(j, kind, slot), to).wait_recv()
                if phase == 2:
                    loads[2 * n + i].wait()
                    part = mine[kind].at[j, i]
                else:
                    part = own(j, kind, k, h)
                buf = slot_ref(j, kind, slot)
                sum_refs(buf, [part], buf, BF, phase)
                c = copy(n, 4 + i, buf, to)
                c.start()
                started.append(c)
                if phase == 2:
                    c = pltpu.make_async_copy(own(j, kind, pos[axis], h), mine[kind].at[j, i], lsem.at[n, i])
                    c.start()
                    loads[2 * n + i] = c
        finish_small()
        for n, (j, kind) in enumerate(streams):
            axis = ORDERS[j][phase]
            to_left = moved(pos, axis, 3)
            for h, slots in ((0, (3, 4)), (1, (2, 5))):
                if not have(kind, h):
                    continue
                for slot in slots:
                    copy(n, slot, slot_ref(j, kind, slot), to_left).wait_recv()
                if phase == 2:
                    loads[2 * n + h].wait()
                    part = mine[kind].at[j, h]
                else:
                    part = own(j, kind, pos[axis], h)
                a, b = (slot_ref(j, kind, s) for s in slots)
                if phase == 0:
                    out = (oin, oout)[kind].at[j]
                    out[...] = part[...].astype(F32) + a[...].astype(F32) + b[...].astype(F32)
                else:
                    final_sum(j, kind, phase, h, part, a, b, acc[phase, kind])
        for c in started:
            c.wait_send()


def sum_refs(a, others, dst, dtype, phase):
    shape = a.shape
    if len(shape) == 2:
        dst[...] = (a[...].astype(F32) + others[0][...].astype(F32)).astype(dtype)
        return
    if len(shape) == 3:
        def one(i, c):
            o = others[0][i] if len(others[0].shape) == 3 else others[0][...]
            dst[i] = (a[i].astype(F32) + o.astype(F32)).astype(dtype)
            return c
        lax.fori_loop(0, shape[0], one, 0)
        return
    def one(i, c):
        for q in range(shape[1]):
            dst[i, q] = (a[i, q].astype(F32) + others[0][i, q].astype(F32)).astype(dtype)
        return c
    lax.fori_loop(0, shape[0], one, 0)


def final_sum(j, kind, phase, h, part, a, b, acc):
    order = ORDERS[j]
    if phase == 1:
        def one(i, c):
            acc[j, 2 * h + i] = (part[i].astype(F32) + a[i].astype(F32) + b[i].astype(F32)).astype(BF)
            return c
        lax.fori_loop(0, 2, one, 0)
        return
    low = min(order[:2])
    def one(i, c):
        for q in range(4):
            first, second = 2 * h + i, q
            at = (first, second) if order[1] == low else (second, first)
            acc[j, at[0], at[1]] = (part[i, q].astype(F32) + a[i, q].astype(F32) + b[i, q].astype(F32)).astype(BF)
        return c
    lax.fori_loop(0, 2, one, 0)


def scatter(win, wout, small):
    any_ = pl.BlockSpec(memory_space=pl.ANY)
    vm = pl.BlockSpec(memory_space=pltpu.VMEM)
    ri, ci = win.shape[-2:]
    ro, co = wout.shape[-2:]
    dims = {0: (ri, ci), 1: (ro, co)}
    scratch = []
    for phase in (2, 1, 0):
        for kind in (0, 1):
            n = {2: (2, 4), 1: (2,), 0: (1,)}[phase]
            scratch.append(pltpu.VMEM((3, 6) + n + dims[kind], BF))
    for phase in (2, 1):
        for kind in (0, 1):
            n = {2: (4, 4), 1: (4,)}[phase]
            scratch.append(pltpu.VMEM((3,) + n + dims[kind], BF))
    for kind in (0, 1):
        scratch.append(pltpu.VMEM((3, 2, 2, 4) + dims[kind], BF))
    for n in ((4, 4), (4,), ()):
        scratch.append(pltpu.VMEM((3,) + n + (8, 128), F32))
    for n in ((4, 4, 4), (4, 4), (4,)):
        scratch.append(pltpu.VMEM(n + (8, 128), F32))
    scratch += [pltpu.SemaphoreType.DMA((3, 6, 6)), pltpu.SemaphoreType.DMA((3, 6, 6)), pltpu.SemaphoreType.DMA((3, 3)), pltpu.SemaphoreType.DMA((3, 3)), pltpu.SemaphoreType.DMA((6, 2)), pltpu.SemaphoreType.DMA((1,))]
    return pl.pallas_call(
        scatter_kernel,
        out_shape=(jax.ShapeDtypeStruct((3, ri, ci), F32), jax.ShapeDtypeStruct((3, ro, co), F32), jax.ShapeDtypeStruct((8, 128), F32)),
        in_specs=[any_] * 3,
        out_specs=(vm,) * 3,
        scratch_shapes=scratch,
        compiler_params=pltpu.CompilerParams(collective_id=1, has_side_effects=True, vmem_limit_bytes=62 * 1024 * 1024),
        name="scatter_grads",
    )(win, wout, small)


def norm_piece(hidden, gain_in, valid_rows):
    return (
        hidden
        * lax.rsqrt(jnp.mean(hidden * hidden, axis=-1, keepdims=True) + EPSILON)
        * gain_in
        * valid_rows[:, None]
    )


def mix_piece(projected, kernel_taps, kernel_bias, rate_bias, decay_log, segment):
    length = projected.shape[0]
    gate_z = projected[:, :DI]
    channels = projected[:, DI : DI + CC]
    rate_raw = projected[:, DI + CC :]
    padded = jnp.concatenate([jnp.zeros((KC - 1, CC), jnp.float32), channels], axis=0)
    seg_pad = jnp.concatenate([jnp.full((KC - 1,), -1, jnp.int32), segment], axis=0)
    convolved = jnp.zeros_like(channels) + kernel_bias[None, :]
    for offset in range(KC):
        same_segment = (seg_pad[offset : offset + length] == segment).astype(jnp.float32)
        convolved = (
            convolved
            + kernel_taps[offset][None, :]
            * padded[offset : offset + length]
            * same_segment[:, None]
        )
    activated = jax.nn.silu(convolved)
    heads_x = activated[:, :DI].reshape(length, DI // HEAD_DIM, HEAD_DIM)
    in_state = activated[:, DI : DI + N]
    out_state = activated[:, DI + N :]
    step_size = jax.nn.softplus(rate_raw + rate_bias[None, :])
    cumulative = jnp.cumsum(step_size * (-jnp.exp(decay_log))[None, :], axis=0)
    return (gate_z, heads_x, in_state, out_state, step_size, cumulative)


def weight_piece(scores, cumulative, step_size, segment):
    length = scores.shape[0]
    positions = jnp.arange(length, dtype=jnp.int32)
    allowed = (positions[:, None] >= positions[None, :]) & (segment[:, None] == segment[None, :])
    across = cumulative.T
    gaps = across[:, :, None] - across[:, None, :]
    decay = jnp.exp(jnp.where(allowed[None, :, :], gaps, 0.0)) * allowed[None, :, :].astype(
        jnp.float32
    )
    return scores[None, :, :] * decay * step_size.T[:, None, :]


def gate_piece(ssd_out, gate_z, gain_out):
    gated = ssd_out * jax.nn.silu(gate_z)
    return gated * lax.rsqrt(jnp.mean(gated * gated, axis=-1, keepdims=True) + EPSILON) * gain_out


def layer_parts(hidden, segment, valid_rows, weights, heads):
    proj_in, proj_out, kernel_taps, kernel_bias, gain_in, gain_out = weights
    rate_bias, decay_log, skip_gain = heads
    length = hidden.shape[0]
    normed_in, norm_pull = jax.vjp(
        lambda a, b: norm_piece(a, b, valid_rows), hidden, gain_in.astype(jnp.float32)
    )
    input_low = normed_in.astype(jnp.bfloat16)
    projected = from_panels([jnp.dot(input_low, w, preferred_element_type=jnp.float32) for w in proj_in])
    mixed, mix_pull = jax.vjp(
        lambda a, b, c, d, e: mix_piece(a, b, c, d, e, segment),
        projected,
        kernel_taps.astype(jnp.float32),
        kernel_bias.astype(jnp.float32),
        rate_bias,
        decay_log,
    )
    gate_z, heads_x, in_state, out_state, step_size, cumulative = mixed
    x_low = heads_x.astype(jnp.bfloat16)
    state_in_low = in_state.astype(jnp.bfloat16)
    state_out_low = out_state.astype(jnp.bfloat16)
    scores = jnp.dot(state_out_low, state_in_low.T, preferred_element_type=jnp.float32)
    mix_weights, weight_pull = jax.vjp(
        lambda a, b, c: weight_piece(a, b, c, segment), scores, cumulative, step_size
    )
    mix_low = mix_weights.astype(jnp.bfloat16)
    ssd_out = (
        jnp.einsum("hts,shp->thp", mix_low, x_low, preferred_element_type=jnp.float32)
        + skip_gain[None, :, None] * heads_x
    )
    ssd_out = ssd_out.reshape(length, DI)
    normed, gate_pull = jax.vjp(gate_piece, ssd_out, gate_z, gain_out.astype(jnp.float32))
    normed_low = normed.astype(jnp.bfloat16)
    return (
        input_low,
        norm_pull,
        mix_pull,
        heads_x,
        x_low,
        state_in_low,
        state_out_low,
        weight_pull,
        mix_low,
        gate_pull,
        normed_low,
    )


def out_product(low, panels):
    return jnp.concatenate([jnp.dot(low, w, preferred_element_type=jnp.float32) for w in panels], axis=1)


def layer_forward(hidden, segment, valid_rows, weights, heads):
    parts = layer_parts(hidden, segment, valid_rows, weights, heads)
    return hidden + out_product(parts[10], weights[1]), parts


def layer_backward(parts, upstream, weights, heads):
    proj_in, proj_out = (weights[0], weights[1])
    skip_gain = heads[2]
    length = upstream.shape[0]
    (
        input_low,
        norm_pull,
        mix_pull,
        heads_x,
        x_low,
        state_in_low,
        state_out_low,
        weight_pull,
        mix_low,
        gate_pull,
        normed_low,
    ) = parts
    upstream_low = upstream.astype(jnp.bfloat16)
    d_normed = sum(jnp.dot(upstream_low[:, 512 * j : 512 * j + 512], w.T, preferred_element_type=jnp.float32) for j, w in enumerate(proj_out))
    d_ssd, d_gate_z, d_gain_out = gate_pull(d_normed)
    d_ssd_low = d_ssd.astype(jnp.bfloat16).reshape(length, DI // HEAD_DIM, HEAD_DIM)
    d_ssd_wide = d_ssd_low.astype(jnp.float32)
    d_mix = jnp.einsum("thp,shp->hts", d_ssd_low, x_low, preferred_element_type=jnp.float32)
    d_heads_x = jnp.einsum("hts,thp->shp", mix_low, d_ssd_low, preferred_element_type=jnp.float32)
    d_heads_x = d_heads_x + skip_gain[None, :, None] * d_ssd_wide
    d_skip = jnp.sum(d_ssd_wide * heads_x, axis=(0, 2))
    d_scores, d_cumulative, d_step = weight_pull(d_mix)
    d_scores_low = d_scores.astype(jnp.bfloat16)
    d_out_state = jnp.dot(d_scores_low, state_in_low, preferred_element_type=jnp.float32)
    d_in_state = jnp.dot(d_scores_low.T, state_out_low, preferred_element_type=jnp.float32)
    d_projected, d_taps, d_kernel_bias, d_rate_bias, d_decay_log = mix_pull(
        (d_gate_z, d_heads_x, d_in_state, d_out_state, d_step, d_cumulative)
    )
    d_projected_low = d_projected.astype(jnp.bfloat16)
    d_panels = to_panels(d_projected_low)
    d_normed_in = sum(jnp.dot(d, w.T, preferred_element_type=jnp.float32) for d, w in zip(d_panels, proj_in))
    d_hidden, d_gain_in = norm_pull(d_normed_in)
    return (
        upstream + d_hidden,
        jnp.concatenate([input_low, normed_low, upstream_low] + d_panels, axis=1),
        (d_taps, d_kernel_bias, d_gain_in, d_gain_out, (d_rate_bias, d_decay_log, d_skip)),
    )


def spread_small(grads):
    taps, bias, gain_in, gain_out, heads = grads
    return pack_small(
        jnp.transpose(taps.reshape(4, 64, 52), (1, 0, 2)),
        bias.reshape(64, 52),
        gain_in.reshape(64, 24),
        gain_out.reshape(64, 48),
        heads,
    )


def body(
    ends_in,
    seg_ids,
    block_counts,
    in_weight,
    conv_weight,
    conv_bias,
    pre_gain,
    gate_gain,
    out_weight,
    dt_bias,
    a_log,
    skip,
):
    section = lax.axis_index("section")
    length = seg_ids.shape[1]
    wide = lambda v: v[0].astype(F32)
    small = pack_small(wide(conv_weight), wide(conv_bias), wide(pre_gain), wide(gate_gain), (wide(dt_bias), wide(a_log), wide(skip)))
    own_in = jnp.stack(to_panels(in_weight[0]))
    own_out = jnp.stack([out_weight[0][:, 512 * j : 512 * j + 512] for j in range(3)])
    all_in, all_out, all_small = gather(own_in, own_out, small)
    weights, heads = [], []
    for l in range(2):
        taps, bias, gain_in, gain_out, head = unpack_small(all_small[l].reshape(64, 8, 128))
        panels_in = [all_in[l, j].reshape(D, 2176) for j in range(3)]
        panels_out = [all_out[l, j].reshape(DI, 512) for j in range(3)]
        weights.append((panels_in, panels_out, taps, bias, gain_in, gain_out))
        heads.append(head)
    mine = lax.dynamic_index_in_dim(ends_in[0].reshape(2, length, D), section, 0, keepdims=False)
    theirs = lax.dynamic_index_in_dim(ends_in[0].reshape(2, length, D), 1 - section, 0, keepdims=False)
    swap = [(0, 1), (1, 0)]
    got = lax.ppermute(theirs, "section", swap)
    block_in = jnp.where(section == 0, mine, got).astype(F32)
    cotangent = jnp.where(section == 0, got, mine).astype(F32)
    segment = lax.dynamic_index_in_dim(seg_ids, section, 0, keepdims=False)
    count = lax.dynamic_index_in_dim(block_counts, section, 0, keepdims=False)
    valid_rows = (jnp.arange(length, dtype=jnp.int32) < count).astype(F32)

    first, first_parts = layer_forward(block_in, segment, valid_rows, weights[0], heads[0])
    middle = first.astype(BF).astype(F32)
    second, second_parts = layer_forward(middle, segment, valid_rows, weights[1], heads[1])
    d_middle, second_terms, second_small = layer_backward(second_parts, cotangent, weights[1], heads[1])
    d_middle = d_middle.astype(BF).astype(F32)
    d_first, first_terms, first_small = layer_backward(first_parts, d_middle, weights[0], heads[0])

    leading = section == 0
    keep = jnp.where(leading, first_terms, second_terms)
    got_terms = lax.ppermute(jnp.where(leading, second_terms, first_terms), "section", swap)
    terms = jnp.concatenate([keep, got_terms], axis=0)
    spread = [spread_small(first_small), spread_small(second_small)]
    small_sum = jnp.where(leading, spread[0], spread[1]) + lax.ppermute(jnp.where(leading, spread[1], spread[0]), "section", swap)
    d_first, second = d_first.astype(BF), second.astype(BF)
    end_got = lax.ppermute(jnp.where(leading, second, d_first), "section", swap)
    ends_out = jnp.where(leading, jnp.stack([d_first, end_got]), jnp.stack([end_got, second])).reshape(1, 2 * length, D)

    u, o, dv = terms[:, :D], terms[:, D : D + DI], terms[:, D + DI : 2 * D + DI]
    dp = terms[:, 2 * D + DI :]
    d_in = jnp.stack([jnp.dot(u.T, dp[:, 2176 * j : 2176 * j + 2176], preferred_element_type=F32).astype(BF) for j in range(3)]).reshape(3, 4, 4, 4, 24, 2176)
    d_out = jnp.stack([jnp.dot(o.T, dv[:, 512 * j : 512 * j + 512], preferred_element_type=F32).astype(BF) for j in range(3)]).reshape(3, 4, 4, 4, 48, 512)
    sum_in, sum_out, sums = scatter(d_in, d_out, small_sum.reshape(4, 4, 4, 8, 128))
    d_in_weight = from_panels([sum_in[j] for j in range(3)])
    d_out_weight = jnp.concatenate([sum_out[j] for j in range(3)], axis=1)
    return (
        ends_out,
        d_in_weight[None],
        sums[None, 0:4, 0:52],
        sums[None, 4, 0:52],
        sums[None, 5, 0:24],
        sums[None, 6, 0:48],
        d_out_weight[None],
        sums[None, 7, 0:48],
        sums[None, 5, 64:112],
        sums[None, 6, 64:112],
    )


def solution(mesh):
    placed = (
        P("section", "dp", None),
        P("dp", None),
        P("dp"),
        P("section", "dp", None),
        P("section", None, "dp"),
        P("section", "dp"),
        P("section", "dp"),
        P("section", "dp"),
        P("section", "dp", None),
        P("section", None),
        P("section", None),
        P("section", None),
    )
    return jax.shard_map(
        body,
        mesh=mesh,
        in_specs=placed,
        out_specs=(
            P("section", "dp", None),
            P("section", "dp", None),
            P("section", None, "dp"),
            P("section", "dp"),
            P("section", "dp"),
            P("section", "dp"),
            P("section", "dp", None),
            P("section", None),
            P("section", None),
            P("section", None),
        ),
        check_vma=False,
    )
```

time: 1610 us -> 705 us (0.44)
  waiting for transfers between devices: 554 us -> 0.79 us
  blocking collectives: 531 us -> 0 us
  Pallas kernels: 0 us -> 269 us
  matrix products: 251 us -> 107 us
  local copies, waits for them, and re-layouts: 115 us -> 215 us
  other arithmetic: 123 us -> 99.6 us
  between operations: 20.1 us -> 3.04 us
    unnamed x1 -> x0, blocking collectives: 352 us -> none
    unnamed x7 -> x0, waiting for transfers between devices: 317 us -> none
    pallas_call x0 -> x2, Pallas kernels: none -> 269 us  [the longest x1 145 us: gather(): pl.pallas_call(gather_kernel, out_shape=(jax.ShapeDtypeStruct((2, 3, 4, 4...]
    reduce_scatter x1 -> x0, waiting for transfers between devices: 237 us -> none  [body(): lax.psum_scatter(totals[1], 'dp', scatter_dimension=0, tiled=True)]
    all_gather x1 -> x0, blocking collectives: 179 us -> none  [body(): lax.all_gather(shards[2], 'dp', axis=1, tiled=True)]
    dot_general x20 -> x30, matrix products: 217 us -> 73.9 us  [the longest x6 21.7 us: layer_parts(): jnp.dot(input_low, w, preferred_element_type=jnp.float32)]
    slice x1 -> x2, local copies, waits for them, and re-layouts: 69.1 us -> 2.25 us  [mix_piece(): kernel_taps[offset][None, :] * padded[offset:offset + length]]
    slice x5 -> x25, local copies, waits for them, and re-layouts: 5.77 us -> 67.3 us  [the longest x1 27.1 us: body(): panels_in = [all_in[l, j].reshape(D, 2176) for j in range(3)]]
  transfers between devices with their start and end apart: 9 -> 4, of which waited for: 3 -> 1; matrix products, arithmetic and copies ran while one was open for 16% -> 16% of each run, Pallas kernels for 0% -> 21%
where the time goes in v1:
time: 705 us; the launch traced here: 696 us
  Pallas kernels  269 us (38%)
  local copies, waits for them, and re-layouts  215 us (30%)
  matrix products  107 us (15%)
  other arithmetic  99.6 us (14%)
    pallas_call x1, Pallas kernels, gather(): pl.pallas_call(gather_kernel, out_shape=(jax.ShapeDtypeStruct((2, 3, 4, 4...  145 us
    pallas_call x1, Pallas kernels, scatter(): pl.pallas_call(scatter_kernel, out_shape=(jax.ShapeDtypeStruct((3, ri, ci...  125 us
    unnamed x420, local copies, waits for them, and re-layouts  67.6 us
    slice x1, local copies, waits for them, and re-layouts, body(): panels_in = [all_in[l, j].reshape(D, 2176) for j in range(3)]  27.1 us
    dot_general x6, matrix products, layer_parts(): jnp.dot(input_low, w, preferred_element_type=jnp.float32)  21.7 us
    slice x12, local copies, waits for them, and re-layouts, from_panels(): z = [p[g // 2][:, 1024 * (g % 2):1024 * (g % 2) + 512] for g in range(6)]  19 us
    dot_general x6, matrix products, layer_backward(): jnp.dot(d, w.T, preferred_element_type=jnp.float32)  18.9 us
    unnamed x19, other arithmetic  18.3 us
  transfers between devices with their start and end apart: 4, of which 1 were waited for; matrix products, arithmetic and copies ran while one was open for 16% of the time, Pallas kernels for 21%

profile of v1, /device:TPU:0, one launch (start us, length us, event | category | flops | bytes accessed | tf_op | source)
XLA Modules:
  0.0 696.4 jit_solution(6828782395876327691)
XLA Ops:
  12.1 144.5 %gather_weights.1 = (bf16[2,3,4,4,4,24,2176]{6,5,4,3,2,1,0:T(8,128)(2,1)}, bf16[2,3,4,4,4,48,512]{6,5,4,3,2,1,0:T(8,128)(2,1)}, f32[2,4,4,4,8,128]{5,4,3,2,1,0:T(8,128)}) custom-call(bf16[3,24,2176]{2,1,0:T(8,128)(2,1)} %pad_maximum_fusion.3.in_ref, bf16[3,48,512]{2,1,0:T(8,128)(2,1)} %pad_maximum_fusion.6.out_ref, f32[8,128]{1,0:T(8,128)} %concatenate.149.small_ref), custom_call_target="tpu_custom_call" | custom-call | tf_op jit(solution)/shard_map/gather_weights/pallas_call | solution.py:185
  162.3 27.1 %fusion.158 = (bf16[1,1,4,4,4,24,2176]{6,5,4,3,2,1,0:T(8,128)(2,1)}, bf16[1,1,4,4,4,24,2176]{6,5,4,3,2,1,0:T(8,128)(2,1)}, bf16[1,1,4,4,4,24,2176]{6,5,4,3,2,1,0...) fusion(bf16[2,3,4,4,4,24,2176]{6,5,4,3,2,1,0:T(8,128)(2,1)} %ge, ...), kind=kLoop, calls=%fused_computation.491 | loop fusion | bytes 80216064 | tf_op jit(solution)/shard_map/slice | solution.py:609
  191.0 12.4 %fusion.159 = (bf16[1,1,4,4,4,48,512]{6,5,4,3,2,1,0:T(8,128)(2,1)}, bf16[1,1,4,4,4,48,512]{6,5,4,3,2,1,0:T(8,128)(2,1)}, bf16[1,1,4,4,4,48,512]{6,5,4,3,2,1,0:T(...) fusion(bf16[2,3,4,4,4,48,512]{6,5,4,3,2,1,0:T(8,128)(2,1)} %get, ...), kind=kLoop, calls=%fused_computation.492 | loop fusion | bytes 37748736 | tf_op jit(solution)/shard_map/slice | solution.py:610
  228.3 4.1 fusion.130
  238.8 4.1 fusion.132
  242.9 4.1 fusion.134
  281.5 4.6 multiply_reduce_fusion.19
  293.0 4.1 fusion.138
  297.1 4.1 fusion.140
  327.7 5.0 multiply_reduce_fusion.18
  334.7 3.4 fusion.51
  346.3 4.1 multiply_reduce_fusion.12
  352.8 5.2 fusion.14
  372.4 7.1 %multiply_reduce_fusion.7 = (f32[3328]{0:T(1024)}, f32[3328]{0:T(1024)}, f32[3328]{0:T(1024)}, f32[3328]{0:T(1024)}, f32[3328]{0:T(1024)}, /*index=5*/f32[128,3328]{1,0:T(8,128)S(1)}) fusion(f32[128,3328]{1,0:T(8,128)} %copy-done.31, f32[128]{0:T(128)} %get-tuple-element.239, f32[128]{0:T(128)} %get-tuple-element.240, f32[128]{0:T(128)} %get-tuple-element.238, ...), kind=kLoop, calls=%fused_computation.67 | loop fusion | flops 9780992 | bytes 6883840 | tf_op jit(solution)/shard_map/transpose(jvp())/reduce_sum | solution.py:443
  424.7 5.0 fusion.16
  445.6 4.1 multiply_reduce_fusion.11
  484.8 5.3 broadcast_select_fusion.1
  493.5 6.7 fusion.39
  525.4 3.9 convolution_convert_fusion.5
  529.3 3.9 convolution_convert_fusion.4
  533.2 3.8 convolution_convert_fusion.3
  537.0 8.4 %pad_maximum_fusion.1.wout = bf16[3,4,4,4,48,512]{5,4,3,2,1,0:T(8,128)(2,1)} fusion(bf16[1,4,4,4,48,512]{5,4,3,2,1,0:T(8,128)(2,1)} %bitcast.270, bf16[1,4,4,4,48,512]{5,4,3,2,1,0:T(8,128)(2,1)} %bitcast.269, bf16[1,4,4,4,48,512]{5,4,3,2,1,0:T(8,128)(2,1)} %bitcast.268), kind=kLoop, calls=%fused_computation.16 | loop fusion | flops 9437184 | bytes 18874368 | tf_op jit(solution)/shard_map/stack | solution.py:643
  555.8 7.4 %pad_maximum_fusion.win = bf16[3,4,4,4,24,2176]{5,4,3,2,1,0:T(8,128)(2,1)} fusion(bf16[1,4,4,4,24,2176]{5,4,3,2,1,0:T(8,128)(2,1)S(1)} %bitcast.259, bf16[1,4,4,4,24,2176]{5,4,3,2,1,0:T(8,128)(2,1)S(1)} %bitcast.258, bf16[1,4,4,4,24,2176]{5,4,3,2,1,0:T(8,128)(2,1)S(1)} %bitcast.257), kind=kLoop, calls=%fused_computation | loop fusion | flops 20054016 | bytes 40108032 | tf_op jit(solution)/shard_map/stack | solution.py:642
  563.2 124.6 %scatter_grads.1 = (f32[3,24,2176]{2,1,0:T(8,128)}, f32[3,48,512]{2,1,0:T(8,128)}, f32[8,128]{1,0:T(8,128)}) custom-call(bf16[3,4,4,4,24,2176]{5,4,3,2,1,0:T(8,128)(2,1)} %pad_maximum_fusion.win, bf16[3,4,4,4,48,512]{5,4,3,2,1,0:T(8,128)(2,1)} %pad_maximum_fusion.1.wout, f32[4,4,4,8,128]{4,3,2,1,0:T(8,128)} %bitcast.293), custom_call_target="tpu_custom_call" | custom-call | tf_op jit(solution)/shard_map/scatter_grads/pallas_call | solution.py:411
  (644 shorter events, 286.2 us)
Async XLA Ops:
  0.6 189.7 %copy-start = (s32[2,128]{1,0:T(2,128)S(1)}, s32[2,128]{1,0:T(2,128)}, u32[]{:S(2)}) copy-start(s32[2,128]{1,0:T(2,128)} %param.14) | copy-start | bytes 3076
  2.4 224.1 %collective-permute-start = (bf16[128,1536]{1,0:T(8,128)(2,1)}, bf16[128,1536]{1,0:T(8,128)(2,1)}, u32[]{:S(2)}, u32[]{:S(2)}) collective-permute-start(bf16[128,1536]{1,0:T(8,128)(2,1)} %dynamic-slice_bitcast_fusion), channel_id=1, source_target_pairs={{0,64},{64,0},{1,65},{65,1},{2,66},{66,2},{3,67},{67,3},{4,68},{68... | collective-permute-start | bytes 1179656 | tf_op jit(solution)/shard_map/ppermute | solution.py:616
  157.7 48.0 %copy-start.55 = (f32[1,4,4,4,8,128]{5,4,3,2,1,0:T(8,128)}, f32[1,4,4,4,8,128]{5,4,3,2,1,0:T(8,128)S(1)}, u32[]{:S(2)}) copy-start(f32[1,4,4,4,8,128]{5,4,3,2,1,0:T(8,128)S(1)} %get-tuple-element.199) | copy-start | bytes 786436
  191.0 18.4 %copy-start.157 = (s32[2]{0:T(128)S(1)}, s32[2]{0:T(128)}, u32[]{:S(2)}) copy-start(s32[2]{0:T(128)} %param.15) | copy-start | bytes 28
  203.3 84.0 %copy-start.11 = (bf16[1,1,4,4,4,48,512]{6,5,4,3,2,1,0:T(8,128)(2,1)}, bf16[1,1,4,4,4,48,512]{6,5,4,3,2,1,0:T(8,128)(2,1)S(1)}, u32[]{:S(2)}) copy-start(bf16[1,1,4,4,4,48,512]{6,5,4,3,2,1,0:T(8,128)(2,1)S(1)} %get-tuple-element.112) | copy-start | bytes 9437188
  227.8 61.7 %copy-start.2 = (bf16[128,1536]{1,0:T(8,128)(2,1)}, bf16[128,1536]{1,0:T(8,128)(2,1)S(1)}, u32[]{:S(2)}) copy-start(bf16[128,1536]{1,0:T(8,128)(2,1)S(1)} %get-tuple-element.101) | copy-start | bytes 1179652
  289.4 122.7 %copy-start.5 = (bf16[128,1536]{1,0:T(8,128)(2,1)}, bf16[128,1536]{1,0:T(8,128)(2,1)S(1)}, u32[]{:S(2)}) copy-start(bf16[128,1536]{1,0:T(8,128)(2,1)S(1)} %get-tuple-element.94) | copy-start | bytes 1179652
  292.9 34.7 %copy-start.126 = (f32[48,128]{1,0:T(8,128)}, f32[48,128]{1,0:T(8,128)S(1)}, u32[]{:S(2)}) copy-start(f32[48,128]{1,0:T(8,128)S(1)} %copy.131) | copy-start | bytes 73732
  293.0 34.7 %copy-start.129 = (f32[48,128]{1,0:T(8,128)}, f32[48,128]{1,0:T(8,128)S(1)}, u32[]{:S(2)}) copy-start(f32[48,128]{1,0:T(8,128)S(1)} %copy.135) | copy-start | bytes 73732
  312.1 15.5 %copy-start.100 = (f32[128,128]{1,0:T(8,128)}, f32[128,128]{1,0:T(8,128)S(1)}, u32[]{:S(2)}) copy-start(f32[128,128]{1,0:T(8,128)S(1)} %fusion.87) | copy-start | bytes 196612
  334.7 11.6 %copy-start.142 = (f32[128]{0:T(128)}, f32[128]{0:T(128)S(1)}, u32[]{:S(2)}) copy-start(f32[128]{0:T(128)S(1)} %fusion.114) | copy-start | bytes 1540
  387.9 17.8 %copy-start.41 = (f32[128,512]{1,0:T(8,128)}, f32[128,512]{1,0:T(8,128)S(1)}, u32[]{:S(2)}) copy-start(f32[128,512]{1,0:T(8,128)S(1)} %fusion.168) | copy-start | bytes 786436
  387.9 10.2 %slice-start.10 = ((s8[6684672]{0:T(1024)(128)(4,1)}), s8[4194304]{0:T(1024)(128)(4,1)S(1)}, s32[]{:S(2)}) async-start(s8[6684672]{0:T(1024)(128)(4,1)} %bitcast.254), calls=%async_computation.10 | async-start | bytes 8388608
  388.5 17.2 %copy-start.42 = (f32[128,512]{1,0:T(8,128)}, f32[128,512]{1,0:T(8,128)S(1)}, u32[]{:S(2)}) copy-start(f32[128,512]{1,0:T(8,128)S(1)} %fusion.169) | copy-start | bytes 786436
  422.5 31.5 %copy-start.9 = (f32[128,3072]{1,0:T(8,128)}, f32[128,3072]{1,0:T(8,128)S(1)}, u32[]{:S(2)}) copy-start(f32[128,3072]{1,0:T(8,128)S(1)} %get-tuple-element.116) | copy-start | bytes 4718596
  435.5 10.0 %copy-start.30 = (f32[128,3328]{1,0:T(8,128)S(1)}, f32[128,3328]{1,0:T(8,128)}, u32[]{:S(2)}) copy-start(f32[128,3328]{1,0:T(8,128)} %copy-done.29) | copy-start | bytes 5111812
  454.4 21.2 %slice-start.2 = ((s8[6684672]{0:T(1024)(128)(4,1)}), s8[2490368]{0:T(1024)(128)(4,1)S(1)}, s32[]{:S(2)}) async-start(s8[6684672]{0:T(1024)(128)(4,1)} %bitcast.240), calls=%async_computation.2 | async-start | bytes 4980736
  490.1 35.3 %collective-permute-start.2 = (bf16[128,12672]{1,0:T(8,128)(2,1)}, bf16[128,12672]{1,0:T(8,128)(2,1)}, u32[]{:S(2)}, u32[]{:S(2)}) collective-permute-start(bf16[128,12672]{1,0:T(8,128)(2,1)} %get-tuple-element.115), channel_id=1, source_target_pairs={{0,64},{64,0},{1,65},{65,1},{2,66},{66,2},{3,67},{67,3},{4,68},{68... | collective-permute-start | bytes 9732104 | tf_op jit(solution)/shard_map/ppermute | solution.py:632
  500.2 19.5 %copy-start.150 = (f32[128]{0:T(128)S(1)}, f32[128]{0:T(128)}, u32[]{:S(2)}) copy-start(f32[128]{0:T(128)} %copy-done.149) | copy-start | bytes 1540
  510.6 9.7 %copy-start.4 = (bf16[128,1536]{1,0:T(8,128)(2,1)S(1)}, bf16[128,1536]{1,0:T(8,128)(2,1)}, u32[]{:S(2)}) copy-start(bf16[128,1536]{1,0:T(8,128)(2,1)} %copy-done.2) | copy-start | bytes 1179652
  510.6 9.7 %copy-start.6 = (bf16[128,1536]{1,0:T(8,128)(2,1)S(1)}, bf16[128,1536]{1,0:T(8,128)(2,1)}, u32[]{:S(2)}) copy-start(bf16[128,1536]{1,0:T(8,128)(2,1)} %copy-done.5) | copy-start | bytes 1179652
  510.6 9.7 %copy-start.40 = (bf16[128,1536]{1,0:T(8,128)(2,1)S(1)}, bf16[128,1536]{1,0:T(8,128)(2,1)}, u32[]{:S(2)}) copy-start(bf16[128,1536]{1,0:T(8,128)(2,1)} %copy-done.39) | copy-start | bytes 1179652
  518.5 4.1 collective-permute-start.3
  522.1 2.2 collective-permute-start.1
  (154 other events, 631.0 us)

commit v2 on v0

v2 whole, which is shorter than its diff:
```python
import jax
import jax.numpy as jnp
from jax import lax
from jax.experimental import pallas as pl
from jax.experimental.pallas import tpu as pltpu
from jax.sharding import PartitionSpec as P

D = 1536
DI = 3072
N = 128
H = 48
CC = 3328
T = 128
EPSILON = 1e-05
F32 = jnp.float32
BF = jnp.bfloat16
GROUPS = 6
LOG2E = 1.4426950408889634
MESH = pl.DeviceIdType.MESH
KINDS = ((48, 1024), (48, 512), (16, 256))
ORDERS = ((2, 1, 0), (1, 0, 2), (0, 2, 1))
STREAMS = tuple((j, kind) for j in range(3) for kind in range(3))


def moved(pos, axis, by):
    out = list(pos)
    out[axis] = lax.rem(pos[axis] + by, 4)
    return tuple(out)


def block_index(order, phase, pos, half, sub=None):
    index = [pos[0], pos[1], pos[2]]
    for a in order[:phase]:
        index[a] = slice(None)
    if phase > 0 and half is not None:
        index[min(order[:phase])] = pl.ds(2 * half, 2) if sub is None else 2 * half + sub
    return tuple(index)


def has_half(kind, phase, half):
    return phase != 0 or half == (0 if kind == 0 else 1)


def dot(a, b, dims=((1,), (0,))):
    return lax.dot_general(a, b, (dims, ((), ())), preferred_element_type=F32)


def sigmoid(v):
    return 1.0 / (1.0 + jnp.exp(-v))


def total(v):
    return jnp.sum(v, axis=0, keepdims=True)


def exact_dot(zeros_ones, wide, dims=((1,), (0,)), flip=False, terms=3):
    out = None
    for _ in range(terms):
        term = wide.astype(BF)
        wide = wide - term.astype(F32)
        part = dot(term, zeros_ones, dims) if flip else dot(zeros_ones, term, dims)
        out = part if out is None else out + part
    return out


def keep_lanes(v, keep):
    return jnp.where(keep, v, jnp.zeros_like(v))


def step_kernel(*refs):
    it = iter(refs)
    take = lambda n: [next(it) for _ in range(n)]
    ends, segs, counts, win, taps_in, bias_in, pre_in, gate_in, wout, dtb_in, alog_in, skip_in = take(12)
    ends_out, d_win, d_taps, d_bias, d_pre, d_gate, d_wout, d_dtb, d_alog, d_skip = take(10)
    gath, grad, recv2, recv1, recv0 = take(3), take(3), take(3), take(3), take(3)
    wgot, egot, fgot, ggot, gs, par, hp, gr, tgot, sg2, sg1, sg0, swapped, leaving, us_, os_, dvs, dps, dpes = take(19)
    (s_misc, r_misc, s_ag, r_ag, s_small, r_small, s_sib, r_sib, s_rs, r_rs, s_terms, r_terms, own_sem, go_sem) = take(14)

    section = lax.axis_index("section")
    dp = lax.axis_index("dp")
    pos = (lax.div(dp, 16), lax.rem(lax.div(dp, 4), 4), lax.rem(dp, 4))
    parity = lax.rem(pos[2], 2)
    even = parity == 0
    partner = (pos[0], pos[1], pos[2] + 1 - 2 * parity)
    leading = section == 0

    def device(at, s=None):
        return {"section": section if s is None else s, "dp": at[0] * 16 + at[1] * 4 + at[2]}

    sibling = device(pos, 1 - section)

    def remote(src, dst, s, r, to):
        return pltpu.make_async_remote_copy(src, dst, s, r, device_id=to, device_id_type=MESH)

    def misc(n, src, dst, to):
        return remote(src, dst, s_misc.at[n], r_misc.at[n], to)

    barrier = pltpu.get_barrier_semaphore()
    for axis in range(3):
        for by in (1, 2, 3):
            pl.semaphore_signal(barrier, inc=1, device_id=device(moved(pos, axis, by)), device_id_type=MESH)
    pl.semaphore_signal(barrier, inc=1, device_id=sibling, device_id_type=MESH)

    def group_columns(g):
        return [pl.ds(pl.multiple_of(512 * g + first, 128), 512) for first in (0, DI)]

    def ag_copy(n, phase, slot, src, index, to):
        j, kind = STREAMS[n]
        return remote(src, gath[kind].at[section, j].at[index], s_ag.at[n, phase], r_ag.at[n, phase, slot], device(to))

    def ag_start(n, phase, unit=None):
        j, kind = STREAMS[n]
        order = ORDERS[j]
        right, left = moved(pos, order[phase], 1), moved(pos, order[phase], 3)
        for slot, (h, to) in enumerate(((0, right), (1, left), (1, right), (0, left))):
            if has_half(kind, phase, h):
                index = block_index(order, phase, pos, h)
                src = unit[kind].at[j] if phase == 0 else gath[kind].at[section, j].at[index]
                ag_copy(n, phase, slot, src, index, to).start()

    def ag_pieces(n, phase, at, h):
        order = ORDERS[STREAMS[n][0]]
        if phase < 2:
            return [block_index(order, phase, at, h)]
        return [block_index(order, phase, at, h, q) for q in range(2)]

    def to_sibling(n, index):
        j, kind = STREAMS[n]
        ref = gath[kind].at[section, j].at[index]
        remote(ref, ref, s_sib.at[n], r_sib.at[n], sibling).start()

    def ag_arrived(n, phase, slot, index):
        j, kind = STREAMS[n]
        ag_copy(n, phase, slot, gath[kind].at[section, j].at[index], index, moved(pos, 0, 1)).wait_recv()
        if phase == 2:
            to_sibling(n, index)

    def ag_forward(phase):
        for n, (j, kind) in enumerate(STREAMS):
            order = ORDERS[j]
            right, left = moved(pos, order[phase], 1), moved(pos, order[phase], 3)
            for slot, h, source, to in ((0, 0, left, right), (1, 1, right, left)):
                if has_half(kind, phase, h):
                    ag_arrived(n, phase, slot, block_index(order, phase, source, h))
                    for q, index in enumerate(ag_pieces(n, phase, source, h)):
                        ag_copy(n, phase, 4 + 2 * slot + q, gath[kind].at[section, j].at[index], index, to).start()

    def ag_rest(phase):
        for n, (j, kind) in enumerate(STREAMS):
            order = ORDERS[j]
            right, left = moved(pos, order[phase], 1), moved(pos, order[phase], 3)
            for slot, h, source in ((2, 1, left), (3, 0, right)):
                if has_half(kind, phase, h):
                    ag_arrived(n, phase, slot, block_index(order, phase, source, h))
        for q in range(2 if phase == 2 else 1):
            for n, (j, kind) in enumerate(STREAMS):
                far = moved(pos, ORDERS[j][phase], 2)
                for slot in (0, 1):
                    if has_half(kind, phase, slot):
                        ag_arrived(n, phase, 4 + 2 * slot + q, ag_pieces(n, phase, far, slot)[q])

    def ag_sent(phase):
        for n, (j, kind) in enumerate(STREAMS):
            index = {0: (0, 0, pl.ds(0, 3)), 1: (0, pl.ds(0, 3)), 2: (pl.ds(0, 3),)}[phase]
            ref = gath[kind].at[section, j].at[index]
            remote(ref, ref, s_ag.at[n, phase], r_ag.at[n, phase, 0], sibling).wait_send()

    def small_gather(phase):
        axis = (2, 1, 0)[phase]
        index = tuple(pos[: 3 - phase])
        sent = []
        for by in (1, 2, 3):
            ref = gs.at[section].at[index]
            c = remote(ref, ref, s_small.at[phase, by - 1], r_small.at[phase, by - 1], device(moved(pos, axis, by)))
            c.start()
            sent.append(c)
        return sent

    swap_ends = misc(2, ends.at[1 - section], swapped, sibling)

    def prologue(wsend, esend, uw, uo, ue, us):
        unit = (uw, uo, ue)
        bc = win[:, 2 * DI : 2 * DI + 2 * N].astype(F32)
        rz = jnp.concatenate([win[:, 2 * DI + 2 * N :].astype(F32), jnp.zeros((24, 2 * N - H), F32)], axis=1)
        for j in range(3):
            for i, at in enumerate(group_columns(2 * j + 1 - parity)):
                wsend[j, :, 512 * i : 512 * i + 512] = win[:, at]
        esend[...] = jnp.where(even, rz, bc).astype(BF)
        us[...] = jnp.zeros((8, 128), F32)
        us[0:4, 0:52] = taps_in[...].astype(F32)
        us[4:5, 0:52] = bias_in[...].astype(F32)
        us[5:6, 0:24] = pre_in[...].astype(F32)
        us[6:7, 0:48] = gate_in[...].astype(F32)
        us[7:8, 0:48] = dtb_in[...].astype(F32)
        us[5:6, 64:112] = alog_in[...].astype(F32)
        us[6:7, 64:112] = skip_in[...].astype(F32)
        gs[section, pos[0], pos[1], pos[2]] = us[...]
        for j in range(3):
            uo[j] = wout[:, 512 * j : 512 * j + 512]

        pl.semaphore_wait(barrier, 10)
        swap_w = misc(0, wsend, wgot, device(partner))
        swap_e = misc(1, esend, egot, device(partner))
        for c in (swap_w, swap_e, swap_ends):
            c.start()

        small = small_gather(0)
        swap_w.wait()
        swap_e.wait()
        for j in range(3):
            for i, at in enumerate(group_columns(2 * j + parity)):
                lanes = slice(512 * i, 512 * i + 512)
                mine, theirs = win[:, at].astype(F32), wgot[j, :, lanes].astype(F32)
                uw[j, :, lanes] = jnp.concatenate([jnp.where(even, mine, theirs), jnp.where(even, theirs, mine)], axis=0).astype(BF)
        mine, theirs = jnp.where(even, bc, rz), egot[...].astype(F32)
        both = jnp.concatenate([jnp.where(even, mine, theirs), jnp.where(even, theirs, mine)], axis=0).astype(BF)
        for j in range(3):
            ue[j] = both[16 * j : 16 * j + 16, :]
        own = []
        for n, (j, kind) in enumerate(STREAMS):
            ag_start(n, 0, unit)
            c = pltpu.make_async_copy(unit[kind].at[j], gath[kind].at[section, j].at[pos], own_sem.at[n])
            c.start()
            own.append(c)
        for c in small:
            c.wait()
        small = small_gather(1)
        ag_forward(0)
        for c in own:
            c.wait()
        ag_rest(0)
        for n in range(9):
            ag_start(n, 1)
        for c in small:
            c.wait()
        small = small_gather(2)
        ag_forward(1)
        ag_rest(1)
        for c in small:
            c.wait()
        ag_sent(0)

    pl.run_scoped(
        prologue,
        pltpu.VMEM((3, 24, 1024), BF), pltpu.VMEM((24, 256), BF), pltpu.VMEM((3, 48, 1024), BF), pltpu.VMEM((3, 48, 512), BF), pltpu.VMEM((3, 16, 256), BF), pltpu.VMEM((8, 128), F32),
    )
    small_across = misc(3, gs.at[section], gs.at[section], sibling)
    small_across.start()

    @pl.when(leading)
    def _():
        for n in range(9):
            ag_start(n, 2)
    for n, (j, kind) in enumerate(STREAMS):
        to_sibling(n, block_index(ORDERS[j], 2, pos, None))
    ag_sent(1)

    misc(3, gs.at[1 - section], gs.at[1 - section], sibling).wait()
    for l in range(2):
        hp[l] = gs[l, 0, 0, 0]
        for i in range(64):
            tile = gs.at[l, i // 16, i // 4 % 4, i % 4]
            par[l, 0:5, 52 * i : 52 * i + 52] = tile[0:5, 0:52]
            par[l, 7:8, 24 * i : 24 * i + 24] = tile[5:6, 0:24]
            par[l, 5:6, 48 * i : 48 * i + 48] = tile[6:7, 0:48]
    swap_ends.wait()

    @pl.when(leading)
    def _():
        ag_forward(2)
        ag_rest(2)
        ag_sent(2)
        pl.semaphore_signal(go_sem, inc=1, device_id=sibling, device_id_type=MESH)

    @pl.when(jnp.logical_not(leading))
    def _():
        pl.semaphore_wait(go_sem, 1)
        for n in range(9):
            ag_start(n, 2)

    def from_sibling(l):
        for n, (j, kind) in enumerate(STREAMS):
            ref = gath[kind].at[l, j]
            remote(ref, ref, s_sib.at[n], r_sib.at[n], sibling).wait_recv()

    @pl.when(jnp.logical_not(leading))
    def _():
        from_sibling(0)

    def rs_copy(n, phase, slot, src, to):
        j, kind = STREAMS[n]
        dst = (recv0, recv1, recv2)[phase][kind].at[j, slot]
        return remote(src, dst, s_rs.at[n, phase], r_rs.at[n, phase, slot], device(to))

    def rs_start(n, phase, part):
        j, kind = STREAMS[n]
        axis = ORDERS[j][phase]
        right, left, far = (moved(pos, axis, by) for by in (1, 3, 2))
        for slot, at, h, to in ((0, far, 0, left), (1, far, 1, right), (2, left, 1, left), (3, right, 0, right)):
            if has_half(kind, phase, h):
                rs_copy(n, phase, slot, part(n, at[axis], h), to).start()

    def grad_part(n, k, h):
        j, kind = STREAMS[n]
        at = list(pos)
        at[ORDERS[j][2]] = k
        return grad[kind].at[(j,) + block_index(ORDERS[j], 2, tuple(at), h)]

    def term(n, src, dst):
        return remote(src, dst, s_terms.at[n], r_terms.at[n], sibling)

    def dterm(g):
        return term(3 + g, dps.at[12 + lax.rem(g, 2)], dps.at[6 + g])

    def layers(wbuf, ebuf, obuf, zbuf, xbuf, ybuf, tbuf, hbuf, pebuf, masks, allowed, tri, sel, qcol, qrow, dtrow, heads, smat, gbuf, dgacc, rowq, rowx, acc, rbuf, wstage, ostage, estage, wsem, esem, osem, wssem, ossem, essem):
        def copy_w(l, g):
            j, p = lax.div(g, 2), lax.rem(g, 2)
            return [pltpu.make_async_copy(gath[0].at[l, j, :, :, 2 * m + p], wbuf.at[g, :, :, pl.ds(48 * m, 48)], wsem.at[g, m]) for m in range(2)]

        def copy_e(l):
            return [pltpu.make_async_copy(gath[2].at[l, j, :, :, 2 * m + p], ebuf.at[p, :, :, m, j], esem.at[p, m, j]) for p in range(2) for m in range(2) for j in range(3)]

        def copy_o(l, j):
            return [pltpu.make_async_copy(gath[1].at[l, j], obuf.at[j], osem.at[j])]

        def start(copies):
            for c in copies:
                c.start()

        def finish(copies):
            for c in copies:
                c.wait()

        def weights_e(p):
            return ebuf[p].reshape(D, 256)

        start(copy_e(0))
        for g in range(GROUPS):
            start(copy_w(0, jnp.int32(g)))
        for j in range(3):
            start(copy_o(0, j))

        rows = lax.broadcasted_iota(jnp.int32, (T, T), 0)
        cols = lax.broadcasted_iota(jnp.int32, (T, T), 1)
        seg = jnp.where(leading, segs[0:1, :], segs[1:2, :]).astype(F32)
        seg_s = jnp.broadcast_to(seg, (T, T))
        seg_t = jnp.transpose(seg_s)
        allowed[...] = jnp.where(rows >= cols, jnp.where(seg_t == seg_s, 1.0, 0.0), 0.0)
        for d in (1, 2, 3):
            masks[d - 1] = jnp.where(rows >= d, jnp.where(pltpu.roll(seg_t, d, 0) == seg_t, 1.0, 0.0), 0.0)
        masks[3] = jnp.where(rows < counts[section], 1.0, 0.0)
        tri[...] = jnp.where(rows >= cols, 1.0, 0.0).astype(BF)
        srow = lax.broadcasted_iota(jnp.int32, (512, T), 0)
        scol = lax.broadcasted_iota(jnp.int32, (512, T), 1)
        sel[...] = jnp.where(lax.div(srow, 64) == scol, 1.0, 0.0).astype(BF)
        low_lanes = cols < 64
        for l in range(2):
            skips = hp[l, 6:7, 64:112]
            skips = jnp.concatenate([skips, jnp.zeros((1, 80), F32)], axis=1)
            skips = jnp.broadcast_to(skips, (8, T))
            for g in range(GROUPS):
                mine = skips if g == 0 else pltpu.roll(skips, T - 8 * g, 1)
                mine = jnp.where(cols[0:8] < 8, mine, 0.0)
                par[l, 6:7, 512 * g : 512 * g + 512] = dot(mine.astype(BF), sel[...], ((1,), (1,)))[0:1]

        def conv(px, taps, bias):
            s1 = pltpu.roll(px, 1, 0) * masks[0]
            s2 = pltpu.roll(px, 2, 0) * masks[1]
            s3 = pltpu.roll(px, 3, 0) * masks[2]
            c = bias + taps[3:4] * px + taps[2:3] * s1 + taps[1:2] * s2 + taps[0:1] * s3
            return c, (s3, s2, s1, px)

        def conv_back(dc, taps):
            out = taps[3:4] * dc
            out = out + taps[2:3] * pltpu.roll(dc * masks[0], T - 1, 0)
            out = out + taps[1:2] * pltpu.roll(dc * masks[1], T - 2, 0)
            return out + taps[0:1] * pltpu.roll(dc * masks[2], T - 3, 0)

        def decay(g, hh):
            gap = jnp.broadcast_to(qcol[g][:, hh : hh + 1], (T, T)) - qrow[g][hh : hh + 1, :]
            return jnp.exp2(jnp.minimum(gap, 0.0)) * dtrow[g][hh : hh + 1, :]

        def rate_bias(l):
            return hp[l, 7:8, :]

        def rate(l):
            tile = pltpu.roll(hp[l], 64, 1)
            return -jnp.exp(jnp.where(cols[0:1] < H, tile[5:6, :], 0.0))

        def tile_at(g, k):
            return pl.ds(pl.multiple_of(512 * g + 128 * k, 128), 128)

        def prepare(l):
            q = heads[l, 1]
            qt = jnp.transpose(q)
            dtt = jnp.transpose(heads[l, 0])
            for g in range(GROUPS):
                qcol[g] = q if g == 0 else pltpu.roll(q, T - 8 * g, 1)
                qrow[g] = qt[8 * g : 8 * g + 8, :]
                dtrow[g] = dtt[8 * g : 8 * g + 8, :]

        def slot(l):
            return lax.select(section == l, 0, 2)

        def first_input():
            return jnp.where(leading, ends[section].astype(F32), swapped[...].astype(F32))

        def forward(l, h):
            if l == 1:
                hbuf[...] = h.astype(BF)
            rs = lax.rsqrt(jnp.sum(h * h, axis=1, keepdims=True) * (1.0 / D) + EPSILON)
            rbuf[l, 0] = jnp.broadcast_to(rs, (T, T))
            us_[slot(l)] = (h * rs * par[l, 7:8, 0:D] * masks[3][:, 0:1]).astype(BF)
            finish(copy_e(l))
            pebuf[l, :, 0:256] = dot(us_[slot(l)], weights_e(0))
            pebuf[l, :, 256:384] = dot(us_[slot(l)], weights_e(1))[:, 0:128]
            for j in range(2):
                at = slice(DI + 128 * j, DI + 128 * j + 128)
                c, _ = conv(pebuf[l, :, 128 * j : 128 * j + 128], par[l, 0:4, at], par[l, 4:5, at])
                smat[l, j] = (c * sigmoid(c)).astype(BF)
            v = pebuf[l, :, 256:384] + rate_bias(l)
            dt = jnp.maximum(v, 0.0) + jnp.log1p(jnp.exp(-jnp.abs(v)))
            heads[l, 0] = dt
            heads[l, 1] = exact_dot(tri[...], dt * rate(l)) * LOG2E
            gbuf[l] = dot(smat[l, 1], smat[l, 0], ((1,), (1,))) * allowed[...]
            prepare(l)
            acc[:, 0:128] = jnp.zeros((T, T), F32)

            def group(g, carry):
                finish(copy_w(l, g))
                p = dot(us_[slot(l)], wbuf[g].reshape(D, 1024))
                wide = pl.ds(pl.multiple_of(512 * g, 128), 512)
                zbuf[l, :, wide] = p[:, 0:512]
                xbuf[l, :, wide] = p[:, 512:1024]
                for k in range(4):
                    at = tile_at(g, k)
                    c, _ = conv(xbuf[l, :, at], par[l, 0:4, at], par[l, 4:5, at])
                    x = c * sigmoid(c)
                    xb = x.astype(BF)
                    both = jnp.concatenate([keep_lanes(xb, low_lanes), keep_lanes(xb, ~low_lanes)], axis=0)
                    w = jnp.concatenate([(gbuf[l] * decay(g, 2 * k + i)).astype(BF) for i in range(2)], axis=1)
                    y = dot(w, both) + par[l, 6:7, at] * x
                    ybuf[l, :, at] = y
                    z = zbuf[l, :, at]
                    e = y * (z * sigmoid(z))
                    tbuf[:, at] = e
                    acc[:, 0:128] += e * e
                return carry

            lax.fori_loop(0, GROUPS, group, 0)
            r = lax.rsqrt(jnp.sum(acc[:, 0:128], axis=1, keepdims=True) * (1.0 / DI) + EPSILON)
            rbuf[l, 1] = jnp.broadcast_to(r, (T, T))
            for g in range(GROUPS):
                at = slice(512 * g, 512 * g + 512)
                os_[slot(l), :, at] = (tbuf[:, at] * r * par[l, 5:6, at]).astype(BF)
            for j in range(3):
                finish(copy_o(l, j))
                acc[:, 512 * j : 512 * j + 512] = dot(os_[slot(l)], obuf[j].reshape(DI, 512))
            return h + acc[...]

        def backward(l, dh):
            dvs[slot(l)] = dh.astype(BF)

            @pl.when(section != l)
            def _():
                for n, ref in enumerate((us_, os_, dvs)):
                    term(n, ref.at[2], ref.at[1]).start()

            if l == 0:
                for j in range(3):
                    finish(copy_o(0, j))
            acc[:, 0:128] = jnp.zeros((T, T), F32)

            def first(zz, carry):
                wide = pl.ds(pl.multiple_of(768 * zz, 128), 768)
                do = None
                for j in range(3):
                    part = dot(dvs[slot(l), :, 512 * j : 512 * j + 512], obuf[j, zz].reshape(768, 512), ((1,), (1,)))
                    do = part if do is None else do + part
                tbuf[:, wide] = do
                for k in range(6):
                    at = pl.ds(pl.multiple_of(768 * zz + 128 * k, 128), 128)
                    z = zbuf[l, :, at]
                    e = ybuf[l, :, at] * (z * sigmoid(z))
                    prod = tbuf[:, at] * e
                    gr[l, 5:6, at] = total(prod * rbuf[l, 1])
                    acc[:, 0:128] += prod * par[l, 5:6, at]
                return carry

            lax.fori_loop(0, 4, first, 0)
            if l == 1:
                for j in range(3):
                    start(copy_o(0, j))
            r = rbuf[l, 1]
            masks[4] = jnp.broadcast_to(jnp.sum(acc[:, 0:128], axis=1, keepdims=True) * (1.0 / DI), (T, T)) * r * r * r
            prepare(l)
            dgacc[...] = jnp.zeros((T, T), F32)
            rowq[...] = jnp.zeros((T, T), F32)
            rowx[...] = jnp.zeros((T, T), F32)
            acc[...] = jnp.zeros((T, D), F32)

            def second(g, carry):
                if l == 0:
                    finish(copy_w(0, g))

                here = lax.select(section == l, g, 12 + lax.rem(g, 2))

                @pl.when(jnp.logical_and(section != l, g >= 2))
                def _():
                    dterm(g - 2).wait_send()

                sums_q, sums_x = None, None
                for k in range(4):
                    at = tile_at(g, k)
                    z = zbuf[l, :, at]
                    y = ybuf[l, :, at]
                    sz = sigmoid(z)
                    silu = z * sz
                    de = rbuf[l, 1] * (tbuf[:, at] * par[l, 5:6, at]) - (y * silu) * masks[4]
                    dyb = (de * silu).astype(BF)
                    dz = de * y * (sz + silu * (1.0 - sz))
                    dps[here, :, 128 * k : 128 * k + 128] = dz.astype(BF)
                    taps = par[l, 0:4, at]
                    c, shifts = conv(xbuf[l, :, at], taps, par[l, 4:5, at])
                    sc = sigmoid(c)
                    x = c * sc
                    xb = x.astype(BF)
                    dyw = dyb.astype(F32)
                    skip = par[l, 6:7, at]
                    xt = jnp.concatenate([keep_lanes(xb, low_lanes), keep_lanes(xb, ~low_lanes)], axis=0)
                    dyt = jnp.concatenate([keep_lanes(dyb, low_lanes), keep_lanes(dyb, ~low_lanes)], axis=0)
                    dw = dot(dyb, xt, ((1,), (1,)))
                    ws, dg = [], None
                    for i in range(2):
                        e = decay(g, 2 * k + i)
                        ws.append((gbuf[l] * e).astype(BF))
                        part = dw[:, 128 * i : 128 * i + 128] * e
                        dg = part if dg is None else dg + part
                    dgacc[...] += dg
                    dx0 = dot(jnp.concatenate(ws, axis=0), dyt, ((0,), (0,)))
                    dx = dx0 + skip * dyw
                    gr[l, 6:7, at] = total(dyw * x)
                    one = sel[128 * k : 128 * k + 128, :]
                    part = exact_dot(one, dyw * (y - skip * x), flip=True, terms=2)
                    sums_q = part if sums_q is None else sums_q + part
                    part = exact_dot(one, xb.astype(F32) * dx0, flip=True, terms=2)
                    sums_x = part if sums_x is None else sums_x + part
                    dc = dx * (sc + x * (1.0 - sc))
                    for t in range(4):
                        gr[l, t : t + 1, at] = total(dc * shifts[t])
                    gr[l, 4:5, at] = total(dc)
                    dps[here, :, 512 + 128 * k : 640 + 128 * k] = conv_back(dc, taps).astype(BF)
                rowq[...] += pltpu.roll(sums_q, 8 * g, 1)
                rowx[...] += pltpu.roll(sums_x, 8 * g, 1)

                @pl.when(section != l)
                def _():
                    dterm(g).start()

                acc[...] += dot(dps[here], wbuf[g].reshape(D, 1024), ((1,), (1,)))
                if l == 1:
                    start(copy_w(0, g))
                return carry

            lax.fori_loop(0, GROUPS, second, 0)
            dg = (dgacc[...] * allowed[...]).astype(BF)
            d_states = (dot(dg, smat[l, 1], ((0,), (0,))), dot(dg, smat[l, 0]))
            for j in range(2):
                at = slice(DI + 128 * j, DI + 128 * j + 128)
                taps = par[l, 0:4, at]
                c, shifts = conv(pebuf[l, :, 128 * j : 128 * j + 128], taps, par[l, 4:5, at])
                sc = sigmoid(c)
                dc = d_states[j] * (sc + c * sc * (1.0 - sc))
                for t in range(4):
                    gr[l, t : t + 1, at] = total(dc * shifts[t])
                gr[l, 4:5, at] = total(dc)
                dpes[slot(l), 0, :, 128 * j : 128 * j + 128] = conv_back(dc, taps).astype(BF)
            v = pebuf[l, :, 256:384] + rate_bias(l)
            sv = sigmoid(v)
            dt = heads[l, 0]
            back = exact_dot(tri[...], rowq[...] - rowx[...], ((0,), (0,)))
            ratio = jnp.where(v < -15.0, 1.0, sv / jnp.maximum(dt, 1e-30))
            dr = jnp.where(cols < H, rowx[...] * ratio + back * rate(l) * sv, 0.0)
            d_rate = total(jnp.where(cols < H, back * dt, 0.0)) * rate(l)
            dpes[slot(l), 1, :, 0:128] = dr.astype(BF)
            dpes[slot(l), 1, :, 128:256] = jnp.zeros((T, T), BF)

            @pl.when(section != l)
            def _():
                term(9, dpes.at[2], dpes.at[1]).start()

            if l == 0:
                finish(copy_e(0))
            du = acc[...]
            for p in range(2):
                du = du + dot(dpes[slot(l), p], weights_e(p), ((1,), (1,)))
            if l == 1:
                start(copy_e(0))
            h = hbuf[...].astype(F32) if l == 1 else first_input()
            hn = h * rbuf[l, 0][:, 0:1]
            du = du * masks[3][:, 0:1]
            gr[l, 7:8, 0:D] = total(du * hn)
            t = du * par[l, 7:8, 0:D]
            s = jnp.sum(t * hn, axis=1, keepdims=True) * (1.0 / D)
            dh_in = dh + rbuf[l, 0][:, 0:1] * (t - hn * s)
            skips = jnp.zeros((8, T), F32)
            for g in range(GROUPS):
                mine = exact_dot(sel[...], jnp.broadcast_to(gr[l, 6:7, 512 * g : 512 * g + 512], (8, 512)), flip=True)
                skips = skips + (mine if g == 0 else pltpu.roll(mine, 8 * g, 1))
            for i in range(64):
                tile = gs.at[l, i // 16, i // 4 % 4, i % 4]
                tile[0:5, 0:52] = gr[l, 0:5, 52 * i : 52 * i + 52]
                tile[5:6, 0:24] = gr[l, 7:8, 24 * i : 24 * i + 24]
                tile[6:7, 0:48] = gr[l, 5:6, 48 * i : 48 * i + 48]
                tile[7:8, 0:128] = total(dr)
                tile[5:6, 64:112] = d_rate[:, 0:48]
                tile[6:7, 64:112] = skips[0:1, 0:48]

            @pl.when(section != l)
            def _():
                term(10, gs.at[l], tgot).start()

            return dh_in

        def products(l):
            for n, ref in enumerate((us_, os_, dvs)):
                term(n, ref.at[2], ref.at[1]).wait_recv()
            for g in range(GROUPS):
                dterm(g).wait_recv()
            term(9, dpes.at[2], dpes.at[1]).wait_recv()

            def stacked(ref, *index):
                return jnp.concatenate([ref[(0,) + index], ref[(1,) + index]], axis=0)

            for p in range(2):
                de = dot(stacked(us_), stacked(dpes, p), ((0,), (0,))).astype(BF).reshape(4, 4, 2, 3, 16, 256)
                for j in range(3):
                    for m in range(2):
                        estage[j, m] = de[:, :, m, j]
                ecopies = [pltpu.make_async_copy(estage.at[j, m], grad[2].at[j, :, :, 2 * m + p], essem.at[j, m]) for j in range(3) for m in range(2)]
                start(ecopies)
                finish(ecopies)
            def w_at(i):
                return lax.div(i, 8), lax.rem(lax.div(i, 2), 4), lax.rem(i, 2), pl.multiple_of(512 * lax.rem(i, 2), 128)

            for j in range(3):
                def wcopy(i):
                    g, zz, b, wide = w_at(i)
                    return [pltpu.make_async_copy(wstage.at[b, :, pl.ds(48 * m, 48)], grad[0].at[j, zz, :, 2 * m + g, :, pl.ds(wide, 512)], wssem.at[b, m]) for m in range(2)]

                def wstep(i, carry):
                    @pl.when(i >= 2)
                    def _():
                        finish(wcopy(i - 2))
                    g, zz, b, wide = w_at(i)
                    u = stacked(us_, slice(None), pl.ds(pl.multiple_of(384 * zz, 128), 384))
                    at = pl.ds(wide, 512)
                    d = jnp.concatenate([dps[2 * j + g, :, at], dps[6 + 2 * j + g, :, at]], axis=0)
                    wstage[b] = dot(u, d, ((0,), (0,))).astype(BF).reshape(4, 96, 512)
                    start(wcopy(i))
                    return carry

                lax.fori_loop(0, 16, wstep, 0)
                for i in (14, 15):
                    finish(wcopy(jnp.int32(i)))
                rs_start(3 * j, 2, grad_part)

                def ocopy(i):
                    b = lax.rem(i, 2)
                    return [pltpu.make_async_copy(ostage.at[b], grad[1].at[j, lax.div(i, 4), pl.ds(2 * lax.rem(lax.div(i, 2), 2), 2), :, :, pl.ds(pl.multiple_of(256 * b, 128), 256)], ossem.at[b])]

                def ostep(i, carry):
                    @pl.when(i >= 2)
                    def _():
                        finish(ocopy(i - 2))
                    o = stacked(os_, slice(None), pl.ds(pl.multiple_of(384 * lax.div(i, 2), 128), 384))
                    b = lax.rem(i, 2)
                    ostage[b] = dot(o, stacked(dvs, slice(None), pl.ds(pl.multiple_of(512 * j + 256 * b, 128), 256)), ((0,), (0,))).astype(BF).reshape(2, 4, 48, 256)
                    start(ocopy(i))
                    return carry

                lax.fori_loop(0, 16, ostep, 0)
                for i in (14, 15):
                    finish(ocopy(jnp.int32(i)))
                rs_start(3 * j + 1, 2, grad_part)
                rs_start(3 * j + 2, 2, grad_part)

        middle = forward(0, first_input()).astype(BF).astype(F32)

        @pl.when(jnp.logical_not(leading))
        def _():
            ag_forward(2)
            ag_rest(2)

        @pl.when(leading)
        def _():
            from_sibling(1)

        start(copy_e(1))
        for g in range(GROUPS):
            start(copy_w(1, jnp.int32(g)))
        for j in range(3):
            start(copy_o(1, j))
        out = forward(1, middle).astype(BF)

        @pl.when(leading)
        def _():
            leaving[...] = out

        @pl.when(jnp.logical_not(leading))
        def _():
            ends_out[section] = out

        cotangent = jnp.where(leading, swapped[...].astype(F32), ends[section].astype(F32))
        d_middle = backward(1, cotangent).astype(BF).astype(F32)

        @pl.when(jnp.logical_not(leading))
        def _():
            products(1)

        d_first = backward(0, d_middle).astype(BF)

        @pl.when(leading)
        def _():
            ends_out[section] = d_first
            products(0)

        @pl.when(jnp.logical_not(leading))
        def _():
            leaving[...] = d_first

    V = pltpu.VMEM
    pl.run_scoped(
        layers,
        V((6, 4, 4, 96, 1024), BF), V((2, 4, 4, 2, 3, 16, 256), BF), V((3, 4, 4, 4, 48, 512), BF),
        V((2, T, DI), F32), V((2, T, DI), F32), V((2, T, DI), F32), V((T, DI), F32), V((T, D), BF), V((2, T, 384), F32),
        V((5, T, T), F32), V((T, T), F32), V((T, T), BF), V((512, T), BF), V((6, T, T), F32), V((6, 8, T), F32), V((6, 8, T), F32),
        V((2, 2, T, T), F32), V((2, 2, T, T), BF), V((2, T, T), F32), V((T, T), F32), V((T, T), F32), V((T, T), F32), V((T, D), F32), V((2, 2, T, T), F32),
        V((2, 4, 96, 512), BF), V((2, 2, 4, 48, 256), BF), V((3, 2, 4, 4, 16, 256), BF),
        pltpu.SemaphoreType.DMA((6, 2)), pltpu.SemaphoreType.DMA((2, 2, 3)), pltpu.SemaphoreType.DMA((3,)), pltpu.SemaphoreType.DMA((2, 2)), pltpu.SemaphoreType.DMA((2,)), pltpu.SemaphoreType.DMA((3, 2)),
    )

    end = misc(4, leaving, ends_out.at[section], sibling)
    end.start()

    def sums(*bufs):
        it = iter(bufs)
        take = lambda n: [next(it) for _ in range(n)]
        ab, ob, db, eb, acc2, acc1, b1, b0, fin = (take(3) for _ in range(9))
        fsend, gsend, sa2, sa1, lsem = it

        def load(n, h, which, src, dst):
            return pltpu.make_async_copy(src, dst, lsem.at[n, h, which])

        def add(dst, parts, dims, dtype, place=None):
            if not dims:
                out = parts[0][...].astype(F32)
                for p in parts[1:]:
                    out = out + p[...].astype(F32)
                dst[...] = out.astype(dtype)
                return
            count = dims[0] * (dims[1] if len(dims) > 1 else 1)

            def one(i, carry):
                index = (i,) if len(dims) == 1 else (lax.div(i, dims[1]), lax.rem(i, dims[1]))
                out = parts[0][index].astype(F32)
                for p in parts[1:]:
                    out = out + p[index].astype(F32)
                dst[index if place is None else place(*index)] = out.astype(dtype)
                return carry

            lax.fori_loop(0, count, one, 0)

        def neighbours(n, phase):
            axis = ORDERS[STREAMS[n][0]][phase]
            right, left = moved(pos, axis, 1), moved(pos, axis, 3)
            return pos[axis], {0: (0, left[axis], left, 4, 3), 1: (1, right[axis], right, 5, 2)}

        def sent(phase):
            for n, (j, kind) in enumerate(STREAMS):
                ref = (recv0, recv1, recv2)[phase][kind].at[j, pl.ds(0, 3 if phase == 0 else 6)]
                remote(ref, ref, s_rs.at[n, phase], r_rs.at[n, phase, 0], sibling).wait_send()

        items = {phase: [(n, h) for n, (j, kind) in enumerate(STREAMS) for h in (0, 1) if has_half(kind, phase, h)] for phase in range(3)}

        def small_start(phase):
            axis = ORDERS[0][phase]
            cur = (sa1, sa2, gs.at[section])[phase]
            got = (sg0, sg1, sg2)[phase]
            copies = []
            for by in (1, 2, 3):
                to = moved(pos, axis, by)
                c = remote(cur.at[to[axis]], got.at[by - 1], s_small.at[3 + phase, by - 1], r_small.at[3 + phase, by - 1], device(to))
                c.start()
                copies.append(c)

            def done():
                for c in copies:
                    c.wait()
                out = cur[pos[axis]] + got[0] + got[1] + got[2]
                if phase == 0:
                    return out
                (sa1, sa2)[phase - 1][...] = out
                return None

            return done

        term(10, tgot, tgot).wait_recv()
        gs[section] += tgot[...]
        done = small_start(2)
        for n, h in items[2]:
            j, kind = STREAMS[n]
            _, halves = neighbours(n, 2)
            load(n, h, 0, grad_part(n, halves[h][1], h), ob[kind].at[j, h]).start()
        for n, h in items[2]:
            j, kind = STREAMS[n]
            slot = neighbours(n, 2)[1][h][0]
            rs_copy(n, 2, slot, ab[kind].at[j, h], moved(pos, 0, 1)).wait_recv()
            load(n, h, 1, recv2[kind].at[j, slot], ab[kind].at[j, h]).start()
        for n, h in items[2]:
            j, kind = STREAMS[n]
            here, halves = neighbours(n, 2)
            _, block, to, slot, _ = halves[h]
            load(n, h, 0, grad_part(n, block, h), ob[kind].at[j, h]).wait()
            load(n, h, 1, recv2[kind].at[j, 0], ab[kind].at[j, h]).wait()
            add(ab[kind].at[j, h], [ab[kind].at[j, h], ob[kind].at[j, h]], (2, 4), BF)
            rs_copy(n, 2, slot, ab[kind].at[j, h], to).start()
            load(n, h, 0, grad_part(n, here, h), ob[kind].at[j, h]).start()
        done()
        for n, h in items[2]:
            j, kind = STREAMS[n]
            slot = neighbours(n, 2)[1][h][4]
            rs_copy(n, 2, slot, ab[kind].at[j, h], moved(pos, 0, 1)).wait_recv()
            load(n, h, 2, recv2[kind].at[j, slot], db[kind].at[j, h]).start()

        def last2(n, h):
            j, kind = STREAMS[n]
            order = ORDERS[j]
            low = min(order[:2])
            load(n, h, 0, grad_part(n, 0, h), ob[kind].at[j, h]).wait()
            load(n, h, 2, recv2[kind].at[j, 0], db[kind].at[j, h]).wait()
            load(n, h, 3, recv2[kind].at[j, 0], eb[kind].at[j, h]).wait()
            place = (lambda a, b: (j, 2 * h + a, b)) if order[1] == low else (lambda a, b: (j, b, 2 * h + a))
            add(acc2[kind], [ob[kind].at[j, h], db[kind].at[j, h], eb[kind].at[j, h]], (2, 4), BF, place)

        before = None
        for n, h in items[2]:
            j, kind = STREAMS[n]
            slot = neighbours(n, 2)[1][h][3]
            rs_copy(n, 2, slot, ab[kind].at[j, h], moved(pos, 0, 1)).wait_recv()
            load(n, h, 3, recv2[kind].at[j, slot], eb[kind].at[j, h]).start()
            if before is not None:
                last2(*before)
            before = (n, h)
        last2(*before)

        for phase in (1, 0):
            recv, buf = (recv0, recv1)[phase], (b0, b1)[phase]

            def part(n, k, h):
                j, kind = STREAMS[n]
                return acc2[kind].at[j, k, pl.ds(2 * h, 2)] if phase == 1 else acc1[kind].at[j, k]

            dims = (2,) if phase == 1 else ()

            def fetch(n, h, slot, which):
                j, kind = STREAMS[n]
                rs_copy(n, phase, slot, buf[kind].at[j, slot], moved(pos, 0, 1)).wait_recv()
                load(n, h, which, recv[kind].at[j, slot], buf[kind].at[j, slot]).start()

            def fetched(n, h, slot, which):
                j, kind = STREAMS[n]
                load(n, h, which, recv[kind].at[j, slot], buf[kind].at[j, slot]).wait()
                return buf[kind].at[j, slot]

            done = small_start(phase)
            for n in range(9):
                rs_start(n, phase, part)
            for n, h in items[phase]:
                fetch(n, h, neighbours(n, phase)[1][h][0], 1)
            for n, h in items[phase]:
                slot, block, to, summed, _ = neighbours(n, phase)[1][h]
                ref = fetched(n, h, slot, 1)
                add(ref, [ref, part(n, block, h)], dims, BF)
                rs_copy(n, phase, summed, ref, to).start()
            last_tile = done()
            for n, h in items[phase]:
                fetch(n, h, neighbours(n, phase)[1][h][4], 2)

            def last(n, h):
                j, kind = STREAMS[n]
                here, halves = neighbours(n, phase)
                parts = [part(n, here, h), fetched(n, h, halves[h][4], 2), fetched(n, h, halves[h][3], 3)]
                if phase == 1:
                    add(acc1[kind], parts, dims, BF, lambda a: (j, 2 * h + a))
                else:
                    add(fin[kind].at[j], parts, dims, F32)

            before = None
            for n, h in items[phase]:
                fetch(n, h, neighbours(n, phase)[1][h][3], 3)
                if before is not None:
                    last(*before)
                before = (n, h)
            last(*before)

        for j in range(3):
            fsend[j] = jnp.where(even, fin[0][j, 24:48, :], fin[0][j, 0:24, :])
        last_e = jnp.concatenate([fin[2][j] for j in range(3)], axis=0)
        gsend[...] = jnp.where(even, last_e[24:48], last_e[0:24])
        swap_f = misc(5, fsend, fgot, device(partner))
        swap_g = misc(6, gsend, ggot, device(partner))
        swap_f.start()
        swap_g.start()
        for j in range(3):
            for i, at in enumerate(group_columns(2 * j + parity)):
                lanes = slice(512 * i, 512 * i + 512)
                d_win[:, at] = jnp.where(even, fin[0][j, 0:24, lanes], fin[0][j, 24:48, lanes])
            d_wout[:, 512 * j : 512 * j + 512] = fin[1][j]
        d_taps[...] = last_tile[0:4, 0:52]
        d_bias[...] = last_tile[4:5, 0:52]
        d_pre[...] = last_tile[5:6, 0:24]
        d_gate[...] = last_tile[6:7, 0:48]
        d_dtb[...] = last_tile[7:8, 0:48]
        d_alog[...] = last_tile[5:6, 64:112]
        d_skip[...] = last_tile[6:7, 64:112]
        swap_f.wait()
        swap_g.wait()
        for j in range(3):
            for i, at in enumerate(group_columns(2 * j + 1 - parity)):
                d_win[:, at] = fgot[j, :, 512 * i : 512 * i + 512]
        mine, theirs = jnp.where(even, last_e[0:24], last_e[24:48]), ggot[...]
        d_win[:, 2 * DI : 2 * DI + 2 * N] = jnp.where(even, mine, theirs)
        d_win[:, 2 * DI + 2 * N :] = jnp.where(even, theirs, mine)[:, 0:H]
        for phase in range(3):
            sent(phase)

    shapes = []
    for lead, dtype in (((3, 2, 2, 4), BF),) * 4 + (((3, 4, 4), BF), ((3, 4), BF), ((3, 6, 2), BF), ((3, 6), BF), ((3,), F32)):
        shapes += [V(lead + dims, dtype) for dims in KINDS]
    shapes += [V((3, 24, 1024), F32), V((24, 256), F32), V((4, 4, 8, 128), F32), V((4, 8, 128), F32)]
    pl.run_scoped(sums, *shapes, pltpu.SemaphoreType.DMA((9, 2, 4)))

    end.wait()
    for n, (j, kind) in enumerate(STREAMS):
        ref = gath[kind].at[section, j]
        remote(ref, ref, s_sib.at[n], r_sib.at[n], sibling).wait_send()

    @pl.when(jnp.logical_not(leading))
    def _():
        ag_sent(2)

    for n, ref in enumerate((us_, os_, dvs)):
        term(n, ref.at[2], ref.at[1]).wait_send()
    for g in (4, 5):
        dterm(g).wait_send()
    term(9, dpes.at[2], dpes.at[1]).wait_send()
    term(10, tgot, tgot).wait_send()


def step(ends, segs, counts, win, taps, bias, pre, gate, wout, dtb, alog, skip):
    vm = pl.BlockSpec(memory_space=pltpu.VMEM)
    any_ = pl.BlockSpec(memory_space=pl.ANY)
    s = jax.ShapeDtypeStruct
    V, S = pltpu.VMEM, pltpu.SemaphoreType.DMA
    large = []
    for lead in ((2, 3, 4, 4, 4), (3, 4, 4, 4), (3, 6, 2, 4), (3, 6, 2), (3, 6)):
        large += [s(lead + dims, BF) for dims in KINDS]
    return pl.pallas_call(
        step_kernel,
        out_shape=[
            s((2, T, D), BF), s((24, 6448), F32), s((4, 52), F32), s((1, 52), F32), s((1, 24), F32), s((1, 48), F32), s((48, D), F32),
            s((1, H), F32), s((1, H), F32), s((1, H), F32),
        ] + large,
        in_specs=[vm, vm, pl.BlockSpec(memory_space=pltpu.SMEM)] + [vm] * 9,
        out_specs=[vm] * 10 + [any_] * 15,
        scratch_shapes=[
            V((3, 24, 1024), BF), V((24, 256), BF), V((3, 24, 1024), F32), V((24, 256), F32), V((2, 4, 4, 4, 8, 128), F32),
            V((2, 8, CC), F32), V((2, 8, 128), F32), V((2, 8, CC), F32), V((4, 4, 4, 8, 128), F32),
            V((3, 4, 4, 8, 128), F32), V((3, 4, 8, 128), F32), V((3, 8, 128), F32),
            V((T, D), BF), V((T, D), BF), V((3, T, D), BF), V((3, T, DI), BF), V((3, T, D), BF), V((14, T, 1024), BF), V((3, 2, T, 256), BF),
            S((7,)), S((7,)), S((9, 3)), S((9, 3, 8)), S((6, 3)), S((6, 3)), S((9,)), S((9,)), S((9, 3)), S((9, 3, 6)), S((11,)), S((11,)), S((9,)),
            pltpu.SemaphoreType.REGULAR,
        ],
        compiler_params=pltpu.CompilerParams(collective_id=0, has_side_effects=True, vmem_limit_bytes=63 * 1024 * 1024),
        name="train_step",
    )(ends, segs, counts, win, taps, bias, pre, gate, wout, dtb, alog, skip)[:10]


def body(ends_in, seg_ids, block_counts, in_weight, conv_weight, conv_bias, pre_gain, gate_gain, out_weight, dt_bias, a_log, skip):
    outs = step(
        ends_in[0].reshape(2, T, D), seg_ids, block_counts, in_weight[0], conv_weight[0], conv_bias, pre_gain, gate_gain, out_weight[0], dt_bias, a_log, skip
    )
    ends_out, d_in, d_taps, d_bias, d_pre, d_gate, d_out, d_dtb, d_alog, d_skip = outs
    return ends_out.reshape(1, 2 * T, D), d_in[None], d_taps[None], d_bias, d_pre, d_gate, d_out[None], d_dtb, d_alog, d_skip


def solution(mesh):
    placed = (
        P("section", "dp", None),
        P("dp", None),
        P("dp"),
        P("section", "dp", None),
        P("section", None, "dp"),
        P("section", "dp"),
        P("section", "dp"),
        P("section", "dp"),
        P("section", "dp", None),
        P("section", None),
        P("section", None),
        P("section", None),
    )
    return jax.shard_map(
        body,
        mesh=mesh,
        in_specs=placed,
        out_specs=(
            P("section", "dp", None),
            P("section", "dp", None),
            P("section", None, "dp"),
            P("section", "dp"),
            P("section", "dp"),
            P("section", "dp"),
            P("section", "dp", None),
            P("section", None),
            P("section", None),
            P("section", None),
        ),
        check_vma=False,
    )
```

time: 1610 us -> 432 us (0.27)
  waiting for transfers between devices: 554 us -> 0 us
  blocking collectives: 531 us -> 0 us
  Pallas kernels: 0 us -> 416 us
  matrix products: 251 us -> 0 us
  other arithmetic: 123 us -> 0 us
  local copies, waits for them, and re-layouts: 115 us -> 13.8 us
  between operations: 20.1 us -> 0.66 us
    pallas_call x0 -> x1, Pallas kernels: none -> 416 us  [step(): pl.pallas_call(step_kernel, out_shape=[s((2, T, D), BF), s((24, 6448), F3...]
    unnamed x1 -> x0, blocking collectives: 352 us -> none
    unnamed x7 -> x0, waiting for transfers between devices: 317 us -> none
    dot_general x42 -> x0, matrix products: 251 us -> none  [the longest x5 63.4 us: layer_parts(): projected = jnp.dot(input_low, proj_in, preferred_element_type=jnp.float32)]
    reduce_scatter x1 -> x0, waiting for transfers between devices: 237 us -> none  [body(): lax.psum_scatter(totals[1], 'dp', scatter_dimension=0, tiled=True)]
    all_gather x1 -> x0, blocking collectives: 179 us -> none  [body(): lax.all_gather(shards[2], 'dp', axis=1, tiled=True)]
    slice x11 -> x0, local copies, waits for them, and re-layouts: 76.6 us -> none  [the longest x1 69.1 us: mix_piece(): kernel_taps[offset][None, :] * padded[offset:offset + length]]
    reduce_sum x20 -> x0, other arithmetic: 52.5 us -> none  [the longest x3 21.2 us: mix_piece(): kernel_taps[offset][None, :] * padded[offset:offset + length]]
  transfers between devices with their start and end apart: 9 -> 0, of which waited for: 3 -> 0; matrix products, arithmetic and copies ran while one was open for 16% -> 0% of each run, Pallas kernels for 0% -> 0%
where the time goes in v2:
time: 432 us; the launch traced here: 431 us
  Pallas kernels  416 us (96%)
  local copies, waits for them, and re-layouts  13.8 us (3%)
    pallas_call x1, Pallas kernels, step(): pl.pallas_call(step_kernel, out_shape=[s((2, T, D), BF), s((24, 6448), F3...  416 us
    unnamed x10, local copies, waits for them, and re-layouts  13.8 us

profile of v2, /device:TPU:0, one launch (start us, length us, event | category | flops | bytes accessed | tf_op | source)
XLA Modules:
  0.0 430.8 jit_solution(11253350981649081971)
XLA Ops:
  0.6 416.4 %train_step.1 = (bf16[2,128,1536]{2,1,0:T(8,128)(2,1)}, f32[24,6448]{1,0:T(8,128)}, f32[4,52]{1,0:T(4,128)}, f32[1,52]{1,0:T(1,128)}, f32[1,24]{1,0:T(1,128)}, /...) custom-call(bf16[2,128,1536]{2,1,0:T(8,128)(2,1)} %bitcast.9, ...), custom_call_target="tpu_custom_call" | custom-call | tf_op jit(solution)/shard_map/train_step/pallas_call | solution.py:969
  417.1 2.1 copy.32
  419.1 1.9 copy.33
  421.1 1.2 copy.34
  422.3 1.2 copy.35
  423.5 1.1 copy.36
  424.6 1.1 copy.37
  425.8 1.7 copy.38
  427.4 1.1 copy.39
  428.5 1.2 copy.40
  429.7 1.1 copy.41

commit v3 on v2

--- a/solution.py
+++ b/solution.py
@@ -71,10 +71,10 @@
     it = iter(refs)
     take = lambda n: [next(it) for _ in range(n)]
     ends, segs, counts, win, taps_in, bias_in, pre_in, gate_in, wout, dtb_in, alog_in, skip_in = take(12)
-    ends_out, d_win, d_taps, d_bias, d_pre, d_gate, d_wout, d_dtb, d_alog, d_skip = take(10)
-    gath, grad, recv2, recv1, recv0 = take(3), take(3), take(3), take(3), take(3)
-    wgot, egot, fgot, ggot, gs, par, hp, gr, tgot, sg2, sg1, sg0, swapped, leaving, us_, os_, dvs, dps, dpes = take(19)
-    (s_misc, r_misc, s_ag, r_ag, s_small, r_small, s_sib, r_sib, s_rs, r_rs, s_terms, r_terms, own_sem, go_sem) = take(14)
+    ends_out, d_win, d_wout, d_small = take(4)
+    gath, grad, recv2 = take(3), take(3), take(3)
+    wgot, egot, gs, par, hp, gr, tgot, sg2, sg1, sg0, swapped, leaving, us_, os_, dvs, dps, dpes = take(17)
+    (s_misc, r_misc, s_ag, r_ag, s_small, r_small, s_sib, r_sib, s_rs, r_rs, s_terms, r_terms, own_sem, go_sem, ready_sem) = take(15)
 
     section = lax.axis_index("section")
     dp = lax.axis_index("dp")
@@ -177,6 +177,7 @@
         return sent
 
     swap_ends = misc(2, ends.at[1 - section], swapped, sibling)
+    small_across = misc(3, gs.at[section], gs.at[section], sibling)
 
     def prologue(wsend, esend, uw, uo, ue, us):
         unit = (uw, uo, ue)
@@ -226,34 +227,33 @@
             c.wait()
         small = small_gather(1)
         ag_forward(0)
+        for c in small:
+            c.wait()
+        small = small_gather(2)
         for c in own:
             c.wait()
         ag_rest(0)
-        for n in range(9):
-            ag_start(n, 1)
         for c in small:
             c.wait()
-        small = small_gather(2)
-        ag_forward(1)
-        ag_rest(1)
-        for c in small:
-            c.wait()
+        small_across.start()
         ag_sent(0)
 
     pl.run_scoped(
         prologue,
         pltpu.VMEM((3, 24, 1024), BF), pltpu.VMEM((24, 256), BF), pltpu.VMEM((3, 48, 1024), BF), pltpu.VMEM((3, 48, 512), BF), pltpu.VMEM((3, 16, 256), BF), pltpu.VMEM((8, 128), F32),
     )
-    small_across = misc(3, gs.at[section], gs.at[section], sibling)
-    small_across.start()
+
+    def own_across():
+        for n, (j, kind) in enumerate(STREAMS):
+            to_sibling(n, block_index(ORDERS[j], 2, pos, None))
+
+    def go(n):
+        pl.semaphore_signal(go_sem.at[n], inc=1, device_id=sibling, device_id_type=MESH)
 
     @pl.when(leading)
     def _():
         for n in range(9):
-            ag_start(n, 2)
-    for n, (j, kind) in enumerate(STREAMS):
-        to_sibling(n, block_index(ORDERS[j], 2, pos, None))
-    ag_sent(1)
+            ag_start(n, 1)
 
     misc(3, gs.at[1 - section], gs.at[1 - section], sibling).wait()
     for l in range(2):
@@ -265,31 +265,46 @@
             par[l, 5:6, 48 * i : 48 * i + 48] = tile[6:7, 0:48]
     swap_ends.wait()
 
-    @pl.when(leading)
-    def _():
-        ag_forward(2)
-        ag_rest(2)
-        ag_sent(2)
-        pl.semaphore_signal(go_sem, inc=1, device_id=sibling, device_id_type=MESH)
-
-    @pl.when(jnp.logical_not(leading))
-    def _():
-        pl.semaphore_wait(go_sem, 1)
-        for n in range(9):
-            ag_start(n, 2)
-
     def from_sibling(l):
         for n, (j, kind) in enumerate(STREAMS):
             ref = gath[kind].at[l, j]
             remote(ref, ref, s_sib.at[n], r_sib.at[n], sibling).wait_recv()
 
+    @pl.when(leading)
+    def _():
+        ag_forward(1)
+        go(0)
+        ag_rest(1)
+        for n in range(9):
+            ag_start(n, 2)
+        own_across()
+        ag_forward(2)
+        go(1)
+        ag_rest(2)
+
     @pl.when(jnp.logical_not(leading))
     def _():
+        pl.semaphore_wait(go_sem.at[0], 1)
+        for n in range(9):
+            ag_start(n, 1)
+        ag_forward(1)
+        ag_rest(1)
+        own_across()
+        pl.semaphore_wait(go_sem.at[1], 1)
+        for n in range(9):
+            ag_start(n, 2)
         from_sibling(0)
+
+    landing = {}
 
     def rs_copy(n, phase, slot, src, to):
         j, kind = STREAMS[n]
-        dst = (recv0, recv1, recv2)[phase][kind].at[j, slot]
+        if phase == 2 and slot >= 4:
+            dst = landing[2, kind].at[j, slot - 4]
+        elif phase == 2:
+            dst = recv2[kind].at[j, slot]
+        else:
+            dst = landing[phase, kind].at[j, slot if phase == 1 else slot // 2]
         return remote(src, dst, s_rs.at[n, phase], r_rs.at[n, phase, slot], device(to))
 
     def rs_start(n, phase, part):
@@ -312,7 +327,7 @@
     def dterm(g):
         return term(3 + g, dps.at[12 + lax.rem(g, 2)], dps.at[6 + g])
 
-    def layers(wbuf, ebuf, obuf, zbuf, xbuf, ybuf, tbuf, hbuf, pebuf, masks, allowed, tri, sel, qcol, qrow, dtrow, heads, smat, gbuf, dgacc, rowq, rowx, acc, rbuf, wstage, ostage, estage, wsem, esem, osem, wssem, ossem, essem):
+    def layers(wbuf, ebuf, obuf, zbuf, xbuf, ybuf, tbuf, hbuf, pebuf, masks, allowed, tri, sel, qcol, qrow, dtrow, heads, smat, gbuf, dgacc, rowq, rowx, acc, rbuf, ut, ot, wsem, esem, osem, gsem):
         def copy_w(l, g):
             j, p = lax.div(g, 2), lax.rem(g, 2)
             return [pltpu.make_async_copy(gath[0].at[l, j, :, :, 2 * m + p], wbuf.at[g, :, :, pl.ds(48 * m, 48)], wsem.at[g, m]) for m in range(2)]
@@ -334,11 +349,14 @@
         def weights_e(p):
             return ebuf[p].reshape(D, 256)
 
-        start(copy_e(0))
-        for g in range(GROUPS):
-            start(copy_w(0, jnp.int32(g)))
-        for j in range(3):
-            start(copy_o(0, j))
+        def start_all(l):
+            start(copy_e(l))
+            for g in range(GROUPS):
+                start(copy_w(l, jnp.int32(g)))
+            for j in range(3):
+                start(copy_o(l, j))
+
+        start_all(0)
 
         rows = lax.broadcasted_iota(jnp.int32, (T, T), 0)
         cols = lax.broadcasted_iota(jnp.int32, (T, T), 1)
@@ -489,8 +507,10 @@
 
             lax.fori_loop(0, 4, first, 0)
             if l == 1:
-                for j in range(3):
-                    start(copy_o(0, j))
+                @pl.when(leading)
+                def _():
+                    for j in range(3):
+                        start(copy_o(0, j))
             r = rbuf[l, 1]
             masks[4] = jnp.broadcast_to(jnp.sum(acc[:, 0:128], axis=1, keepdims=True) * (1.0 / DI), (T, T)) * r * r * r
             prepare(l)
@@ -559,7 +579,9 @@
 
                 acc[...] += dot(dps[here], wbuf[g].reshape(D, 1024), ((1,), (1,)))
                 if l == 1:
-                    start(copy_w(0, g))
+                    @pl.when(leading)
+                    def _():
+                        start(copy_w(0, g))
                 return carry
 
             lax.fori_loop(0, GROUPS, second, 0)
@@ -595,7 +617,10 @@
             for p in range(2):
                 du = du + dot(dpes[slot(l), p], weights_e(p), ((1,), (1,)))
             if l == 1:
-                start(copy_e(0))
+                @pl.when(leading)
+                def _():
+                    start(copy_e(0))
+
             h = hbuf[...].astype(F32) if l == 1 else first_input()
             hn = h * rbuf[l, 0][:, 0:1]
             du = du * masks[3][:, 0:1]
@@ -632,58 +657,57 @@
             def stacked(ref, *index):
                 return jnp.concatenate([ref[(0,) + index], ref[(1,) + index]], axis=0)
 
+            for ref, turned, count in ((us_, ut, D // 128), (os_, ot, DI // 128)):
+                def turn(i, carry):
+                    at = pl.ds(pl.multiple_of(128 * i, 128), 128)
+                    turned[at, :] = jnp.transpose(stacked(ref, slice(None), at))
+                    return carry
+
+                lax.fori_loop(0, count, turn, 0)
+
             for p in range(2):
-                de = dot(stacked(us_), stacked(dpes, p), ((0,), (0,))).astype(BF).reshape(4, 4, 2, 3, 16, 256)
-                for j in range(3):
-                    for m in range(2):
-                        estage[j, m] = de[:, :, m, j]
-                ecopies = [pltpu.make_async_copy(estage.at[j, m], grad[2].at[j, :, :, 2 * m + p], essem.at[j, m]) for j in range(3) for m in range(2)]
-                start(ecopies)
-                finish(ecopies)
-            def w_at(i):
-                return lax.div(i, 8), lax.rem(lax.div(i, 2), 4), lax.rem(i, 2), pl.multiple_of(512 * lax.rem(i, 2), 128)
+                for zz in range(4):
+                    de = dot(ut[384 * zz : 384 * zz + 384, :], stacked(dpes, p))
+                    ebuf[p, zz] = de.astype(BF).reshape(4, 2, 3, 16, 256)
+            for p in range(2):
+                for m in range(2):
+                    for j in range(3):
+                        pltpu.make_async_copy(ebuf.at[p, :, :, m, j], grad[2].at[j, :, :, 2 * m + p], gsem.at[j, 2]).start()
+
+            def wstep(i, carry):
+                g, zz = lax.div(i, 4), lax.rem(i, 4)
+                u = ut[pl.ds(pl.multiple_of(384 * zz, 128), 384), :]
+                for half in range(2):
+                    at = slice(512 * half, 512 * half + 512)
+                    d = jnp.concatenate([dps[g, :, at], dps[6 + g, :, at]], axis=0)
+                    wbuf[g, zz, :, :, at] = dot(u, d).astype(BF).reshape(4, 96, 512)
+                j, p = lax.div(g, 2), lax.rem(g, 2)
+                for m in range(2):
+                    pltpu.make_async_copy(wbuf.at[g, zz, :, pl.ds(48 * m, 48)], grad[0].at[j, zz, :, 2 * m + p], gsem.at[j, 0]).start()
+                return carry
+
+            def ostep(i, carry):
+                j, zz = lax.div(i, 4), lax.rem(i, 4)
+                d = stacked(dvs, slice(None), pl.ds(pl.multiple_of(512 * j, 128), 512))
+                for half in range(2):
+                    o = ot[pl.ds(pl.multiple_of(768 * zz + 384 * half, 128), 384), :]
+                    obuf[j, zz, 2 * half : 2 * half + 2] = dot(o, d).astype(BF).reshape(2, 4, 48, 512)
+                pltpu.make_async_copy(obuf.at[j, zz], grad[1].at[j, zz], gsem.at[j, 1]).start()
+                return carry
+
+            def written(j, kind):
+                pltpu.make_async_copy(grad[kind].at[j], grad[kind].at[j], gsem.at[j, kind]).wait()
+                rs_start(3 * j + kind, 2, grad_part)
 
             for j in range(3):
-                def wcopy(i):
-                    g, zz, b, wide = w_at(i)
-                    return [pltpu.make_async_copy(wstage.at[b, :, pl.ds(48 * m, 48)], grad[0].at[j, zz, :, 2 * m + g, :, pl.ds(wide, 512)], wssem.at[b, m]) for m in range(2)]
-
-                def wstep(i, carry):
-                    @pl.when(i >= 2)
-                    def _():
-                        finish(wcopy(i - 2))
-                    g, zz, b, wide = w_at(i)
-                    u = stacked(us_, slice(None), pl.ds(pl.multiple_of(384 * zz, 128), 384))
-                    at = pl.ds(wide, 512)
-                    d = jnp.concatenate([dps[2 * j + g, :, at], dps[6 + 2 * j + g, :, at]], axis=0)
-                    wstage[b] = dot(u, d, ((0,), (0,))).astype(BF).reshape(4, 96, 512)
-                    start(wcopy(i))
-                    return carry
-
-                lax.fori_loop(0, 16, wstep, 0)
-                for i in (14, 15):
-                    finish(wcopy(jnp.int32(i)))
-                rs_start(3 * j, 2, grad_part)
-
-                def ocopy(i):
-                    b = lax.rem(i, 2)
-                    return [pltpu.make_async_copy(ostage.at[b], grad[1].at[j, lax.div(i, 4), pl.ds(2 * lax.rem(lax.div(i, 2), 2), 2), :, :, pl.ds(pl.multiple_of(256 * b, 128), 256)], ossem.at[b])]
-
-                def ostep(i, carry):
-                    @pl.when(i >= 2)
-                    def _():
-                        finish(ocopy(i - 2))
-                    o = stacked(os_, slice(None), pl.ds(pl.multiple_of(384 * lax.div(i, 2), 128), 384))
-                    b = lax.rem(i, 2)
-                    ostage[b] = dot(o, stacked(dvs, slice(None), pl.ds(pl.multiple_of(512 * j + 256 * b, 128), 256)), ((0,), (0,))).astype(BF).reshape(2, 4, 48, 256)
-                    start(ocopy(i))
-                    return carry
-
-                lax.fori_loop(0, 16, ostep, 0)
-                for i in (14, 15):
-                    finish(ocopy(jnp.int32(i)))
-                rs_start(3 * j + 1, 2, grad_part)
-                rs_start(3 * j + 2, 2, grad_part)
+                lax.fori_loop(8 * j, 8 * j + 8, wstep, 0)
+                if j > 0:
+                    written(j - 1, 1)
+                lax.fori_loop(4 * j, 4 * j + 4, ostep, 0)
+                written(j, 0)
+            written(2, 1)
+            for j in range(3):
+                written(j, 2)
 
         middle = forward(0, first_input()).astype(BF).astype(F32)
 
@@ -696,11 +720,7 @@
         def _():
             from_sibling(1)
 
-        start(copy_e(1))
-        for g in range(GROUPS):
-            start(copy_w(1, jnp.int32(g)))
-        for j in range(3):
-            start(copy_o(1, j))
+        start_all(1)
         out = forward(1, middle).astype(BF)
 
         @pl.when(leading)
@@ -717,6 +737,11 @@
         @pl.when(jnp.logical_not(leading))
         def _():
             products(1)
+            for j in range(3):
+                start(copy_o(0, j))
+            for g in range(GROUPS):
+                start(copy_w(0, jnp.int32(g)))
+            start(copy_e(0))
 
         d_first = backward(0, d_middle).astype(BF)
 
@@ -736,8 +761,8 @@
         V((2, T, DI), F32), V((2, T, DI), F32), V((2, T, DI), F32), V((T, DI), F32), V((T, D), BF), V((2, T, 384), F32),
         V((5, T, T), F32), V((T, T), F32), V((T, T), BF), V((512, T), BF), V((6, T, T), F32), V((6, 8, T), F32), V((6, 8, T), F32),
         V((2, 2, T, T), F32), V((2, 2, T, T), BF), V((2, T, T), F32), V((T, T), F32), V((T, T), F32), V((T, T), F32), V((T, D), F32), V((2, 2, T, T), F32),
-        V((2, 4, 96, 512), BF), V((2, 2, 4, 48, 256), BF), V((3, 2, 4, 4, 16, 256), BF),
-        pltpu.SemaphoreType.DMA((6, 2)), pltpu.SemaphoreType.DMA((2, 2, 3)), pltpu.SemaphoreType.DMA((3,)), pltpu.SemaphoreType.DMA((2, 2)), pltpu.SemaphoreType.DMA((2,)), pltpu.SemaphoreType.DMA((3, 2)),
+        V((D, 256), BF), V((DI, 256), BF),
+        pltpu.SemaphoreType.DMA((6, 2)), pltpu.SemaphoreType.DMA((2, 2, 3)), pltpu.SemaphoreType.DMA((3,)), pltpu.SemaphoreType.DMA((3, 3)),
     )
 
     end = misc(4, leaving, ends_out.at[section], sibling)
@@ -747,7 +772,12 @@
         it = iter(bufs)
         take = lambda n: [next(it) for _ in range(n)]
         ab, ob, db, eb, acc2, acc1, b1, b0, fin = (take(3) for _ in range(9))
-        fsend, gsend, sa2, sa1, lsem = it
+        fsend, gsend, fgot, ggot, sa2, sa1, lsem = it
+        for kind in range(3):
+            landing[2, kind], landing[1, kind], landing[0, kind] = eb[kind], b1[kind], b0[kind]
+        for axis in range(3):
+            for by in (1, 3):
+                pl.semaphore_signal(ready_sem, inc=1, device_id=device(moved(pos, axis, by)), device_id_type=MESH)
 
         def load(n, h, which, src, dst):
             return pltpu.make_async_copy(src, dst, lsem.at[n, h, which])
@@ -778,10 +808,14 @@
 
         def sent(phase):
             for n, (j, kind) in enumerate(STREAMS):
-                ref = (recv0, recv1, recv2)[phase][kind].at[j, pl.ds(0, 3 if phase == 0 else 6)]
+                if phase == 2:
+                    ref = grad[kind].at[j, pl.ds(0, 3)]
+                else:
+                    ref = landing[phase, kind].at[j, pl.ds(0, 3 if phase == 0 else 6)]
                 remote(ref, ref, s_rs.at[n, phase], r_rs.at[n, phase, 0], sibling).wait_send()
 
-        items = {phase: [(n, h) for n, (j, kind) in enumerate(STREAMS) for h in (0, 1) if has_half(kind, phase, h)] for phase in range(3)}
+        items = {phase: [(3 * j + kind, h) for kind in range(3) for j in range(3) for h in (0, 1) if has_half(kind, phase, h)] for phase in range(3)}
+        by_kind = [3 * j + kind for kind in range(3) for j in range(3)]
 
         def small_start(phase):
             axis = ORDERS[0][phase]
@@ -807,7 +841,6 @@
 
         term(10, tgot, tgot).wait_recv()
         gs[section] += tgot[...]
-        done = small_start(2)
         for n, h in items[2]:
             j, kind = STREAMS[n]
             _, halves = neighbours(n, 2)
@@ -817,6 +850,8 @@
             slot = neighbours(n, 2)[1][h][0]
             rs_copy(n, 2, slot, ab[kind].at[j, h], moved(pos, 0, 1)).wait_recv()
             load(n, h, 1, recv2[kind].at[j, slot], ab[kind].at[j, h]).start()
+        pl.semaphore_wait(ready_sem, 6)
+        done = small_start(2)
         for n, h in items[2]:
             j, kind = STREAMS[n]
             here, halves = neighbours(n, 2)
@@ -839,70 +874,50 @@
             low = min(order[:2])
             load(n, h, 0, grad_part(n, 0, h), ob[kind].at[j, h]).wait()
             load(n, h, 2, recv2[kind].at[j, 0], db[kind].at[j, h]).wait()
-            load(n, h, 3, recv2[kind].at[j, 0], eb[kind].at[j, h]).wait()
             place = (lambda a, b: (j, 2 * h + a, b)) if order[1] == low else (lambda a, b: (j, b, 2 * h + a))
             add(acc2[kind], [ob[kind].at[j, h], db[kind].at[j, h], eb[kind].at[j, h]], (2, 4), BF, place)
 
-        before = None
-        for n, h in items[2]:
-            j, kind = STREAMS[n]
-            slot = neighbours(n, 2)[1][h][3]
-            rs_copy(n, 2, slot, ab[kind].at[j, h], moved(pos, 0, 1)).wait_recv()
-            load(n, h, 3, recv2[kind].at[j, slot], eb[kind].at[j, h]).start()
-            if before is not None:
-                last2(*before)
-            before = (n, h)
-        last2(*before)
-
-        for phase in (1, 0):
-            recv, buf = (recv0, recv1)[phase], (b0, b1)[phase]
-
+        def part_of(phase):
             def part(n, k, h):
                 j, kind = STREAMS[n]
                 return acc2[kind].at[j, k, pl.ds(2 * h, 2)] if phase == 1 else acc1[kind].at[j, k]
 
+            return part
+
+        def arrived(n, phase, slot):
+            j, kind = STREAMS[n]
+            ref = landing[phase, kind].at[j, {2: slot - 4, 1: slot, 0: slot // 2}[phase]]
+            rs_copy(n, phase, slot, ref, moved(pos, 0, 1)).wait_recv()
+            return ref
+
+        for n, h in items[2]:
+            arrived(n, 2, neighbours(n, 2)[1][h][3])
+            last2(n, h)
+            if h == 1:
+                rs_start(n, 1, part_of(1))
+        done = small_start(1)
+        last_tile = None
+        for phase in (1, 0):
+            part = part_of(phase)
             dims = (2,) if phase == 1 else ()
-
-            def fetch(n, h, slot, which):
-                j, kind = STREAMS[n]
-                rs_copy(n, phase, slot, buf[kind].at[j, slot], moved(pos, 0, 1)).wait_recv()
-                load(n, h, which, recv[kind].at[j, slot], buf[kind].at[j, slot]).start()
-
-            def fetched(n, h, slot, which):
-                j, kind = STREAMS[n]
-                load(n, h, which, recv[kind].at[j, slot], buf[kind].at[j, slot]).wait()
-                return buf[kind].at[j, slot]
-
-            done = small_start(phase)
-            for n in range(9):
-                rs_start(n, phase, part)
-            for n, h in items[phase]:
-                fetch(n, h, neighbours(n, phase)[1][h][0], 1)
             for n, h in items[phase]:
                 slot, block, to, summed, _ = neighbours(n, phase)[1][h]
-                ref = fetched(n, h, slot, 1)
+                ref = arrived(n, phase, slot)
                 add(ref, [ref, part(n, block, h)], dims, BF)
                 rs_copy(n, phase, summed, ref, to).start()
             last_tile = done()
             for n, h in items[phase]:
-                fetch(n, h, neighbours(n, phase)[1][h][4], 2)
-
-            def last(n, h):
                 j, kind = STREAMS[n]
                 here, halves = neighbours(n, phase)
-                parts = [part(n, here, h), fetched(n, h, halves[h][4], 2), fetched(n, h, halves[h][3], 3)]
-                if phase == 1:
-                    add(acc1[kind], parts, dims, BF, lambda a: (j, 2 * h + a))
-                else:
+                parts = [part(n, here, h), arrived(n, phase, halves[h][4]), arrived(n, phase, halves[h][3])]
+                if phase == 0:
                     add(fin[kind].at[j], parts, dims, F32)
-
-            before = None
-            for n, h in items[phase]:
-                fetch(n, h, neighbours(n, phase)[1][h][3], 3)
-                if before is not None:
-                    last(*before)
-                before = (n, h)
-            last(*before)
+                    continue
+                add(acc1[kind], parts, dims, BF, lambda a: (j, 2 * h + a))
+                if h == 1:
+                    rs_start(n, 0, part_of(0))
+            if phase == 1:
+                done = small_start(0)
 
         for j in range(3):
             fsend[j] = jnp.where(even, fin[0][j, 24:48, :], fin[0][j, 0:24, :])
@@ -917,13 +932,7 @@
                 lanes = slice(512 * i, 512 * i + 512)
                 d_win[:, at] = jnp.where(even, fin[0][j, 0:24, lanes], fin[0][j, 24:48, lanes])
             d_wout[:, 512 * j : 512 * j + 512] = fin[1][j]
-        d_taps[...] = last_tile[0:4, 0:52]
-        d_bias[...] = last_tile[4:5, 0:52]
-        d_pre[...] = last_tile[5:6, 0:24]
-        d_gate[...] = last_tile[6:7, 0:48]
-        d_dtb[...] = last_tile[7:8, 0:48]
-        d_alog[...] = last_tile[5:6, 64:112]
-        d_skip[...] = last_tile[6:7, 64:112]
+        d_small[...] = last_tile
         swap_f.wait()
         swap_g.wait()
         for j in range(3):
@@ -936,9 +945,9 @@
             sent(phase)
 
     shapes = []
-    for lead, dtype in (((3, 2, 2, 4), BF),) * 4 + (((3, 4, 4), BF), ((3, 4), BF), ((3, 6, 2), BF), ((3, 6), BF), ((3,), F32)):
+    for lead, dtype in (((3, 2, 2, 4), BF),) * 4 + (((3, 4, 4), BF), ((3, 4), BF), ((3, 6, 2), BF), ((3, 3), BF), ((3,), F32)):
         shapes += [V(lead + dims, dtype) for dims in KINDS]
-    shapes += [V((3, 24, 1024), F32), V((24, 256), F32), V((4, 4, 8, 128), F32), V((4, 8, 128), F32)]
+    shapes += [V((3, 24, 1024), F32), V((24, 256), F32)] * 2 + [V((4, 4, 8, 128), F32), V((4, 8, 128), F32)]
     pl.run_scoped(sums, *shapes, pltpu.SemaphoreType.DMA((9, 2, 4)))
 
     end.wait()
@@ -946,10 +955,8 @@
         ref = gath[kind].at[section, j]
         remote(ref, ref, s_sib.at[n], r_sib.at[n], sibling).wait_send()
 
-    @pl.when(jnp.logical_not(leading))
-    def _():
-        ag_sent(2)
-
+    ag_sent(1)
+    ag_sent(2)
     for n, ref in enumerate((us_, os_, dvs)):
         term(n, ref.at[2], ref.at[1]).wait_send()
     for g in (4, 5):
@@ -964,33 +971,60 @@
     s = jax.ShapeDtypeStruct
     V, S = pltpu.VMEM, pltpu.SemaphoreType.DMA
     large = []
-    for lead in ((2, 3, 4, 4, 4), (3, 4, 4, 4), (3, 6, 2, 4), (3, 6, 2), (3, 6)):
+    for lead in ((2, 3, 4, 4, 4), (3, 4, 4, 4), (3, 4, 2, 4)):
         large += [s(lead + dims, BF) for dims in KINDS]
     return pl.pallas_call(
         step_kernel,
         out_shape=[
-            s((2, T, D), BF), s((24, 6448), F32), s((4, 52), F32), s((1, 52), F32), s((1, 24), F32), s((1, 48), F32), s((48, D), F32),
-            s((1, H), F32), s((1, H), F32), s((1, H), F32),
+            s((2, T, D), BF), s((24, 6448), F32), s((48, D), F32), s((8, 128), F32),
         ] + large,
         in_specs=[vm, vm, pl.BlockSpec(memory_space=pltpu.SMEM)] + [vm] * 9,
-        out_specs=[vm] * 10 + [any_] * 15,
+        out_specs=[vm] * 4 + [any_] * 9,
         scratch_shapes=[
-            V((3, 24, 1024), BF), V((24, 256), BF), V((3, 24, 1024), F32), V((24, 256), F32), V((2, 4, 4, 4, 8, 128), F32),
+            V((3, 24, 1024), BF), V((24, 256), BF), V((2, 4, 4, 4, 8, 128), F32),
             V((2, 8, CC), F32), V((2, 8, 128), F32), V((2, 8, CC), F32), V((4, 4, 4, 8, 128), F32),
             V((3, 4, 4, 8, 128), F32), V((3, 4, 8, 128), F32), V((3, 8, 128), F32),
             V((T, D), BF), V((T, D), BF), V((3, T, D), BF), V((3, T, DI), BF), V((3, T, D), BF), V((14, T, 1024), BF), V((3, 2, T, 256), BF),
             S((7,)), S((7,)), S((9, 3)), S((9, 3, 8)), S((6, 3)), S((6, 3)), S((9,)), S((9,)), S((9, 3)), S((9, 3, 6)), S((11,)), S((11,)), S((9,)),
-            pltpu.SemaphoreType.REGULAR,
+            pltpu.SemaphoreType.REGULAR((2,)), pltpu.SemaphoreType.REGULAR,
         ],
         compiler_params=pltpu.CompilerParams(collective_id=0, has_side_effects=True, vmem_limit_bytes=63 * 1024 * 1024),
         name="train_step",
-    )(ends, segs, counts, win, taps, bias, pre, gate, wout, dtb, alog, skip)[:10]
+    )(ends, segs, counts, win, taps, bias, pre, gate, wout, dtb, alog, skip)[:4]
+
+
+def results_kernel(ends, win, wout, tile, ends_out, d_win, d_taps, d_bias, d_pre, d_gate, d_wout, d_dtb, d_alog, d_skip):
+    ends_out[...] = ends[...]
+    d_win[...] = win[...]
+    d_wout[...] = wout[...]
+    d_taps[...] = tile[0:4, 0:52]
+    d_bias[...] = tile[4:5, 0:52]
+    d_pre[...] = tile[5:6, 0:24]
+    d_gate[...] = tile[6:7, 0:48]
+    d_dtb[...] = tile[7:8, 0:48]
+    d_alog[...] = tile[5:6, 64:112]
+    d_skip[...] = tile[6:7, 64:112]
+
+
+def results(ends, win, wout, tile):
+    vm = pl.BlockSpec(memory_space=pltpu.VMEM)
+    s = jax.ShapeDtypeStruct
+    return pl.pallas_call(
+        results_kernel,
+        out_shape=[
+            s((2, T, D), BF), s((24, 6448), F32), s((4, 52), F32), s((1, 52), F32), s((1, 24), F32), s((1, 48), F32), s((48, D), F32),
+            s((1, H), F32), s((1, H), F32), s((1, H), F32),
+        ],
+        in_specs=[vm] * 4,
+        out_specs=[vm] * 10,
+        name="results",
+    )(ends, win, wout, tile)
 
 
 def body(ends_in, seg_ids, block_counts, in_weight, conv_weight, conv_bias, pre_gain, gate_gain, out_weight, dt_bias, a_log, skip):
-    outs = step(
+    outs = results(*step(
         ends_in[0].reshape(2, T, D), seg_ids, block_counts, in_weight[0], conv_weight[0], conv_bias, pre_gain, gate_gain, out_weight[0], dt_bias, a_log, skip
-    )
+    ))
     ends_out, d_in, d_taps, d_bias, d_pre, d_gate, d_out, d_dtb, d_alog, d_skip = outs
     return ends_out.reshape(1, 2 * T, D), d_in[None], d_taps[None], d_bias, d_pre, d_gate, d_out[None], d_dtb, d_alog, d_skip
 

time: 432 us -> 346 us (0.80)
  Pallas kernels: 416 us -> 345 us
  local copies, waits for them, and re-layouts: 13.8 us -> 0 us
    pallas_call x1, Pallas kernels: 416 us -> 342 us  [step(): pl.pallas_call(step_kernel, out_shape=[s((2, T, D), BF), s((24, 6448), F3...]
    unnamed x10 -> x0, local copies, waits for them, and re-layouts: 13.8 us -> none
where the time goes in v3:
time: 346 us
  Pallas kernels  345 us (100%)
    pallas_call x1, Pallas kernels, step(): pl.pallas_call(step_kernel, out_shape=[s((2, T, D), BF), s((24, 6448), F3...  342 us

profile of v3, /device:TPU:0, one launch (start us, length us, event | category | flops | bytes accessed | tf_op | source)
XLA Modules:
  0.0 345.8 jit_solution(17312711670753630773)
XLA Ops:
  0.6 342.4 %train_step.1 = (bf16[2,128,1536]{2,1,0:T(8,128)(2,1)}, f32[24,6448]{1,0:T(8,128)}, f32[48,1536]{1,0:T(8,128)}, f32[8,128]{1,0:T(8,128)}, bf16[2,3,4,4,4,48,1024...) custom-call(bf16[2,128,1536]{2,1,0:T(8,128)(2,1)} %bitcast.8, ...), custom_call_target="tpu_custom_call" | custom-call | tf_op jit(solution)/shard_map/train_step/pallas_call | solution.py:976
  343.1 2.6 results.1

commit v4 on v3

--- a/solution.py
+++ b/solution.py
@@ -73,7 +73,8 @@
     ends, segs, counts, win, taps_in, bias_in, pre_in, gate_in, wout, dtb_in, alog_in, skip_in = take(12)
     ends_out, d_win, d_wout, d_small = take(4)
     gath, grad, recv2 = take(3), take(3), take(3)
-    wgot, egot, gs, par, hp, gr, tgot, sg2, sg1, sg0, swapped, leaving, us_, os_, dvs, dps, dpes = take(17)
+    spill, = take(1)
+    wgot, egot, gs, par, hp, gr, hg, sg2, sg1, sg0, swapped, hbuf, us_, os_, dvs, dps, dpes = take(17)
     (s_misc, r_misc, s_ag, r_ag, s_small, r_small, s_sib, r_sib, s_rs, r_rs, s_terms, r_terms, own_sem, go_sem, ready_sem) = take(15)
 
     section = lax.axis_index("section")
@@ -129,35 +130,35 @@
         ref = gath[kind].at[section, j].at[index]
         remote(ref, ref, s_sib.at[n], r_sib.at[n], sibling).start()
 
-    def ag_arrived(n, phase, slot, index):
+    def ag_arrived(n, phase, slot, index, share):
         j, kind = STREAMS[n]
         ag_copy(n, phase, slot, gath[kind].at[section, j].at[index], index, moved(pos, 0, 1)).wait_recv()
-        if phase == 2:
+        if share:
             to_sibling(n, index)
 
-    def ag_forward(phase):
+    def ag_forward(phase, share=False):
         for n, (j, kind) in enumerate(STREAMS):
             order = ORDERS[j]
             right, left = moved(pos, order[phase], 1), moved(pos, order[phase], 3)
             for slot, h, source, to in ((0, 0, left, right), (1, 1, right, left)):
                 if has_half(kind, phase, h):
-                    ag_arrived(n, phase, slot, block_index(order, phase, source, h))
+                    ag_arrived(n, phase, slot, block_index(order, phase, source, h), share)
                     for q, index in enumerate(ag_pieces(n, phase, source, h)):
                         ag_copy(n, phase, 4 + 2 * slot + q, gath[kind].at[section, j].at[index], index, to).start()
 
-    def ag_rest(phase):
+    def ag_rest(phase, share=False):
         for n, (j, kind) in enumerate(STREAMS):
             order = ORDERS[j]
             right, left = moved(pos, order[phase], 1), moved(pos, order[phase], 3)
             for slot, h, source in ((2, 1, left), (3, 0, right)):
                 if has_half(kind, phase, h):
-                    ag_arrived(n, phase, slot, block_index(order, phase, source, h))
+                    ag_arrived(n, phase, slot, block_index(order, phase, source, h), share)
         for q in range(2 if phase == 2 else 1):
             for n, (j, kind) in enumerate(STREAMS):
                 far = moved(pos, ORDERS[j][phase], 2)
                 for slot in (0, 1):
                     if has_half(kind, phase, slot):
-                        ag_arrived(n, phase, 4 + 2 * slot + q, ag_pieces(n, phase, far, slot)[q])
+                        ag_arrived(n, phase, 4 + 2 * slot + q, ag_pieces(n, phase, far, slot)[q], share)
 
     def ag_sent(phase):
         for n, (j, kind) in enumerate(STREAMS):
@@ -176,7 +177,8 @@
             sent.append(c)
         return sent
 
-    swap_ends = misc(2, ends.at[1 - section], swapped, sibling)
+    trailing = jnp.logical_not(leading)
+    cotangent_0 = misc(2, ends.at[0], swapped, sibling)
     small_across = misc(3, gs.at[section], gs.at[section], sibling)
 
     def prologue(wsend, esend, uw, uo, ue, us):
@@ -202,8 +204,13 @@
         pl.semaphore_wait(barrier, 10)
         swap_w = misc(0, wsend, wgot, device(partner))
         swap_e = misc(1, esend, egot, device(partner))
-        for c in (swap_w, swap_e, swap_ends):
-            c.start()
+        swap_w.start()
+        swap_e.start()
+
+        @pl.when(trailing)
+        def _():
+            cotangent_0.start()
+
 
         small = small_gather(0)
         swap_w.wait()
@@ -263,8 +270,6 @@
             par[l, 0:5, 52 * i : 52 * i + 52] = tile[0:5, 0:52]
             par[l, 7:8, 24 * i : 24 * i + 24] = tile[5:6, 0:24]
             par[l, 5:6, 48 * i : 48 * i + 48] = tile[6:7, 0:48]
-    swap_ends.wait()
-
     def from_sibling(l):
         for n, (j, kind) in enumerate(STREAMS):
             ref = gath[kind].at[l, j]
@@ -277,12 +282,11 @@
         ag_rest(1)
         for n in range(9):
             ag_start(n, 2)
-        own_across()
         ag_forward(2)
         go(1)
         ag_rest(2)
 
-    @pl.when(jnp.logical_not(leading))
+    @pl.when(trailing)
     def _():
         pl.semaphore_wait(go_sem.at[0], 1)
         for n in range(9):
@@ -293,7 +297,6 @@
         pl.semaphore_wait(go_sem.at[1], 1)
         for n in range(9):
             ag_start(n, 2)
-        from_sibling(0)
 
     landing = {}
 
@@ -327,7 +330,7 @@
     def dterm(g):
         return term(3 + g, dps.at[12 + lax.rem(g, 2)], dps.at[6 + g])
 
-    def layers(wbuf, ebuf, obuf, zbuf, xbuf, ybuf, tbuf, hbuf, pebuf, masks, allowed, tri, sel, qcol, qrow, dtrow, heads, smat, gbuf, dgacc, rowq, rowx, acc, rbuf, ut, ot, wsem, esem, osem, gsem):
+    def layers(wbuf, ebuf, obuf, zbuf, xbuf, ybuf, tbuf, pebuf, masks, coef, allowed, tri, sel, qcol, qrow, dtrow, heads, smat, gbuf, dgacc, rowq, rowx, acc, rbuf, ut, ot, wsem, esem, osem, gsem, psem):
         def copy_w(l, g):
             j, p = lax.div(g, 2), lax.rem(g, 2)
             return [pltpu.make_async_copy(gath[0].at[l, j, :, :, 2 * m + p], wbuf.at[g, :, :, pl.ds(48 * m, 48)], wsem.at[g, m]) for m in range(2)]
@@ -356,17 +359,21 @@
             for j in range(3):
                 start(copy_o(l, j))
 
-        start_all(0)
+        @pl.when(leading)
+        def _():
+            start_all(0)
 
         rows = lax.broadcasted_iota(jnp.int32, (T, T), 0)
         cols = lax.broadcasted_iota(jnp.int32, (T, T), 1)
-        seg = jnp.where(leading, segs[0:1, :], segs[1:2, :]).astype(F32)
-        seg_s = jnp.broadcast_to(seg, (T, T))
-        seg_t = jnp.transpose(seg_s)
-        allowed[...] = jnp.where(rows >= cols, jnp.where(seg_t == seg_s, 1.0, 0.0), 0.0)
-        for d in (1, 2, 3):
-            masks[d - 1] = jnp.where(rows >= d, jnp.where(pltpu.roll(seg_t, d, 0) == seg_t, 1.0, 0.0), 0.0)
-        masks[3] = jnp.where(rows < counts[section], 1.0, 0.0)
+        def set_block(b):
+            seg = jnp.where(b == 0, segs[0:1, :], segs[1:2, :]).astype(F32)
+            seg_s = jnp.broadcast_to(seg, (T, T))
+            seg_t = jnp.transpose(seg_s)
+            allowed[...] = jnp.where(rows >= cols, jnp.where(seg_t == seg_s, 1.0, 0.0), 0.0)
+            for d in (1, 2, 3):
+                masks[d - 1] = jnp.where(rows >= d, jnp.where(pltpu.roll(seg_t, d, 0) == seg_t, 1.0, 0.0), 0.0)
+            masks[3] = jnp.where(rows < counts[b], 1.0, 0.0)
+
         tri[...] = jnp.where(rows >= cols, 1.0, 0.0).astype(BF)
         srow = lax.broadcasted_iota(jnp.int32, (512, T), 0)
         scol = lax.broadcasted_iota(jnp.int32, (512, T), 1)
@@ -408,112 +415,111 @@
         def tile_at(g, k):
             return pl.ds(pl.multiple_of(512 * g + 128 * k, 128), 128)
 
-        def prepare(l):
-            q = heads[l, 1]
+        def prepare(s):
+            q = heads[s, 1]
             qt = jnp.transpose(q)
-            dtt = jnp.transpose(heads[l, 0])
+            dtt = jnp.transpose(heads[s, 0])
             for g in range(GROUPS):
                 qcol[g] = q if g == 0 else pltpu.roll(q, T - 8 * g, 1)
                 qrow[g] = qt[8 * g : 8 * g + 8, :]
                 dtrow[g] = dtt[8 * g : 8 * g + 8, :]
 
-        def slot(l):
-            return lax.select(section == l, 0, 2)
-
-        def first_input():
-            return jnp.where(leading, ends[section].astype(F32), swapped[...].astype(F32))
-
-        def forward(l, h):
-            if l == 1:
-                hbuf[...] = h.astype(BF)
+        def when_first(first, fn):
+            if first is True:
+                fn()
+            else:
+                pl.when(first)(fn)
+
+        def forward(l, h, s, z, b, sl, first):
+            set_block(b)
             rs = lax.rsqrt(jnp.sum(h * h, axis=1, keepdims=True) * (1.0 / D) + EPSILON)
-            rbuf[l, 0] = jnp.broadcast_to(rs, (T, T))
-            us_[slot(l)] = (h * rs * par[l, 7:8, 0:D] * masks[3][:, 0:1]).astype(BF)
-            finish(copy_e(l))
-            pebuf[l, :, 0:256] = dot(us_[slot(l)], weights_e(0))
-            pebuf[l, :, 256:384] = dot(us_[slot(l)], weights_e(1))[:, 0:128]
+            rbuf[s, 0] = jnp.broadcast_to(rs, (T, T))
+            us_[sl] = (h * rs * par[l, 7:8, 0:D] * masks[3][:, 0:1]).astype(BF)
+            when_first(first, lambda: finish(copy_e(l)))
+            pebuf[s, :, 0:256] = dot(us_[sl], weights_e(0))
+            pebuf[s, :, 256:384] = dot(us_[sl], weights_e(1))[:, 0:128]
             for j in range(2):
                 at = slice(DI + 128 * j, DI + 128 * j + 128)
-                c, _ = conv(pebuf[l, :, 128 * j : 128 * j + 128], par[l, 0:4, at], par[l, 4:5, at])
-                smat[l, j] = (c * sigmoid(c)).astype(BF)
-            v = pebuf[l, :, 256:384] + rate_bias(l)
+                c, _ = conv(pebuf[s, :, 128 * j : 128 * j + 128], par[l, 0:4, at], par[l, 4:5, at])
+                smat[s, j] = (c * sigmoid(c)).astype(BF)
+            v = pebuf[s, :, 256:384] + rate_bias(l)
             dt = jnp.maximum(v, 0.0) + jnp.log1p(jnp.exp(-jnp.abs(v)))
-            heads[l, 0] = dt
-            heads[l, 1] = exact_dot(tri[...], dt * rate(l)) * LOG2E
-            gbuf[l] = dot(smat[l, 1], smat[l, 0], ((1,), (1,))) * allowed[...]
-            prepare(l)
+            heads[s, 0] = dt
+            heads[s, 1] = exact_dot(tri[...], dt * rate(l)) * LOG2E
+            gbuf[s] = dot(smat[s, 1], smat[s, 0], ((1,), (1,))) * allowed[...]
+            prepare(s)
             acc[:, 0:128] = jnp.zeros((T, T), F32)
 
             def group(g, carry):
-                finish(copy_w(l, g))
-                p = dot(us_[slot(l)], wbuf[g].reshape(D, 1024))
+                when_first(first, lambda: finish(copy_w(l, g)))
                 wide = pl.ds(pl.multiple_of(512 * g, 128), 512)
-                zbuf[l, :, wide] = p[:, 0:512]
-                xbuf[l, :, wide] = p[:, 512:1024]
+                zbuf[z, :, wide] = dot(us_[sl], wbuf[g, :, :, :, 0:512].reshape(D, 512))
+                xbuf[z, :, wide] = dot(us_[sl], wbuf[g, :, :, :, 512:1024].reshape(D, 512))
                 for k in range(4):
                     at = tile_at(g, k)
-                    c, _ = conv(xbuf[l, :, at], par[l, 0:4, at], par[l, 4:5, at])
+                    c, _ = conv(xbuf[z, :, at], par[l, 0:4, at], par[l, 4:5, at])
                     x = c * sigmoid(c)
                     xb = x.astype(BF)
                     both = jnp.concatenate([keep_lanes(xb, low_lanes), keep_lanes(xb, ~low_lanes)], axis=0)
-                    w = jnp.concatenate([(gbuf[l] * decay(g, 2 * k + i)).astype(BF) for i in range(2)], axis=1)
+                    w = jnp.concatenate([(gbuf[s] * decay(g, 2 * k + i)).astype(BF) for i in range(2)], axis=1)
                     y = dot(w, both) + par[l, 6:7, at] * x
-                    ybuf[l, :, at] = y
-                    z = zbuf[l, :, at]
-                    e = y * (z * sigmoid(z))
+                    ybuf[z, :, at] = y
+                    zz_ = zbuf[z, :, at]
+                    e = y * (zz_ * sigmoid(zz_))
                     tbuf[:, at] = e
                     acc[:, 0:128] += e * e
                 return carry
 
             lax.fori_loop(0, GROUPS, group, 0)
             r = lax.rsqrt(jnp.sum(acc[:, 0:128], axis=1, keepdims=True) * (1.0 / DI) + EPSILON)
-            rbuf[l, 1] = jnp.broadcast_to(r, (T, T))
+            rbuf[s, 1] = jnp.broadcast_to(r, (T, T))
             for g in range(GROUPS):
                 at = slice(512 * g, 512 * g + 512)
-                os_[slot(l), :, at] = (tbuf[:, at] * r * par[l, 5:6, at]).astype(BF)
+                os_[sl, :, at] = (tbuf[:, at] * r * par[l, 5:6, at]).astype(BF)
             for j in range(3):
-                finish(copy_o(l, j))
-                acc[:, 512 * j : 512 * j + 512] = dot(os_[slot(l)], obuf[j].reshape(DI, 512))
+                when_first(first, lambda j=j: finish(copy_o(l, j)))
+                acc[:, 512 * j : 512 * j + 512] = dot(os_[sl], obuf[j].reshape(DI, 512))
             return h + acc[...]
 
-        def backward(l, dh):
-            dvs[slot(l)] = dh.astype(BF)
-
-            @pl.when(section != l)
-            def _():
-                for n, ref in enumerate((us_, os_, dvs)):
-                    term(n, ref.at[2], ref.at[1]).start()
-
-            if l == 0:
-                for j in range(3):
-                    finish(copy_o(0, j))
+        def backward(l, h, dh, s, z, b, sl, gi, first):
+            set_block(b)
+            if l == 1:
+                dvs[sl] = dh.astype(BF)
+
+            if l == 1:
+                @pl.when(leading)
+                def _():
+                    for n, ref in enumerate((us_, os_, dvs)):
+                        term(n, ref.at[2], ref.at[1]).start()
+            else:
+                when_first(first, lambda: [finish(copy_o(0, j)) for j in range(3)] and None)
             acc[:, 0:128] = jnp.zeros((T, T), F32)
 
-            def first(zz, carry):
+            def gated_back(zz, carry):
                 wide = pl.ds(pl.multiple_of(768 * zz, 128), 768)
                 do = None
                 for j in range(3):
-                    part = dot(dvs[slot(l), :, 512 * j : 512 * j + 512], obuf[j, zz].reshape(768, 512), ((1,), (1,)))
+                    part = dot(dvs[sl, :, 512 * j : 512 * j + 512], obuf[j, zz].reshape(768, 512), ((1,), (1,)))
                     do = part if do is None else do + part
                 tbuf[:, wide] = do
                 for k in range(6):
                     at = pl.ds(pl.multiple_of(768 * zz + 128 * k, 128), 128)
-                    z = zbuf[l, :, at]
-                    e = ybuf[l, :, at] * (z * sigmoid(z))
+                    zz_ = zbuf[z, :, at]
+                    e = ybuf[z, :, at] * (zz_ * sigmoid(zz_))
                     prod = tbuf[:, at] * e
-                    gr[l, 5:6, at] = total(prod * rbuf[l, 1])
+                    gr[gi, 5:6, at] = total(prod * rbuf[s, 1])
                     acc[:, 0:128] += prod * par[l, 5:6, at]
                 return carry
 
-            lax.fori_loop(0, 4, first, 0)
+            lax.fori_loop(0, 4, gated_back, 0)
             if l == 1:
                 @pl.when(leading)
                 def _():
                     for j in range(3):
                         start(copy_o(0, j))
-            r = rbuf[l, 1]
-            masks[4] = jnp.broadcast_to(jnp.sum(acc[:, 0:128], axis=1, keepdims=True) * (1.0 / DI), (T, T)) * r * r * r
-            prepare(l)
+            r = rbuf[s, 1]
+            coef[...] = jnp.broadcast_to(jnp.sum(acc[:, 0:128], axis=1, keepdims=True) * (1.0 / DI), (T, T)) * r * r * r
+            prepare(s)
             dgacc[...] = jnp.zeros((T, T), F32)
             rowq[...] = jnp.zeros((T, T), F32)
             rowx[...] = jnp.zeros((T, T), F32)
@@ -521,27 +527,28 @@
 
             def second(g, carry):
                 if l == 0:
-                    finish(copy_w(0, g))
-
-                here = lax.select(section == l, g, 12 + lax.rem(g, 2))
-
-                @pl.when(jnp.logical_and(section != l, g >= 2))
-                def _():
-                    dterm(g - 2).wait_send()
+                    when_first(first, lambda: finish(copy_w(0, g)))
+                    here = 6 * b + g
+                else:
+                    here = lax.select(leading, 12 + lax.rem(g, 2), g)
+
+                    @pl.when(jnp.logical_and(leading, g >= 2))
+                    def _():
+                        dterm(g - 2).wait_send()
 
                 sums_q, sums_x = None, None
                 for k in range(4):
                     at = tile_at(g, k)
-                    z = zbuf[l, :, at]
-                    y = ybuf[l, :, at]
-                    sz = sigmoid(z)
-                    silu = z * sz
-                    de = rbuf[l, 1] * (tbuf[:, at] * par[l, 5:6, at]) - (y * silu) * masks[4]
+                    zz_ = zbuf[z, :, at]
+                    y = ybuf[z, :, at]
+                    sz = sigmoid(zz_)
+                    silu = zz_ * sz
+                    de = rbuf[s, 1] * (tbuf[:, at] * par[l, 5:6, at]) - (y * silu) * coef[...]
                     dyb = (de * silu).astype(BF)
                     dz = de * y * (sz + silu * (1.0 - sz))
                     dps[here, :, 128 * k : 128 * k + 128] = dz.astype(BF)
                     taps = par[l, 0:4, at]
-                    c, shifts = conv(xbuf[l, :, at], taps, par[l, 4:5, at])
+                    c, shifts = conv(xbuf[z, :, at], taps, par[l, 4:5, at])
                     sc = sigmoid(c)
                     x = c * sc
                     xb = x.astype(BF)
@@ -553,13 +560,13 @@
                     ws, dg = [], None
                     for i in range(2):
                         e = decay(g, 2 * k + i)
-                        ws.append((gbuf[l] * e).astype(BF))
+                        ws.append((gbuf[s] * e).astype(BF))
                         part = dw[:, 128 * i : 128 * i + 128] * e
                         dg = part if dg is None else dg + part
                     dgacc[...] += dg
                     dx0 = dot(jnp.concatenate(ws, axis=0), dyt, ((0,), (0,)))
                     dx = dx0 + skip * dyw
-                    gr[l, 6:7, at] = total(dyw * x)
+                    gr[gi, 6:7, at] = total(dyw * x)
                     one = sel[128 * k : 128 * k + 128, :]
                     part = exact_dot(one, dyw * (y - skip * x), flip=True, terms=2)
                     sums_q = part if sums_q is None else sums_q + part
@@ -567,17 +574,19 @@
                     sums_x = part if sums_x is None else sums_x + part
                     dc = dx * (sc + x * (1.0 - sc))
                     for t in range(4):
-                        gr[l, t : t + 1, at] = total(dc * shifts[t])
-                    gr[l, 4:5, at] = total(dc)
+                        gr[gi, t : t + 1, at] = total(dc * shifts[t])
+                    gr[gi, 4:5, at] = total(dc)
                     dps[here, :, 512 + 128 * k : 640 + 128 * k] = conv_back(dc, taps).astype(BF)
                 rowq[...] += pltpu.roll(sums_q, 8 * g, 1)
                 rowx[...] += pltpu.roll(sums_x, 8 * g, 1)
 
-                @pl.when(section != l)
-                def _():
-                    dterm(g).start()
-
-                acc[...] += dot(dps[here], wbuf[g].reshape(D, 1024), ((1,), (1,)))
+                if l == 1:
+                    @pl.when(leading)
+                    def _():
+                        dterm(g).start()
+
+                for zz in range(4):
+                    acc[:, 384 * zz : 384 * zz + 384] += dot(dps[here], wbuf[g, zz].reshape(384, 1024), ((1,), (1,)))
                 if l == 1:
                     @pl.when(leading)
                     def _():
@@ -586,84 +595,82 @@
 
             lax.fori_loop(0, GROUPS, second, 0)
             dg = (dgacc[...] * allowed[...]).astype(BF)
-            d_states = (dot(dg, smat[l, 1], ((0,), (0,))), dot(dg, smat[l, 0]))
+            d_states = (dot(dg, smat[s, 1], ((0,), (0,))), dot(dg, smat[s, 0]))
             for j in range(2):
                 at = slice(DI + 128 * j, DI + 128 * j + 128)
                 taps = par[l, 0:4, at]
-                c, shifts = conv(pebuf[l, :, 128 * j : 128 * j + 128], taps, par[l, 4:5, at])
+                c, shifts = conv(pebuf[s, :, 128 * j : 128 * j + 128], taps, par[l, 4:5, at])
                 sc = sigmoid(c)
                 dc = d_states[j] * (sc + c * sc * (1.0 - sc))
                 for t in range(4):
-                    gr[l, t : t + 1, at] = total(dc * shifts[t])
-                gr[l, 4:5, at] = total(dc)
-                dpes[slot(l), 0, :, 128 * j : 128 * j + 128] = conv_back(dc, taps).astype(BF)
-            v = pebuf[l, :, 256:384] + rate_bias(l)
+                    gr[gi, t : t + 1, at] = total(dc * shifts[t])
+                gr[gi, 4:5, at] = total(dc)
+                dpes[sl, 0, :, 128 * j : 128 * j + 128] = conv_back(dc, taps).astype(BF)
+            v = pebuf[s, :, 256:384] + rate_bias(l)
             sv = sigmoid(v)
-            dt = heads[l, 0]
+            dt = heads[s, 0]
             back = exact_dot(tri[...], rowq[...] - rowx[...], ((0,), (0,)))
             ratio = jnp.where(v < -15.0, 1.0, sv / jnp.maximum(dt, 1e-30))
             dr = jnp.where(cols < H, rowx[...] * ratio + back * rate(l) * sv, 0.0)
             d_rate = total(jnp.where(cols < H, back * dt, 0.0)) * rate(l)
-            dpes[slot(l), 1, :, 0:128] = dr.astype(BF)
-            dpes[slot(l), 1, :, 128:256] = jnp.zeros((T, T), BF)
-
-            @pl.when(section != l)
-            def _():
-                term(9, dpes.at[2], dpes.at[1]).start()
-
-            if l == 0:
-                finish(copy_e(0))
+            dpes[sl, 1, :, 0:128] = dr.astype(BF)
+            dpes[sl, 1, :, 128:256] = jnp.zeros((T, T), BF)
+
+            if l == 1:
+                @pl.when(leading)
+                def _():
+                    term(9, dpes.at[2], dpes.at[1]).start()
+            else:
+                when_first(first, lambda: finish(copy_e(0)))
             du = acc[...]
             for p in range(2):
-                du = du + dot(dpes[slot(l), p], weights_e(p), ((1,), (1,)))
+                du = du + dot(dpes[sl, p], weights_e(p), ((1,), (1,)))
             if l == 1:
                 @pl.when(leading)
                 def _():
                     start(copy_e(0))
 
-            h = hbuf[...].astype(F32) if l == 1 else first_input()
-            hn = h * rbuf[l, 0][:, 0:1]
+            hn = h * rbuf[s, 0][:, 0:1]
             du = du * masks[3][:, 0:1]
-            gr[l, 7:8, 0:D] = total(du * hn)
+            gr[gi, 7:8, 0:D] = total(du * hn)
             t = du * par[l, 7:8, 0:D]
-            s = jnp.sum(t * hn, axis=1, keepdims=True) * (1.0 / D)
-            dh_in = dh + rbuf[l, 0][:, 0:1] * (t - hn * s)
+            mean = jnp.sum(t * hn, axis=1, keepdims=True) * (1.0 / D)
+            dh_in = dh + rbuf[s, 0][:, 0:1] * (t - hn * mean)
+            hg[gi, 0:1] = total(dr)
+            hg[gi, 1:2] = d_rate
+            return dh_in
+
+        def small_tiles(l):
             skips = jnp.zeros((8, T), F32)
             for g in range(GROUPS):
-                mine = exact_dot(sel[...], jnp.broadcast_to(gr[l, 6:7, 512 * g : 512 * g + 512], (8, 512)), flip=True)
+                mine = exact_dot(sel[...], jnp.broadcast_to(gr[0, 6:7, 512 * g : 512 * g + 512], (8, 512)), flip=True)
                 skips = skips + (mine if g == 0 else pltpu.roll(mine, 8 * g, 1))
             for i in range(64):
                 tile = gs.at[l, i // 16, i // 4 % 4, i % 4]
-                tile[0:5, 0:52] = gr[l, 0:5, 52 * i : 52 * i + 52]
-                tile[5:6, 0:24] = gr[l, 7:8, 24 * i : 24 * i + 24]
-                tile[6:7, 0:48] = gr[l, 5:6, 48 * i : 48 * i + 48]
-                tile[7:8, 0:128] = total(dr)
-                tile[5:6, 64:112] = d_rate[:, 0:48]
+                tile[0:5, 0:52] = gr[0, 0:5, 52 * i : 52 * i + 52]
+                tile[5:6, 0:24] = gr[0, 7:8, 24 * i : 24 * i + 24]
+                tile[6:7, 0:48] = gr[0, 5:6, 48 * i : 48 * i + 48]
+                tile[7:8, 0:128] = hg[0, 0:1]
+                tile[5:6, 64:112] = hg[0, 1:2, 0:48]
                 tile[6:7, 64:112] = skips[0:1, 0:48]
 
-            @pl.when(section != l)
-            def _():
-                term(10, gs.at[l], tgot).start()
-
-            return dh_in
-
         def products(l):
-            for n, ref in enumerate((us_, os_, dvs)):
-                term(n, ref.at[2], ref.at[1]).wait_recv()
-            for g in range(GROUPS):
-                dterm(g).wait_recv()
-            term(9, dpes.at[2], dpes.at[1]).wait_recv()
+            if l == 1:
+                for n, ref in enumerate((us_, os_, dvs)):
+                    term(n, ref.at[2], ref.at[1]).wait_recv()
+                for g in range(GROUPS):
+                    dterm(g).wait_recv()
+                term(9, dpes.at[2], dpes.at[1]).wait_recv()
 
             def stacked(ref, *index):
                 return jnp.concatenate([ref[(0,) + index], ref[(1,) + index]], axis=0)
 
-            for ref, turned, count in ((us_, ut, D // 128), (os_, ot, DI // 128)):
-                def turn(i, carry):
-                    at = pl.ds(pl.multiple_of(128 * i, 128), 128)
-                    turned[at, :] = jnp.transpose(stacked(ref, slice(None), at))
-                    return carry
-
-                lax.fori_loop(0, count, turn, 0)
+            def turn(i, carry):
+                at = pl.ds(pl.multiple_of(128 * i, 128), 128)
+                ut[at, :] = jnp.transpose(stacked(us_, slice(None), at))
+                return carry
+
+            lax.fori_loop(0, D // 128, turn, 0)
 
             for p in range(2):
                 for zz in range(4):
@@ -686,13 +693,16 @@
                     pltpu.make_async_copy(wbuf.at[g, zz, :, pl.ds(48 * m, 48)], grad[0].at[j, zz, :, 2 * m + p], gsem.at[j, 0]).start()
                 return carry
 
-            def ostep(i, carry):
-                j, zz = lax.div(i, 4), lax.rem(i, 4)
-                d = stacked(dvs, slice(None), pl.ds(pl.multiple_of(512 * j, 128), 512))
-                for half in range(2):
-                    o = ot[pl.ds(pl.multiple_of(768 * zz + 384 * half, 128), 384), :]
-                    obuf[j, zz, 2 * half : 2 * half + 2] = dot(o, d).astype(BF).reshape(2, 4, 48, 512)
-                pltpu.make_async_copy(obuf.at[j, zz], grad[1].at[j, zz], gsem.at[j, 1]).start()
+            def ostep(zz, carry):
+                for i in range(6):
+                    at = pl.ds(pl.multiple_of(768 * zz + 128 * i, 128), 128)
+                    ot[128 * i : 128 * i + 128, :] = jnp.transpose(stacked(os_, slice(None), at))
+                for j in range(3):
+                    d = stacked(dvs, slice(None), slice(512 * j, 512 * j + 512))
+                    for half in range(2):
+                        o = ot[384 * half : 384 * half + 384, :]
+                        obuf[j, zz, 2 * half : 2 * half + 2] = dot(o, d).astype(BF).reshape(2, 4, 48, 512)
+                    pltpu.make_async_copy(obuf.at[j, zz], grad[1].at[j, zz], gsem.at[j, 1]).start()
                 return carry
 
             def written(j, kind):
@@ -702,71 +712,108 @@
             for j in range(3):
                 lax.fori_loop(8 * j, 8 * j + 8, wstep, 0)
                 if j > 0:
-                    written(j - 1, 1)
-                lax.fori_loop(4 * j, 4 * j + 4, ostep, 0)
-                written(j, 0)
-            written(2, 1)
-            for j in range(3):
-                written(j, 2)
-
-        middle = forward(0, first_input()).astype(BF).astype(F32)
-
-        @pl.when(jnp.logical_not(leading))
-        def _():
-            ag_forward(2)
-            ag_rest(2)
+                    written(j - 1, 0)
+            lax.fori_loop(0, 4, ostep, 0)
+            written(2, 0)
+            for kind in (1, 2):
+                for j in range(3):
+                    written(j, kind)
+
+        middle_1 = misc(7, dvs.at[0], hbuf, sibling)
+        out_0 = misc(4, ends_out.at[0], ends_out.at[0], sibling)
+        d_middle_1 = misc(8, dvs.at[2], dvs.at[1], sibling)
+        sets = [pltpu.make_async_copy(ref.at[0], spill.at[n], psem.at[n]) for n, ref in enumerate((zbuf, xbuf, ybuf))]
+        sets_back = [pltpu.make_async_copy(spill.at[n], ref.at[0], psem.at[n]) for n, ref in enumerate((zbuf, xbuf, ybuf))]
 
         @pl.when(leading)
         def _():
+            def block(b, carry):
+                out = forward(0, ends[b].astype(F32), b, b, b, b, b == 0).astype(BF)
+
+                @pl.when(b == 0)
+                def _():
+                    hbuf[...] = out
+                    start(sets)
+
+                @pl.when(b == 1)
+                def _():
+                    dvs[0] = out
+                    middle_1.start()
+
+                return carry
+
+            lax.fori_loop(0, 2, block, 0)
+            finish(sets)
+            cotangent_0.wait_recv()
             from_sibling(1)
 
+        @pl.when(trailing)
+        def _():
+            ag_forward(2, True)
+            ag_rest(2, True)
+            cotangent_0.wait_send()
+            middle_1.wait_recv()
+
         start_all(1)
-        out = forward(1, middle).astype(BF)
+        out = forward(1, hbuf[...].astype(F32), 2, 0, section, lax.select(leading, 2, 0), True).astype(BF)
 
         @pl.when(leading)
         def _():
-            leaving[...] = out
-
-        @pl.when(jnp.logical_not(leading))
+            ends_out[0] = out
+            out_0.start()
+
+        @pl.when(trailing)
         def _():
-            ends_out[section] = out
-
-        cotangent = jnp.where(leading, swapped[...].astype(F32), ends[section].astype(F32))
-        d_middle = backward(1, cotangent).astype(BF).astype(F32)
-
-        @pl.when(jnp.logical_not(leading))
+            ends_out[1] = out
+
+        cotangent = jnp.where(leading, swapped[...].astype(F32), ends[1].astype(F32))
+        d_middle = backward(1, hbuf[...].astype(F32), cotangent, 2, 0, section, lax.select(leading, 2, 0), 0, True).astype(BF)
+
+        @pl.when(trailing)
         def _():
+            dvs[2] = d_middle
+            d_middle_1.start()
+            small_tiles(1)
             products(1)
-            for j in range(3):
-                start(copy_o(0, j))
-            for g in range(GROUPS):
-                start(copy_w(0, jnp.int32(g)))
-            start(copy_e(0))
-
-        d_first = backward(0, d_middle).astype(BF)
+            d_middle_1.wait_send()
+            out_0.wait_recv()
 
         @pl.when(leading)
         def _():
-            ends_out[section] = d_first
+            start(sets_back)
+            middle_1.wait_send()
+            dvs[0] = d_middle
+            small_tiles(1)
+            term(10, gs.at[1], gs.at[0]).start()
+            out_0.wait_send()
+            d_middle_1.wait_recv()
+
+            def block(i, carry):
+                b = 1 - i
+
+                @pl.when(i == 1)
+                def _():
+                    finish(sets_back)
+
+                ends_out[b] = backward(0, ends[b].astype(F32), dvs[b].astype(F32), b, b, b, b, i, i == 0).astype(BF)
+                return carry
+
+            lax.fori_loop(0, 2, block, 0)
+            gr[0] += gr[1]
+            hg[0] += hg[1]
+            small_tiles(0)
             products(0)
-
-        @pl.when(jnp.logical_not(leading))
-        def _():
-            leaving[...] = d_first
 
     V = pltpu.VMEM
     pl.run_scoped(
         layers,
         V((6, 4, 4, 96, 1024), BF), V((2, 4, 4, 2, 3, 16, 256), BF), V((3, 4, 4, 4, 48, 512), BF),
-        V((2, T, DI), F32), V((2, T, DI), F32), V((2, T, DI), F32), V((T, DI), F32), V((T, D), BF), V((2, T, 384), F32),
-        V((5, T, T), F32), V((T, T), F32), V((T, T), BF), V((512, T), BF), V((6, T, T), F32), V((6, 8, T), F32), V((6, 8, T), F32),
-        V((2, 2, T, T), F32), V((2, 2, T, T), BF), V((2, T, T), F32), V((T, T), F32), V((T, T), F32), V((T, T), F32), V((T, D), F32), V((2, 2, T, T), F32),
-        V((D, 256), BF), V((DI, 256), BF),
-        pltpu.SemaphoreType.DMA((6, 2)), pltpu.SemaphoreType.DMA((2, 2, 3)), pltpu.SemaphoreType.DMA((3,)), pltpu.SemaphoreType.DMA((3, 3)),
+        V((2, T, DI), F32), V((2, T, DI), F32), V((2, T, DI), F32), V((T, DI), F32), V((3, T, 384), F32),
+        V((4, T, T), F32), V((T, T), F32), V((T, T), F32), V((T, T), BF), V((512, T), BF), V((6, T, T), F32), V((6, 8, T), F32), V((6, 8, T), F32),
+        V((3, 2, T, T), F32), V((3, 2, T, T), BF), V((3, T, T), F32), V((T, T), F32), V((T, T), F32), V((T, T), F32), V((T, D), F32), V((3, 2, T, T), F32),
+        V((D, 256), BF), V((768, 256), BF),
+        pltpu.SemaphoreType.DMA((6, 2)), pltpu.SemaphoreType.DMA((2, 2, 3)), pltpu.SemaphoreType.DMA((3,)), pltpu.SemaphoreType.DMA((3, 3)), pltpu.SemaphoreType.DMA((3,)),
     )
-
-    end = misc(4, leaving, ends_out.at[section], sibling)
-    end.start()
 
     def sums(*bufs):
         it = iter(bufs)
@@ -839,8 +886,11 @@
 
             return done
 
-        term(10, tgot, tgot).wait_recv()
-        gs[section] += tgot[...]
+        @pl.when(trailing)
+        def _():
+            term(10, gs.at[1], gs.at[0]).wait_recv()
+            gs[1] += gs[0]
+
         for n, h in items[2]:
             j, kind = STREAMS[n]
             _, halves = neighbours(n, 2)
@@ -950,19 +1000,23 @@
     shapes += [V((3, 24, 1024), F32), V((24, 256), F32)] * 2 + [V((4, 4, 8, 128), F32), V((4, 8, 128), F32)]
     pl.run_scoped(sums, *shapes, pltpu.SemaphoreType.DMA((9, 2, 4)))
 
-    end.wait()
-    for n, (j, kind) in enumerate(STREAMS):
-        ref = gath[kind].at[section, j]
-        remote(ref, ref, s_sib.at[n], r_sib.at[n], sibling).wait_send()
+    @pl.when(trailing)
+    def _():
+        for n, (j, kind) in enumerate(STREAMS):
+            ref = gath[kind].at[1, j]
+            remote(ref, ref, s_sib.at[n], r_sib.at[n], sibling).wait_send()
+
+    @pl.when(leading)
+    def _():
+        for n, ref in enumerate((us_, os_, dvs)):
+            term(n, ref.at[2], ref.at[1]).wait_send()
+        for g in (4, 5):
+            dterm(g).wait_send()
+        term(9, dpes.at[2], dpes.at[1]).wait_send()
+        term(10, gs.at[1], gs.at[0]).wait_send()
 
     ag_sent(1)
     ag_sent(2)
-    for n, ref in enumerate((us_, os_, dvs)):
-        term(n, ref.at[2], ref.at[1]).wait_send()
-    for g in (4, 5):
-        dterm(g).wait_send()
-    term(9, dpes.at[2], dpes.at[1]).wait_send()
-    term(10, tgot, tgot).wait_send()
 
 
 def step(ends, segs, counts, win, taps, bias, pre, gate, wout, dtb, alog, skip):
@@ -977,18 +1031,18 @@
         step_kernel,
         out_shape=[
             s((2, T, D), BF), s((24, 6448), F32), s((48, D), F32), s((8, 128), F32),
-        ] + large,
+        ] + large + [s((3, T, DI), F32)],
         in_specs=[vm, vm, pl.BlockSpec(memory_space=pltpu.SMEM)] + [vm] * 9,
-        out_specs=[vm] * 4 + [any_] * 9,
+        out_specs=[vm] * 4 + [any_] * 10,
         scratch_shapes=[
             V((3, 24, 1024), BF), V((24, 256), BF), V((2, 4, 4, 4, 8, 128), F32),
-            V((2, 8, CC), F32), V((2, 8, 128), F32), V((2, 8, CC), F32), V((4, 4, 4, 8, 128), F32),
+            V((2, 8, CC), F32), V((2, 8, 128), F32), V((2, 8, CC), F32), V((2, 8, 128), F32),
             V((3, 4, 4, 8, 128), F32), V((3, 4, 8, 128), F32), V((3, 8, 128), F32),
             V((T, D), BF), V((T, D), BF), V((3, T, D), BF), V((3, T, DI), BF), V((3, T, D), BF), V((14, T, 1024), BF), V((3, 2, T, 256), BF),
-            S((7,)), S((7,)), S((9, 3)), S((9, 3, 8)), S((6, 3)), S((6, 3)), S((9,)), S((9,)), S((9, 3)), S((9, 3, 6)), S((11,)), S((11,)), S((9,)),
+            S((9,)), S((9,)), S((9, 3)), S((9, 3, 8)), S((6, 3)), S((6, 3)), S((9,)), S((9,)), S((9, 3)), S((9, 3, 6)), S((11,)), S((11,)), S((9,)),
             pltpu.SemaphoreType.REGULAR((2,)), pltpu.SemaphoreType.REGULAR,
         ],
-        compiler_params=pltpu.CompilerParams(collective_id=0, has_side_effects=True, vmem_limit_bytes=63 * 1024 * 1024),
+        compiler_params=pltpu.CompilerParams(collective_id=0, has_side_effects=True, vmem_limit_bytes=65280 * 1024),
         name="train_step",
     )(ends, segs, counts, win, taps, bias, pre, gate, wout, dtb, alog, skip)[:4]
 

time: 346 us -> 332 us (0.960)
  Pallas kernels: 345 us -> 330 us
    pallas_call x1, Pallas kernels: 342 us -> 328 us  [step(): pl.pallas_call(step_kernel, out_shape=[s((2, T, D), BF), s((24, 6448), F3...]
where the time goes in v4:
time: 332 us; the launch traced here: 331 us
  Pallas kernels  330 us (99%)
    pallas_call x1, Pallas kernels, step(): pl.pallas_call(step_kernel, out_shape=[s((2, T, D), BF), s((24, 6448), F3...  328 us

profile of v4, /device:TPU:0, one launch (start us, length us, event | category | flops | bytes accessed | tf_op | source)
XLA Modules:
  0.0 331.2 jit_solution(7471394847843397377)
XLA Ops:
  0.6 327.8 %train_step.1 = (bf16[2,128,1536]{2,1,0:T(8,128)(2,1)}, f32[24,6448]{1,0:T(8,128)}, f32[48,1536]{1,0:T(8,128)}, f32[8,128]{1,0:T(8,128)}, bf16[2,3,4,4,4,48,1024...) custom-call(bf16[2,128,1536]{2,1,0:T(8,128)(2,1)} %bitcast.8, ...), custom_call_target="tpu_custom_call" | custom-call | tf_op jit(solution)/shard_map/train_step/pallas_call | solution.py:1030
  328.4 2.6 results.1

commit v5 on v4

--- a/solution.py
+++ b/solution.py
@@ -20,6 +20,9 @@
 KINDS = ((48, 1024), (48, 512), (16, 256))
 ORDERS = ((2, 1, 0), (1, 0, 2), (0, 2, 1))
 STREAMS = tuple((j, kind) for j in range(3) for kind in range(3))
+ALL = (0, 3, 6, 1, 4, 7, 2, 5, 8)
+OUT = (1, 4, 7)
+REST = (0, 3, 6, 2, 5, 8)
 
 
 def moved(pos, axis, by):
@@ -46,7 +49,7 @@
 
 
 def sigmoid(v):
-    return 1.0 / (1.0 + jnp.exp(-v))
+    return 0.5 * jnp.tanh(0.5 * v) + 0.5
 
 
 def total(v):
@@ -136,8 +139,9 @@
         if share:
             to_sibling(n, index)
 
-    def ag_forward(phase, share=False):
-        for n, (j, kind) in enumerate(STREAMS):
+    def ag_forward(phase, share=False, part=ALL):
+        for n in part:
+            j, kind = STREAMS[n]
             order = ORDERS[j]
             right, left = moved(pos, order[phase], 1), moved(pos, order[phase], 3)
             for slot, h, source, to in ((0, 0, left, right), (1, 1, right, left)):
@@ -146,15 +150,17 @@
                     for q, index in enumerate(ag_pieces(n, phase, source, h)):
                         ag_copy(n, phase, 4 + 2 * slot + q, gath[kind].at[section, j].at[index], index, to).start()
 
-    def ag_rest(phase, share=False):
-        for n, (j, kind) in enumerate(STREAMS):
+    def ag_rest(phase, share=False, part=ALL):
+        for n in part:
+            j, kind = STREAMS[n]
             order = ORDERS[j]
             right, left = moved(pos, order[phase], 1), moved(pos, order[phase], 3)
             for slot, h, source in ((2, 1, left), (3, 0, right)):
                 if has_half(kind, phase, h):
                     ag_arrived(n, phase, slot, block_index(order, phase, source, h), share)
         for q in range(2 if phase == 2 else 1):
-            for n, (j, kind) in enumerate(STREAMS):
+            for n in part:
+                j, kind = STREAMS[n]
                 far = moved(pos, ORDERS[j][phase], 2)
                 for slot in (0, 1):
                     if has_half(kind, phase, slot):
@@ -212,7 +218,18 @@
             cotangent_0.start()
 
 
+        def first_phase(part):
+            copies = []
+            for n in part:
+                j, kind = STREAMS[n]
+                ag_start(n, 0, unit)
+                c = pltpu.make_async_copy(unit[kind].at[j], gath[kind].at[section, j].at[pos], own_sem.at[n])
+                c.start()
+                copies.append(c)
+            return copies
+
         small = small_gather(0)
+        own = first_phase(OUT)
         swap_w.wait()
         swap_e.wait()
         for j in range(3):
@@ -224,25 +241,40 @@
         both = jnp.concatenate([jnp.where(even, mine, theirs), jnp.where(even, theirs, mine)], axis=0).astype(BF)
         for j in range(3):
             ue[j] = both[16 * j : 16 * j + 16, :]
-        own = []
-        for n, (j, kind) in enumerate(STREAMS):
-            ag_start(n, 0, unit)
-            c = pltpu.make_async_copy(unit[kind].at[j], gath[kind].at[section, j].at[pos], own_sem.at[n])
-            c.start()
-            own.append(c)
+        own_rest = first_phase(REST)
         for c in small:
             c.wait()
         small = small_gather(1)
-        ag_forward(0)
+        ag_forward(0, part=OUT)
+        for c in own:
+            c.wait()
+        ag_rest(0, part=OUT)
+        for n in OUT:
+            ag_start(n, 1)
+        ag_forward(0, part=REST)
         for c in small:
             c.wait()
         small = small_gather(2)
-        for c in own:
+        for c in own_rest:
             c.wait()
-        ag_rest(0)
+        ag_rest(0, part=REST)
+
+        @pl.when(leading)
+        def _():
+            for n in REST:
+                ag_start(n, 1)
+
         for c in small:
             c.wait()
         small_across.start()
+        ag_forward(1, part=OUT)
+        ag_rest(1, part=OUT)
+
+        @pl.when(leading)
+        def _():
+            for n in OUT:
+                ag_start(n, 2)
+
         ag_sent(0)
 
     pl.run_scoped(
@@ -253,14 +285,6 @@
     def own_across():
         for n, (j, kind) in enumerate(STREAMS):
             to_sibling(n, block_index(ORDERS[j], 2, pos, None))
-
-    def go(n):
-        pl.semaphore_signal(go_sem.at[n], inc=1, device_id=sibling, device_id_type=MESH)
-
-    @pl.when(leading)
-    def _():
-        for n in range(9):
-            ag_start(n, 1)
 
     misc(3, gs.at[1 - section], gs.at[1 - section], sibling).wait()
     for l in range(2):
@@ -270,32 +294,30 @@
             par[l, 0:5, 52 * i : 52 * i + 52] = tile[0:5, 0:52]
             par[l, 7:8, 24 * i : 24 * i + 24] = tile[5:6, 0:24]
             par[l, 5:6, 48 * i : 48 * i + 48] = tile[6:7, 0:48]
-    def from_sibling(l):
-        for n, (j, kind) in enumerate(STREAMS):
-            ref = gath[kind].at[l, j]
-            remote(ref, ref, s_sib.at[n], r_sib.at[n], sibling).wait_recv()
+    def from_sibling(n):
+        j, kind = STREAMS[n]
+        ref = gath[kind].at[1, j]
+        remote(ref, ref, s_sib.at[n], r_sib.at[n], sibling).wait_recv()
 
     @pl.when(leading)
     def _():
-        ag_forward(1)
-        go(0)
-        ag_rest(1)
-        for n in range(9):
+        ag_forward(1, part=REST)
+        ag_rest(1, part=REST)
+        for n in REST:
             ag_start(n, 2)
         ag_forward(2)
-        go(1)
+        pl.semaphore_signal(go_sem, inc=1, device_id=sibling, device_id_type=MESH)
         ag_rest(2)
 
     @pl.when(trailing)
     def _():
-        pl.semaphore_wait(go_sem.at[0], 1)
-        for n in range(9):
+        for n in REST:
             ag_start(n, 1)
-        ag_forward(1)
-        ag_rest(1)
+        ag_forward(1, part=REST)
+        ag_rest(1, part=REST)
         own_across()
-        pl.semaphore_wait(go_sem.at[1], 1)
-        for n in range(9):
+        pl.semaphore_wait(go_sem, 1)
+        for n in ALL:
             ag_start(n, 2)
 
     landing = {}
@@ -607,7 +629,7 @@
                 gr[gi, 4:5, at] = total(dc)
                 dpes[sl, 0, :, 128 * j : 128 * j + 128] = conv_back(dc, taps).astype(BF)
             v = pebuf[s, :, 256:384] + rate_bias(l)
-            sv = sigmoid(v)
+            sv = 1.0 / (1.0 + jnp.exp(-v))
             dt = heads[s, 0]
             back = exact_dot(tri[...], rowq[...] - rowx[...], ((0,), (0,)))
             ratio = jnp.where(v < -15.0, 1.0, sv / jnp.maximum(dt, 1e-30))
@@ -745,16 +767,24 @@
             lax.fori_loop(0, 2, block, 0)
             finish(sets)
             cotangent_0.wait_recv()
-            from_sibling(1)
+            for n in range(9):
+                j, kind = STREAMS[n]
+                from_sibling(n)
+                if kind == 0:
+                    start(copy_w(1, jnp.int32(2 * j)))
+                    start(copy_w(1, jnp.int32(2 * j + 1)))
+                elif kind == 1:
+                    start(copy_o(1, j))
+            start(copy_e(1))
 
         @pl.when(trailing)
         def _():
             ag_forward(2, True)
             ag_rest(2, True)
+            start_all(1)
             cotangent_0.wait_send()
             middle_1.wait_recv()
 
-        start_all(1)
         out = forward(1, hbuf[...].astype(F32), 2, 0, section, lax.select(leading, 2, 0), True).astype(BF)
 
         @pl.when(leading)
@@ -862,7 +892,7 @@
                 remote(ref, ref, s_rs.at[n, phase], r_rs.at[n, phase, 0], sibling).wait_send()
 
         items = {phase: [(3 * j + kind, h) for kind in range(3) for j in range(3) for h in (0, 1) if has_half(kind, phase, h)] for phase in range(3)}
-        by_kind = [3 * j + kind for kind in range(3) for j in range(3)]
+
 
         def small_start(phase):
             axis = ORDERS[0][phase]
@@ -940,42 +970,62 @@
             rs_copy(n, phase, slot, ref, moved(pos, 0, 1)).wait_recv()
             return ref
 
-        for n, h in items[2]:
-            arrived(n, 2, neighbours(n, 2)[1][h][3])
-            last2(n, h)
-            if h == 1:
-                rs_start(n, 1, part_of(1))
+        def phase_2_last(kind):
+            for n, h in items[2]:
+                if STREAMS[n][1] == kind:
+                    arrived(n, 2, neighbours(n, 2)[1][h][3])
+                    last2(n, h)
+                    if h == 1:
+                        rs_start(n, 1, part_of(1))
+
+        def first(phase, kind):
+            for n, h in items[phase]:
+                if STREAMS[n][1] == kind:
+                    slot, block, to, summed, _ = neighbours(n, phase)[1][h]
+                    ref = arrived(n, phase, slot)
+                    add(ref, [ref, part_of(phase)(n, block, h)], (2,) if phase == 1 else (), BF)
+                    rs_copy(n, phase, summed, ref, to).start()
+
+        def last(phase, kind):
+            for n, h in items[phase]:
+                j, own_kind = STREAMS[n]
+                if own_kind == kind:
+                    here, halves = neighbours(n, phase)
+                    parts = [part_of(phase)(n, here, h), arrived(n, phase, halves[h][4]), arrived(n, phase, halves[h][3])]
+                    if phase == 0:
+                        add(fin[kind].at[j], parts, (), F32)
+                    else:
+                        add(acc1[kind], parts, (2,), BF, lambda a: (j, 2 * h + a))
+                        if h == 1:
+                            rs_start(n, 0, part_of(0))
+
+        phase_2_last(0)
         done = small_start(1)
-        last_tile = None
-        for phase in (1, 0):
-            part = part_of(phase)
-            dims = (2,) if phase == 1 else ()
-            for n, h in items[phase]:
-                slot, block, to, summed, _ = neighbours(n, phase)[1][h]
-                ref = arrived(n, phase, slot)
-                add(ref, [ref, part(n, block, h)], dims, BF)
-                rs_copy(n, phase, summed, ref, to).start()
-            last_tile = done()
-            for n, h in items[phase]:
-                j, kind = STREAMS[n]
-                here, halves = neighbours(n, phase)
-                parts = [part(n, here, h), arrived(n, phase, halves[h][4]), arrived(n, phase, halves[h][3])]
-                if phase == 0:
-                    add(fin[kind].at[j], parts, dims, F32)
-                    continue
-                add(acc1[kind], parts, dims, BF, lambda a: (j, 2 * h + a))
-                if h == 1:
-                    rs_start(n, 0, part_of(0))
-            if phase == 1:
-                done = small_start(0)
-
+        phase_2_last(1)
+        first(1, 0)
+        phase_2_last(2)
+        first(1, 1)
+        last(1, 0)
+        done()
+        done = small_start(0)
+        first(1, 2)
+        last(1, 1)
+        first(0, 0)
+        last(1, 2)
+        first(0, 1)
+        last(0, 0)
         for j in range(3):
             fsend[j] = jnp.where(even, fin[0][j, 24:48, :], fin[0][j, 0:24, :])
+        swap_f = misc(5, fsend, fgot, device(partner))
+        swap_f.start()
+        first(0, 2)
+        last(0, 1)
+        last(0, 2)
+        last_tile = done()
+
         last_e = jnp.concatenate([fin[2][j] for j in range(3)], axis=0)
         gsend[...] = jnp.where(even, last_e[24:48], last_e[0:24])
-        swap_f = misc(5, fsend, fgot, device(partner))
         swap_g = misc(6, gsend, ggot, device(partner))
-        swap_f.start()
         swap_g.start()
         for j in range(3):
             for i, at in enumerate(group_columns(2 * j + parity)):
@@ -1040,7 +1090,7 @@
             V((3, 4, 4, 8, 128), F32), V((3, 4, 8, 128), F32), V((3, 8, 128), F32),
             V((T, D), BF), V((T, D), BF), V((3, T, D), BF), V((3, T, DI), BF), V((3, T, D), BF), V((14, T, 1024), BF), V((3, 2, T, 256), BF),
             S((9,)), S((9,)), S((9, 3)), S((9, 3, 8)), S((6, 3)), S((6, 3)), S((9,)), S((9,)), S((9, 3)), S((9, 3, 6)), S((11,)), S((11,)), S((9,)),
-            pltpu.SemaphoreType.REGULAR((2,)), pltpu.SemaphoreType.REGULAR,
+            pltpu.SemaphoreType.REGULAR, pltpu.SemaphoreType.REGULAR,
         ],
         compiler_params=pltpu.CompilerParams(collective_id=0, has_side_effects=True, vmem_limit_bytes=65280 * 1024),
         name="train_step",

time: 332 us -> 330 us (level)
  no operation moved by 1% of the time
where the time goes in v5:
time: 330 us
  Pallas kernels  329 us (100%)
    pallas_call x1, Pallas kernels, step(): pl.pallas_call(step_kernel, out_shape=[s((2, T, D), BF), s((24, 6448), F3...  326 us

profile of v5, /device:TPU:0, one launch (start us, length us, event | category | flops | bytes accessed | tf_op | source)
XLA Modules:
  0.0 329.8 jit_solution(6094338189764924993)
XLA Ops:
  0.6 326.5 %train_step.1 = (bf16[2,128,1536]{2,1,0:T(8,128)(2,1)}, f32[24,6448]{1,0:T(8,128)}, f32[48,1536]{1,0:T(8,128)}, f32[8,128]{1,0:T(8,128)}, bf16[2,3,4,4,4,48,1024...) custom-call(bf16[2,128,1536]{2,1,0:T(8,128)(2,1)} %bitcast.8, ...), custom_call_target="tpu_custom_call" | custom-call | tf_op jit(solution)/shard_map/train_step/pallas_call | solution.py:1080
  327.1 2.6 results.1

commit v6 on v5

--- a/solution.py
+++ b/solution.py
@@ -49,7 +49,7 @@
 
 
 def sigmoid(v):
-    return 0.5 * jnp.tanh(0.5 * v) + 0.5
+    return 1.0 / (1.0 + jnp.exp(-v))
 
 
 def total(v):
@@ -294,10 +294,10 @@
             par[l, 0:5, 52 * i : 52 * i + 52] = tile[0:5, 0:52]
             par[l, 7:8, 24 * i : 24 * i + 24] = tile[5:6, 0:24]
             par[l, 5:6, 48 * i : 48 * i + 48] = tile[6:7, 0:48]
-    def from_sibling(n):
-        j, kind = STREAMS[n]
-        ref = gath[kind].at[1, j]
-        remote(ref, ref, s_sib.at[n], r_sib.at[n], sibling).wait_recv()
+    def from_sibling(l):
+        for n, (j, kind) in enumerate(STREAMS):
+            ref = gath[kind].at[l, j]
+            remote(ref, ref, s_sib.at[n], r_sib.at[n], sibling).wait_recv()
 
     @pl.when(leading)
     def _():
@@ -629,7 +629,7 @@
                 gr[gi, 4:5, at] = total(dc)
                 dpes[sl, 0, :, 128 * j : 128 * j + 128] = conv_back(dc, taps).astype(BF)
             v = pebuf[s, :, 256:384] + rate_bias(l)
-            sv = 1.0 / (1.0 + jnp.exp(-v))
+            sv = sigmoid(v)
             dt = heads[s, 0]
             back = exact_dot(tri[...], rowq[...] - rowx[...], ((0,), (0,)))
             ratio = jnp.where(v < -15.0, 1.0, sv / jnp.maximum(dt, 1e-30))
@@ -767,24 +767,16 @@
             lax.fori_loop(0, 2, block, 0)
             finish(sets)
             cotangent_0.wait_recv()
-            for n in range(9):
-                j, kind = STREAMS[n]
-                from_sibling(n)
-                if kind == 0:
-                    start(copy_w(1, jnp.int32(2 * j)))
-                    start(copy_w(1, jnp.int32(2 * j + 1)))
-                elif kind == 1:
-                    start(copy_o(1, j))
-            start(copy_e(1))
+            from_sibling(1)
 
         @pl.when(trailing)
         def _():
             ag_forward(2, True)
             ag_rest(2, True)
-            start_all(1)
             cotangent_0.wait_send()
             middle_1.wait_recv()
 
+        start_all(1)
         out = forward(1, hbuf[...].astype(F32), 2, 0, section, lax.select(leading, 2, 0), True).astype(BF)
 
         @pl.when(leading)

time: 330 us -> 326 us (0.988)
  Pallas kernels: 329 us -> 325 us
    pallas_call x1, Pallas kernels: 326 us -> 322 us  [step(): pl.pallas_call(step_kernel, out_shape=[s((2, T, D), BF), s((24, 6448), F3...]
where the time goes in v6:
time: 326 us; the launch traced here: 325 us
  Pallas kernels  325 us (100%)
    pallas_call x1, Pallas kernels, step(): pl.pallas_call(step_kernel, out_shape=[s((2, T, D), BF), s((24, 6448), F3...  322 us

profile of v6, /device:TPU:0, one launch (start us, length us, event | category | flops | bytes accessed | tf_op | source)
XLA Modules:
  0.0 325.4 jit_solution(1826429918720110713)
XLA Ops:
  0.6 322.1 %train_step.1 = (bf16[2,128,1536]{2,1,0:T(8,128)(2,1)}, f32[24,6448]{1,0:T(8,128)}, f32[48,1536]{1,0:T(8,128)}, f32[8,128]{1,0:T(8,128)}, bf16[2,3,4,4,4,48,1024...) custom-call(bf16[2,128,1536]{2,1,0:T(8,128)(2,1)} %bitcast.8, ...), custom_call_target="tpu_custom_call" | custom-call | tf_op jit(solution)/shard_map/train_step/pallas_call | solution.py:1072
  322.7 2.6 results.1
